TPU v7x, 32 devices: a whole 2x2x4 slice. The times are simulated.
32 devices in a mesh: ctx: 8 (over z, x), tp: 4 (over y, core).
Axes of the slice: x: 2, y: 2, z: 4, core: 2. Of those that a mesh axis runs over, the one named last changes fastest.
Arguments:
- query_head_matrix: bfloat16 [1024, 4096], P('ctx', 'tp'), may hold values from -6 to 6
- key_head_matrix: bfloat16 [1024, 1024], P('ctx', 'tp'), may hold values from -6 to 6
- value_head_matrix: bfloat16 [1024, 1024], P('ctx', 'tp'), may hold values from -6 to 6
- ssm_input: bfloat16 [1024, 8192], P('ctx', 'tp'), may hold values from -0.59765625 to 0.59765625
- log_decay: float32 [1024, 128], P('ctx', 'tp'), may hold values from -1 to 0
- state_write: bfloat16 [1024, 128], P('ctx'), may hold values from -1.796875 to 1.796875
- state_read: bfloat16 [1024, 128], P('ctx'), may hold values from -1.796875 to 1.796875
- document_ids: int32 [1024], P('ctx'), may hold values from 0 to 7, never falling along the last dimension, each value on 1 to 256 neighbouring positions
- attention_output_gradient: bfloat16 [1024, 4096], P('ctx', 'tp'), may hold values from -6 to 6
- cot_mixer: bfloat16 [1024, 8192], P('ctx', 'tp'), may hold values from -6 to 6
Outputs:
- attention_out: bfloat16 [1024, 4096], P('ctx', 'tp')
- mixer_out: bfloat16 [1024, 8192], P('ctx', 'tp')
- grad_key: bfloat16 [1024, 1024], P('ctx', 'tp')
- grad_value: bfloat16 [1024, 1024], P('ctx', 'tp')
- grad_input: bfloat16 [1024, 8192], P('ctx', 'tp')
Inputs may be any that keep to these rules, and one draw needn't show every extreme that they name: `document_ids`: never falls along the sequence; each document holds 1 to 256 tokens.
All inputs are finite; a program needn't handle non-finite values.
Results may differ from a plain program's by a relative error of at most 0.0062.
Values may be sent and summed in bfloat16 or wider, within the bound.
No kernel may reach another device: no remote copies, remote signals or barrier semaphores. Data moves between devices by JAX's collectives and lax.ppermute only.
A program may use at most 320 MiB of HBM per device.

v0:
```python
import math

import jax
import jax.numpy as jnp
from jax import lax
from jax.sharding import PartitionSpec as P

HEAD_CHANNELS = 128
SPAN = 2


def passed_along(block, axis, distance):
    devices = range(lax.axis_size(axis))
    route = [(i - distance, i) for i in devices if i - distance in devices]
    return lax.ppermute(block, axis, route)


def combine_carry(earlier, nearer):
    return (earlier[0] * nearer[0], nearer[0][:, None, None] * earlier[1] + nearer[1])


def mixer_pieces(decays, scores, reads_f32, writes_f32, inside, doc_float, prev_doc):
    running = jnp.cumsum(decays, axis=0).T
    log_gaps = running[:, :, None] - running[:, None, :]
    decay_mat = jnp.exp(jnp.where(inside[None], log_gaps, -jnp.inf))
    weights = (decay_mat * scores[None]).astype(jnp.bfloat16)
    entry_w = jnp.exp(running) * (doc_float == prev_doc).astype(jnp.float32)[None]
    read_w = (entry_w[:, :, None] * reads_f32[None]).astype(jnp.bfloat16)
    exit_w = (
        jnp.exp(running[:, -1:] - running) * (doc_float == doc_float[-1]).astype(jnp.float32)[None]
    )
    write_w = (exit_w[:, :, None] * writes_f32[None]).astype(jnp.bfloat16)
    block_gain = jnp.exp(running[:, -1]) * (doc_float[-1] == prev_doc).astype(jnp.float32)
    weights, read_w, write_w = lax.optimization_barrier((weights, read_w, write_w))
    return (weights, read_w, write_w, block_gain)


def attn_probs(query_grp, key_grp, inside, inv_root):
    scores = (
        jnp.einsum("tid,sd->its", query_grp, key_grp, preferred_element_type=jnp.float32) * inv_root
    )
    scores = jnp.where(inside[None], scores, -jnp.inf)
    row_peak = jnp.max(scores, axis=-1, keepdims=True)
    raised = jnp.exp(scores - row_peak)
    return (raised / jnp.sum(raised, axis=-1, keepdims=True)).astype(jnp.bfloat16)


def attn_grads(query_grp, value_grp, cot_grp, prob_mat, inv_root):
    prob_grad = jnp.einsum("tid,sd->its", cot_grp, value_grp, preferred_element_type=jnp.float32)
    probability_single = prob_mat.astype(jnp.float32)
    inner_sum = jnp.sum(probability_single * prob_grad, axis=-1, keepdims=True)
    score_gradient = (probability_single * (prob_grad - inner_sum) * inv_root).astype(jnp.bfloat16)
    key_gradient = jnp.einsum(
        "its,tid->sd", score_gradient, query_grp, preferred_element_type=jnp.float32
    )
    value_gradient = jnp.einsum(
        "its,tid->sd", prob_mat, cot_grp, preferred_element_type=jnp.float32
    )
    return (key_gradient, value_gradient)


def shards(
    query_head_matrix,
    key_head_matrix,
    value_head_matrix,
    ssm_input,
    log_decay,
    state_write,
    state_read,
    document_ids,
    attention_output_gradient,
    cot_mixer,
):
    tokens = key_head_matrix.shape[0]
    kv_local = key_head_matrix.shape[1] // HEAD_CHANNELS
    queries_per_group = query_head_matrix.shape[1] // (HEAD_CHANNELS * kv_local)
    inv_root = 1.0 / math.sqrt(HEAD_CHANNELS)
    position = lax.axis_index("ctx")
    doc_float = document_ids.astype(jnp.float32)
    doc_wire = document_ids.astype(jnp.bfloat16)
    row_ids = jnp.arange(tokens)

    def assemble(tile_list):
        keys_all = jnp.concatenate(
            [tile_list[num][0] for num in reversed(range(SPAN))] + [key_head_matrix], axis=0
        )
        values_all = jnp.concatenate(
            [tile_list[num][1] for num in reversed(range(SPAN))] + [value_head_matrix], axis=0
        )
        docs_all = jnp.concatenate(
            [tile_list[num][2] for num in reversed(range(SPAN))] + [doc_float], axis=0
        )
        column = jnp.arange(keys_all.shape[0]) - SPAN * tokens
        inside = (docs_all[None, :] == doc_float[:, None]) & (column[None, :] <= row_ids[:, None])
        return (keys_all, values_all, inside)

    first_tiles = []
    for offset in range(1, SPAN + 1):
        fetched = passed_along((key_head_matrix, value_head_matrix, doc_wire), "ctx", offset)
        usable = position >= offset
        first_tiles.append(
            (fetched[0], fetched[1], jnp.where(usable, fetched[2].astype(jnp.float32), -1.0))
        )
    keys_all, values_all, inside_attn = assemble(first_tiles)
    prev_doc = first_tiles[0][2][-1]
    query_grps = []
    cot_grps = []
    fwd_probs = []
    out_cols = []
    for head_grp in range(kv_local):
        low_col = head_grp * queries_per_group * HEAD_CHANNELS
        high_col = (head_grp + 1) * queries_per_group * HEAD_CHANNELS
        query_grp = query_head_matrix[:, low_col:high_col].reshape(
            tokens, queries_per_group, HEAD_CHANNELS
        )
        cot_grp = attention_output_gradient[:, low_col:high_col].reshape(
            tokens, queries_per_group, HEAD_CHANNELS
        )
        prob_mat = attn_probs(
            query_grp,
            keys_all[:, head_grp * HEAD_CHANNELS : (head_grp + 1) * HEAD_CHANNELS],
            inside_attn,
            inv_root,
        )
        out_grp = jnp.einsum(
            "its,sd->tid",
            prob_mat,
            values_all[:, head_grp * HEAD_CHANNELS : (head_grp + 1) * HEAD_CHANNELS],
            preferred_element_type=jnp.float32,
        ).astype(jnp.bfloat16)
        out_cols.append(out_grp.reshape(tokens, queries_per_group * HEAD_CHANNELS))
        query_grps.append(query_grp)
        cot_grps.append(cot_grp)
        fwd_probs.append(prob_mat)
    attention_out = jnp.concatenate(out_cols, axis=1)
    nheads = log_decay.shape[1]
    head_width = ssm_input.shape[1] // nheads
    head_block = math.gcd(nheads, 8)
    block_count = nheads // head_block
    scores_mix = jnp.dot(state_read, state_write.T, preferred_element_type=jnp.float32)
    reads_f32 = state_read.astype(jnp.float32)
    writes_f32 = state_write.astype(jnp.float32)
    inside_mix = (row_ids[:, None] >= row_ids[None, :]) & (doc_float[:, None] == doc_float[None, :])
    block_parts = []
    gain_list = []
    state_list = []
    back_list = []
    for block_no in range(block_count):
        low_col = block_no * head_block * head_width
        high_col = (block_no + 1) * head_block * head_width
        inputs = ssm_input[:, low_col:high_col].reshape(tokens, head_block, head_width)
        cot_rows = cot_mixer[:, low_col:high_col].reshape(tokens, head_block, head_width)
        decays = log_decay[:, block_no * head_block : (block_no + 1) * head_block]
        weights, read_w, write_w, block_gain = mixer_pieces(
            decays, scores_mix, reads_f32, writes_f32, inside_mix, doc_float, prev_doc
        )
        state_list.append(
            jnp.einsum("shp,hsn->hpn", inputs, write_w, preferred_element_type=jnp.float32)
        )
        back_list.append(
            jnp.einsum("thp,htn->hpn", cot_rows, read_w, preferred_element_type=jnp.float32)
        )
        gain_list.append(block_gain)
        block_parts.append((inputs, cot_rows, weights, read_w, write_w))
    block_gains = jnp.concatenate(gain_list, axis=0)
    block_states = jnp.concatenate(state_list, axis=0)
    block_backs = jnp.concatenate(back_list, axis=0)
    identity = (jnp.ones_like(block_gains), jnp.zeros_like(block_states))
    moving = identity
    for section_no in range(SPAN):
        moving = passed_along(combine_carry(moving, (block_gains, block_states)), "ctx", 1)
    carry_in = moving[1]
    moving = identity
    for section_no in range(SPAN):
        moving = passed_along(combine_carry(moving, (block_gains, block_backs)), "ctx", -1)
    carry_out = moving[1]
    mixed_cols = []
    grad_cols = []
    for block_no in range(block_count):
        inputs, cot_rows, weights, read_w, write_w = block_parts[block_no]
        low_head = block_no * head_block
        high_head = (block_no + 1) * head_block
        mixed_out = jnp.einsum("hts,shp->thp", weights, inputs, preferred_element_type=jnp.float32)
        mixed_out = mixed_out + jnp.einsum(
            "hpn,htn->thp",
            carry_in[low_head:high_head],
            read_w.astype(jnp.float32),
            precision=lax.Precision.HIGHEST,
        )
        grad_rows = jnp.einsum(
            "hts,thp->shp", weights, cot_rows, preferred_element_type=jnp.float32
        )
        grad_rows = grad_rows + jnp.einsum(
            "hpn,hsn->shp",
            carry_out[low_head:high_head],
            write_w.astype(jnp.float32),
            precision=lax.Precision.HIGHEST,
        )
        mixed_cols.append(mixed_out.astype(jnp.bfloat16).reshape(tokens, head_block * head_width))
        grad_cols.append(grad_rows.astype(jnp.bfloat16).reshape(tokens, head_block * head_width))
    mixer_out = jnp.concatenate(mixed_cols, axis=1)
    grad_input = jnp.concatenate(grad_cols, axis=1)
    second_tiles = []
    for offset in range(1, SPAN + 1):
        fetched = passed_along((key_head_matrix, value_head_matrix, doc_wire), "ctx", offset)
        usable = position >= offset
        second_tiles.append(
            (fetched[0], fetched[1], jnp.where(usable, fetched[2].astype(jnp.float32), -1.0))
        )
    keys_back, values_back, inside_back = assemble(second_tiles)
    saved_probs = [
        attn_probs(
            query_grps[head_grp],
            keys_back[:, head_grp * HEAD_CHANNELS : (head_grp + 1) * HEAD_CHANNELS],
            inside_back,
            inv_root,
        )
        for head_grp in range(kv_local)
    ]
    key_cols = []
    value_cols = []
    for head_grp in range(kv_local):
        key_gradient, value_gradient = attn_grads(
            query_grps[head_grp],
            values_back[:, head_grp * HEAD_CHANNELS : (head_grp + 1) * HEAD_CHANNELS],
            cot_grps[head_grp],
            saved_probs[head_grp],
            inv_root,
        )
        key_cols.append(key_gradient)
        value_cols.append(value_gradient)
    key_window = jnp.concatenate(key_cols, axis=1)
    value_window = jnp.concatenate(value_cols, axis=1)
    key_total = key_window[SPAN * tokens :]
    value_total = value_window[SPAN * tokens :]
    for offset in range(1, SPAN + 1):
        low_row = (SPAN - offset) * tokens
        returned = passed_along(
            (key_window[low_row : low_row + tokens], value_window[low_row : low_row + tokens]),
            "ctx",
            -offset,
        )
        key_total = key_total + returned[0]
        value_total = value_total + returned[1]
    grad_key = key_total.astype(jnp.bfloat16)
    grad_value = value_total.astype(jnp.bfloat16)
    return (attention_out, mixer_out, grad_key, grad_value, grad_input)


def solution(mesh):
    return jax.shard_map(
        shards,
        mesh=mesh,
        in_specs=(
            P("ctx", "tp"),
            P("ctx", "tp"),
            P("ctx", "tp"),
            P("ctx", "tp"),
            P("ctx", "tp"),
            P("ctx", None),
            P("ctx", None),
            P("ctx"),
            P("ctx", "tp"),
            P("ctx", "tp"),
        ),
        out_specs=(P("ctx", "tp"), P("ctx", "tp"), P("ctx", "tp"), P("ctx", "tp"), P("ctx", "tp")),
        check_vma=False,
    )
```

profile of v0, /device:TPU:14, one launch (start us, length us, event | category | flops | bytes accessed | tf_op | source)
XLA Modules:
  0.0 181.6 jit_solution(9184415128369813937)
XLA Ops:
  0.6 1.2 fusion.75
  1.8 3.4 %collective-permute-start.3 = (bf16[128]{0:T(256)(128)(2,1)}, bf16[128]{0:T(256)(128)(2,1)S(1)}, u32[]{:S(2)}, u32[]{:S(2)}) collective-permute-start(bf16[128]{0:T(256)(128)(2,1)} %get-tuple-element.103), channel_id=1, source_target_pairs={{0,4},{4,8},{8,12},{12,16},{16,20},{20,24},{24,28},{1,5},{5,9},{9,... | collective-permute-start | bytes 776 | tf_op jit(solution)/shard_map/ppermute | solution.py:15
  5.3 3.5 %collective-permute-start.2 = (bf16[128]{0:T(256)(128)(2,1)}, bf16[128]{0:T(256)(128)(2,1)}, u32[]{:S(2)}, u32[]{:S(2)}) collective-permute-start(bf16[128]{0:T(256)(128)(2,1)} %get-tuple-element.103), channel_id=1, source_target_pairs={{0,8},{4,12},{8,16},{12,20},{16,24},{20,28},{1,9},{5,13},{9,17},{1... | collective-permute-start | bytes 776 | tf_op jit(solution)/shard_map/ppermute | solution.py:15
  8.8 1.9 %collective-permute-start.4 = (bf16[128,256]{1,0:T(8,128)(2,1)}, bf16[128,256]{1,0:T(8,128)(2,1)}, u32[]{:S(2)}, u32[]{:S(2)}) collective-permute-start(bf16[128,256]{1,0:T(8,128)(2,1)} %param.11), channel_id=1, source_target_pairs={{0,8},{4,12},{8,16},{12,20},{16,24},{20,28},{1,9},{5,13},{9,17},{1... | collective-permute-start | bytes 196616 | tf_op jit(solution)/shard_map/ppermute | solution.py:15
  10.7 3.4 %collective-permute-start.5 = (bf16[128,256]{1,0:T(8,128)(2,1)}, bf16[128,256]{1,0:T(8,128)(2,1)}, u32[]{:S(2)}, u32[]{:S(2)}) collective-permute-start(bf16[128,256]{1,0:T(8,128)(2,1)} %param.11), channel_id=1, source_target_pairs={{0,4},{4,8},{8,12},{12,16},{16,20},{20,24},{24,28},{1,5},{5,9},{9,... | collective-permute-start | bytes 196616 | tf_op jit(solution)/shard_map/ppermute | solution.py:15
  14.1 1.6 copy.176
  15.7 1.9 %collective-permute-start = (bf16[128,256]{0,1:T(8,128)(2,1)}, bf16[128,256]{0,1:T(8,128)(2,1)}, u32[]{:S(2)}, u32[]{:S(2)}) collective-permute-start(bf16[128,256]{0,1:T(8,128)(2,1)} %copy.176), channel_id=1, source_target_pairs={{0,8},{4,12},{8,16},{12,20},{16,24},{20,28},{1,9},{5,13},{9,17},{1... | collective-permute-start | bytes 196616 | tf_op jit(solution)/shard_map/ppermute | solution.py:15
  32.2 2.0 %collective-permute-start.1 = (bf16[128,256]{0,1:T(8,128)(2,1)}, bf16[128,256]{0,1:T(8,128)(2,1)}, u32[]{:S(2)}, u32[]{:S(2)}) collective-permute-start(bf16[128,256]{0,1:T(8,128)(2,1)} %copy.176), channel_id=1, source_target_pairs={{0,4},{4,8},{8,12},{12,16},{16,20},{20,24},{24,28},{1,5},{5,9},{9,... | collective-permute-start | bytes 196616 | tf_op jit(solution)/shard_map/ppermute | solution.py:15
  34.9 1.3 compare_convert_fusion
  37.6 1.3 multiply_convert_fusion.9
  39.1 1.0 fusion.79
  40.1 0.9 fusion.83
  42.1 1.0 fusion.80
  43.1 1.0 fusion.84
  45.2 1.0 fusion.81
  46.2 0.9 fusion.85
  48.2 0.9 fusion.86
  49.5 1.5 fusion.36
  51.0 1.0 fusion.82
  52.0 3.9 %collective-permute-start.12 = (f32[32,64,128]{2,1,0:T(8,128)}, f32[32,64,128]{2,1,0:T(8,128)}, u32[]{:S(2)}, u32[]{:S(2)}) collective-permute-start(f32[32,64,128]{2,1,0:T(8,128)} %get-tuple-element.99), channel_id=1, source_target_pairs={{4,0},{8,4},{12,8},{16,12},{20,16},{24,20},{28,24},{5,1},{9,5},{13... | collective-permute-start | bytes 3145736 | tf_op jit(solution)/shard_map/ppermute | solution.py:15
  56.8 2.8 %collective-permute-start.6 = (f32[32,64,128]{2,1,0:T(8,128)}, f32[32,64,128]{2,1,0:T(8,128)}, u32[]{:S(2)}, u32[]{:S(2)}) collective-permute-start(f32[32,64,128]{2,1,0:T(8,128)} %get-tuple-element.100), channel_id=1, source_target_pairs={{0,4},{4,8},{8,12},{12,16},{16,20},{20,24},{24,28},{1,5},{5,9},{9,... | collective-permute-start | bytes 3145736 | tf_op jit(solution)/shard_map/ppermute | solution.py:15
  59.6 0.9 constant_dynamic-update-slice_fusion.2
  60.5 0.9 constant_dynamic-update-slice_fusion.1
  61.4 1.3 fusion.77
  62.7 1.2 divide_convert_fusion.1
  64.0 1.3 fusion.76
  65.2 1.0 pad_maximum_fusion.5
  66.2 1.2 convolution_bitcast_fusion.1
  67.4 1.2 convolution_bitcast_fusion
  68.6 2.5 %fusion.31 = f32[384,128]{0,1:T(8,128)} fusion(bf16[128,4,128]{0,2,1:T(8,128)(2,1)S(1)} %bitcast.217, f32[4,128,384]{1,2,0:T(8,128)} %convolution_bitcast_fusion.1, bf16[4,128,384]{1,2,0:T(8,128)(2,1)S(1)} %divide_convert_fusion.1), kind=kOutput, calls=%fused_computation.51 | convolution fusion | flops 51708800 | bytes 1507328 | tf_op jit(solution)/shard_map/its,tid->sd/dot_general | solution.py:53
  71.1 1.2 divide_convert_fusion
  72.3 2.6 %fusion.30 = f32[384,128]{0,1:T(8,128)} fusion(bf16[128,4,128]{0,2,1:T(8,128)(2,1)} %bitcast.218, f32[4,128,384]{1,2,0:T(8,128)} %convolution_bitcast_fusion, bf16[4,128,384]{1,2,0:T(8,128)(2,1)S(1)} %divide_convert_fusion), kind=kOutput, calls=%fused_computation.50 | convolution fusion | flops 51708800 | bytes 1507328 | tf_op jit(solution)/shard_map/its,tid->sd/dot_general | solution.py:53
  74.9 1.7 fusion.54
  76.6 3.1 %collective-permute-start.8 = (f32[128,256]{0,1:T(8,128)}, f32[128,256]{0,1:T(8,128)}, u32[]{:S(2)}, u32[]{:S(2)}) collective-permute-start(f32[128,256]{0,1:T(8,128)} %get-tuple-element.61), channel_id=1, source_target_pairs={{4,0},{8,4},{12,8},{16,12},{20,16},{24,20},{28,24},{5,1},{9,5},{13... | collective-permute-start | bytes 393224 | tf_op jit(solution)/shard_map/ppermute | solution.py:15
  79.7 6.0 %collective-permute-start.9 = (f32[128,256]{0,1:T(8,128)}, f32[128,256]{0,1:T(8,128)}, u32[]{:S(2)}, u32[]{:S(2)}) collective-permute-start(f32[128,256]{0,1:T(8,128)} %get-tuple-element.62), channel_id=1, source_target_pairs={{8,0},{12,4},{16,8},{20,12},{24,16},{28,20},{9,1},{13,5},{17,9},{2... | collective-permute-start | bytes 393224 | tf_op jit(solution)/shard_map/ppermute | solution.py:15
  86.1 0.9 convolution_convert_fusion.1
  87.0 14.3 %collective-permute-done.12 = f32[32,64,128]{2,1,0:T(8,128)} collective-permute-done((f32[32,64,128]{2,1,0:T(8,128)}, f32[32,64,128]{2,1,0:T(8,128)}, u32[]{:S(2)}, u32[]{:S(2)}) %collective-permute-start.12) | collective-permute-done | bytes 1048608 | tf_op jit(solution)/shard_map/ppermute | solution.py:15
  101.4 3.1 %collective-permute-done.6 = f32[32,64,128]{2,1,0:T(8,128)} collective-permute-done((f32[32,64,128]{2,1,0:T(8,128)}, f32[32,64,128]{2,1,0:T(8,128)}, u32[]{:S(2)}, u32[]{:S(2)}) %collective-permute-start.6) | collective-permute-done | bytes 1048608 | tf_op jit(solution)/shard_map/ppermute | solution.py:15
  104.5 3.1 %multiply_add_fusion = (f32[32,64,128]{2,1,0:T(8,128)}, f32[32,64,128]{2,1,0:T(8,128)}) fusion(f32[32,64,128]{2,1,0:T(8,128)} %collective-permute-done.12, f32[8,64,128]{2,1,0:T(8,128)S(1)} %copy-done.9, f32[8,64,128]{2,1,0:T(8,128)S(1)} %copy-done.7, f32[8,64,128]{2,1,0:T(8,128)S(1)} %copy-done.3, f32[8,64,128]{2,1,0:T(8,128)S(1)} %convolution_bitcast_fusion.5, ...), kind=kLoop, calls=%fused_computation.58 | loop fusion | flops 2621440 | bytes 6291584 | tf_op jit(solution)/shard_map/add | solution.py:19
  107.6 1.9 %collective-permute-start.13 = (f32[32,64,128]{2,1,0:T(8,128)}, f32[32,64,128]{2,1,0:T(8,128)}, u32[]{:S(2)}, u32[]{:S(2)}) collective-permute-start(f32[32,64,128]{2,1,0:T(8,128)} %get-tuple-element.97), channel_id=1, source_target_pairs={{4,0},{8,4},{12,8},{16,12},{20,16},{24,20},{28,24},{5,1},{9,5},{13... | collective-permute-start | bytes 3145736 | tf_op jit(solution)/shard_map/ppermute | solution.py:15
  109.8 0.9 convolution_convert_fusion
  111.4 5.8 %collective-permute-start.10 = (f32[128,256]{0,1:T(8,128)}, f32[128,256]{0,1:T(8,128)}, u32[]{:S(2)}, u32[]{:S(2)}) collective-permute-start(f32[128,256]{0,1:T(8,128)} %get-tuple-element.59), channel_id=1, source_target_pairs={{4,0},{8,4},{12,8},{16,12},{20,16},{24,20},{28,24},{5,1},{9,5},{13... | collective-permute-start | bytes 393224 | tf_op jit(solution)/shard_map/ppermute | solution.py:15
  117.3 1.9 %collective-permute-start.11 = (f32[128,256]{0,1:T(8,128)}, f32[128,256]{0,1:T(8,128)}, u32[]{:S(2)}, u32[]{:S(2)}) collective-permute-start(f32[128,256]{0,1:T(8,128)} %get-tuple-element.60), channel_id=1, source_target_pairs={{8,0},{12,4},{16,8},{20,12},{24,16},{28,20},{9,1},{13,5},{17,9},{2... | collective-permute-start | bytes 393224 | tf_op jit(solution)/shard_map/ppermute | solution.py:15
  120.0 1.0 copy.186
  121.0 1.6 pad_maximum_fusion.4
  122.6 1.1 fusion.58
  123.7 3.6 %collective-permute-start.7 = (f32[32,64,128]{2,1,0:T(8,128)S(1)}, f32[32,64,128]{2,1,0:T(8,128)}, u32[]{:S(2)}, u32[]{:S(2)}) collective-permute-start(f32[32,64,128]{2,1,0:T(8,128)S(1)} %copy-done.26), channel_id=1, source_target_pairs={{0,4},{4,8},{8,12},{12,16},{16,20},{20,24},{24,28},{1,5},{5,9},{9,... | collective-permute-start | bytes 3145736 | tf_op jit(solution)/shard_map/ppermute | solution.py:15
  127.3 30.7 %collective-permute-done.10 = f32[128,256]{0,1:T(8,128)} collective-permute-done((f32[128,256]{0,1:T(8,128)}, f32[128,256]{0,1:T(8,128)}, u32[]{:S(2)}, u32[]{:S(2)}) %collective-permute-start.10) | collective-permute-done | bytes 131104 | tf_op jit(solution)/shard_map/ppermute | solution.py:15
  158.0 1.0 fusion.53
  160.5 1.6 fusion.26
  162.2 0.8 copy-done.31
  163.1 1.6 fusion.27
  164.8 0.8 copy-done.32
  165.6 1.6 fusion.28
  167.3 0.8 copy-done.33
  168.1 1.6 fusion.29
  170.6 1.6 fusion.22
  172.3 0.8 copy-done.28
  173.1 1.6 fusion.23
  174.8 0.8 copy-done.29
  175.6 1.6 fusion.24
  178.2 1.6 fusion.25
  179.9 0.8 pad_maximum_fusion.3
  180.7 0.8 pad_maximum_fusion.2
  (174 shorter events, 26.1 us)
Async XLA Ops:
  1.8 30.4 %collective-permute-start.3 = (bf16[128]{0:T(256)(128)(2,1)}, bf16[128]{0:T(256)(128)(2,1)S(1)}, u32[]{:S(2)}, u32[]{:S(2)}) collective-permute-start(bf16[128]{0:T(256)(128)(2,1)} %get-tuple-element.103), channel_id=1, source_target_pairs={{0,4},{4,8},{8,12},{12,16},{16,20},{20,24},{24,28},{1,5},{5,9},{9,... | collective-permute-start | bytes 776 | tf_op jit(solution)/shard_map/ppermute | solution.py:15
  5.3 46.7 %collective-permute-start.2 = (bf16[128]{0:T(256)(128)(2,1)}, bf16[128]{0:T(256)(128)(2,1)}, u32[]{:S(2)}, u32[]{:S(2)}) collective-permute-start(bf16[128]{0:T(256)(128)(2,1)} %get-tuple-element.103), channel_id=1, source_target_pairs={{0,8},{4,12},{8,16},{12,20},{16,24},{20,28},{1,9},{5,13},{9,17},{1... | collective-permute-start | bytes 776 | tf_op jit(solution)/shard_map/ppermute | solution.py:15
  8.8 48.0 %collective-permute-start.4 = (bf16[128,256]{1,0:T(8,128)(2,1)}, bf16[128,256]{1,0:T(8,128)(2,1)}, u32[]{:S(2)}, u32[]{:S(2)}) collective-permute-start(bf16[128,256]{1,0:T(8,128)(2,1)} %param.11), channel_id=1, source_target_pairs={{0,8},{4,12},{8,16},{12,20},{16,24},{20,28},{1,9},{5,13},{9,17},{1... | collective-permute-start | bytes 196616 | tf_op jit(solution)/shard_map/ppermute | solution.py:15
  10.7 49.8 %collective-permute-start.5 = (bf16[128,256]{1,0:T(8,128)(2,1)}, bf16[128,256]{1,0:T(8,128)(2,1)}, u32[]{:S(2)}, u32[]{:S(2)}) collective-permute-start(bf16[128,256]{1,0:T(8,128)(2,1)} %param.11), channel_id=1, source_target_pairs={{0,4},{4,8},{8,12},{12,16},{16,20},{20,24},{24,28},{1,5},{5,9},{9,... | collective-permute-start | bytes 196616 | tf_op jit(solution)/shard_map/ppermute | solution.py:15
  14.1 4.2 %copy-start.43 = (bf16[128,128]{1,0:T(8,128)(2,1)S(1)}, bf16[128,128]{1,0:T(8,128)(2,1)}, u32[]{:S(2)}) copy-start(bf16[128,128]{1,0:T(8,128)(2,1)} %param.16) | copy-start | bytes 98308
  15.7 49.5 %collective-permute-start = (bf16[128,256]{0,1:T(8,128)(2,1)}, bf16[128,256]{0,1:T(8,128)(2,1)}, u32[]{:S(2)}, u32[]{:S(2)}) collective-permute-start(bf16[128,256]{0,1:T(8,128)(2,1)} %copy.176), channel_id=1, source_target_pairs={{0,8},{4,12},{8,16},{12,20},{16,24},{20,28},{1,9},{5,13},{9,17},{1... | collective-permute-start | bytes 196616 | tf_op jit(solution)/shard_map/ppermute | solution.py:15
  18.4 0.8 copy-start.44
  19.8 0.7 copy-start.46
  20.6 2.0 %copy-start.35 = (bf16[128,2048]{1,0:T(8,128)(2,1)S(1)}, bf16[128,2048]{1,0:T(8,128)(2,1)}, u32[]{:S(2)}) copy-start(bf16[128,2048]{1,0:T(8,128)(2,1)} %param.13) | copy-start | bytes 1572868
  22.7 1.5 copy-start.36
  27.3 0.9 copy-start.39
  28.2 1.0 copy-start.40
  31.5 3.4 %copy-start.47 = (s32[128]{0:T(128)S(1)}, s32[128]{0:T(128)}, u32[]{:S(2)}) copy-start(s32[128]{0:T(128)} %param.17) | copy-start | bytes 1540
  31.5 6.1 %copy-start.38 = (f32[128,128]{1,0:T(8,128)S(1)}, f32[128,128]{1,0:T(8,128)}, u32[]{:S(2)}) copy-start(f32[128,128]{1,0:T(8,128)} %convert_element_type.183) | copy-start | bytes 196612
  32.2 5.3 %copy-start.37 = (f32[128,128]{1,0:T(8,128)S(1)}, f32[128,128]{1,0:T(8,128)}, u32[]{:S(2)}) copy-start(f32[128,128]{1,0:T(8,128)} %convert_element_type.180) | copy-start | bytes 196612
  32.2 33.0 %collective-permute-start.1 = (bf16[128,256]{0,1:T(8,128)(2,1)}, bf16[128,256]{0,1:T(8,128)(2,1)}, u32[]{:S(2)}, u32[]{:S(2)}) collective-permute-start(bf16[128,256]{0,1:T(8,128)(2,1)} %copy.176), channel_id=1, source_target_pairs={{0,4},{4,8},{8,12},{12,16},{16,20},{20,24},{24,28},{1,5},{5,9},{9,... | collective-permute-start | bytes 196616 | tf_op jit(solution)/shard_map/ppermute | solution.py:15
  37.6 1.3 copy-start.20
  39.1 1.0 copy-start.22
  41.0 0.9 copy-start.16
  42.1 7.3 %copy-start = (f32[8,64,128]{2,1,0:T(8,128)}, f32[8,64,128]{2,1,0:T(8,128)S(1)}, u32[]{:S(2)}) copy-start(f32[8,64,128]{2,1,0:T(8,128)S(1)} %convolution_bitcast_fusion.8) | copy-start | bytes 786436
  42.1 1.0 copy-start.21
  44.1 0.9 copy-start.18
  44.3 5.2 %copy-start.2 = (f32[8,64,128]{2,1,0:T(8,128)}, f32[8,64,128]{2,1,0:T(8,128)S(1)}, u32[]{:S(2)}) copy-start(f32[8,64,128]{2,1,0:T(8,128)S(1)} %convolution_bitcast_fusion.4) | copy-start | bytes 786436
  45.2 4.3 %copy-start.4 = (f32[8,64,128]{2,1,0:T(8,128)}, f32[8,64,128]{2,1,0:T(8,128)S(1)}, u32[]{:S(2)}) copy-start(f32[8,64,128]{2,1,0:T(8,128)S(1)} %convolution_bitcast_fusion.7) | copy-start | bytes 786436
  45.2 1.0 copy-start.19
  47.1 0.9 copy-start.17
  47.3 2.1 %copy-start.6 = (f32[8,64,128]{2,1,0:T(8,128)}, f32[8,64,128]{2,1,0:T(8,128)S(1)}, u32[]{:S(2)}) copy-start(f32[8,64,128]{2,1,0:T(8,128)S(1)} %convolution_bitcast_fusion.3) | copy-start | bytes 786436
  48.2 1.3 copy-start.8
  49.3 1.7 copy-start.10
  52.0 49.4 %collective-permute-start.12 = (f32[32,64,128]{2,1,0:T(8,128)}, f32[32,64,128]{2,1,0:T(8,128)}, u32[]{:S(2)}, u32[]{:S(2)}) collective-permute-start(f32[32,64,128]{2,1,0:T(8,128)} %get-tuple-element.99), channel_id=1, source_target_pairs={{4,0},{8,4},{12,8},{16,12},{20,16},{24,20},{28,24},{5,1},{9,5},{13... | collective-permute-start | bytes 3145736 | tf_op jit(solution)/shard_map/ppermute | solution.py:15
  56.8 47.6 %collective-permute-start.6 = (f32[32,64,128]{2,1,0:T(8,128)}, f32[32,64,128]{2,1,0:T(8,128)}, u32[]{:S(2)}, u32[]{:S(2)}) collective-permute-start(f32[32,64,128]{2,1,0:T(8,128)} %get-tuple-element.100), channel_id=1, source_target_pairs={{0,4},{4,8},{8,12},{12,16},{16,20},{20,24},{24,28},{1,5},{5,9},{9,... | collective-permute-start | bytes 3145736 | tf_op jit(solution)/shard_map/ppermute | solution.py:15
  59.6 1.8 copy-start.45
  60.5 0.9 copy-start.41
  62.7 1.2 copy-start.42
  65.2 1.0 copy-start.24
  66.2 1.2 copy-start.14
  66.2 1.2 copy-start.23
  74.9 10.9 %copy-start.25 = (bf16[128,512]{0,1:T(8,128)(2,1)S(1)}, bf16[128,512]{0,1:T(8,128)(2,1)}, u32[]{:S(2)}) copy-start(bf16[128,512]{0,1:T(8,128)(2,1)} %copy.239) | copy-start | bytes 393220
  74.9 11.2 %copy-start.15 = (bf16[384,256]{0,1:T(8,128)(2,1)S(1)}, bf16[384,256]{0,1:T(8,128)(2,1)}, u32[]{:S(2)}) copy-start(bf16[384,256]{0,1:T(8,128)(2,1)} %copy-done.14) | copy-start | bytes 589828
  74.9 29.5 %copy-start.11 = (f32[8,64,128]{2,1,0:T(8,128)S(1)}, f32[8,64,128]{2,1,0:T(8,128)}, u32[]{:S(2)}) copy-start(f32[8,64,128]{2,1,0:T(8,128)} %copy-done.10) | copy-start | bytes 786436
  76.6 46.0 %collective-permute-start.8 = (f32[128,256]{0,1:T(8,128)}, f32[128,256]{0,1:T(8,128)}, u32[]{:S(2)}, u32[]{:S(2)}) collective-permute-start(f32[128,256]{0,1:T(8,128)} %get-tuple-element.61), channel_id=1, source_target_pairs={{4,0},{8,4},{12,8},{16,12},{20,16},{24,20},{28,24},{5,1},{9,5},{13... | collective-permute-start | bytes 393224 | tf_op jit(solution)/shard_map/ppermute | solution.py:15
  79.7 42.9 %collective-permute-start.9 = (f32[128,256]{0,1:T(8,128)}, f32[128,256]{0,1:T(8,128)}, u32[]{:S(2)}, u32[]{:S(2)}) collective-permute-start(f32[128,256]{0,1:T(8,128)} %get-tuple-element.62), channel_id=1, source_target_pairs={{8,0},{12,4},{16,8},{20,12},{24,16},{28,20},{9,1},{13,5},{17,9},{2... | collective-permute-start | bytes 393224 | tf_op jit(solution)/shard_map/ppermute | solution.py:15
  85.8 18.7 %copy-start.5 = (f32[8,64,128]{2,1,0:T(8,128)S(1)}, f32[8,64,128]{2,1,0:T(8,128)}, u32[]{:S(2)}) copy-start(f32[8,64,128]{2,1,0:T(8,128)} %copy-done.4) | copy-start | bytes 786436
  85.8 18.6 %copy-start.7 = (f32[8,64,128]{2,1,0:T(8,128)S(1)}, f32[8,64,128]{2,1,0:T(8,128)}, u32[]{:S(2)}) copy-start(f32[8,64,128]{2,1,0:T(8,128)} %copy-done.6) | copy-start | bytes 786436
  85.8 18.6 %copy-start.9 = (f32[8,64,128]{2,1,0:T(8,128)S(1)}, f32[8,64,128]{2,1,0:T(8,128)}, u32[]{:S(2)}) copy-start(f32[8,64,128]{2,1,0:T(8,128)} %copy-done.8) | copy-start | bytes 786436
  86.1 24.6 %copy-start.12 = (f32[384,128]{0,1:T(8,128)}, f32[384,128]{0,1:T(8,128)S(1)}, u32[]{:S(2)}) copy-start(f32[384,128]{0,1:T(8,128)S(1)} %convolution_bitcast_fusion.11) | copy-start | bytes 589828
  86.1 18.3 %copy-start.1 = (f32[8,64,128]{2,1,0:T(8,128)S(1)}, f32[8,64,128]{2,1,0:T(8,128)}, u32[]{:S(2)}) copy-start(f32[8,64,128]{2,1,0:T(8,128)} %copy-done) | copy-start | bytes 786436
  86.1 18.3 %copy-start.3 = (f32[8,64,128]{2,1,0:T(8,128)S(1)}, f32[8,64,128]{2,1,0:T(8,128)}, u32[]{:S(2)}) copy-start(f32[8,64,128]{2,1,0:T(8,128)} %copy-done.2) | copy-start | bytes 786436
  107.6 52.9 %collective-permute-start.13 = (f32[32,64,128]{2,1,0:T(8,128)}, f32[32,64,128]{2,1,0:T(8,128)}, u32[]{:S(2)}, u32[]{:S(2)}) collective-permute-start(f32[32,64,128]{2,1,0:T(8,128)} %get-tuple-element.97), channel_id=1, source_target_pairs={{4,0},{8,4},{12,8},{16,12},{20,16},{24,20},{28,24},{5,1},{9,5},{13... | collective-permute-start | bytes 3145736 | tf_op jit(solution)/shard_map/ppermute | solution.py:15
  110.7 8.5 %copy-start.34 = (bf16[128,4,128]{2,0,1:T(8,128)(2,1)S(1)}, bf16[128,4,128]{2,0,1:T(8,128)(2,1)}, u32[]{:S(2)}) copy-start(bf16[128,4,128]{2,0,1:T(8,128)(2,1)} %convolution_convert_fusion.1) | copy-start | bytes 393220
  111.4 12.3 %copy-start.26 = (f32[32,64,128]{2,1,0:T(8,128)S(1)}, f32[32,64,128]{2,1,0:T(8,128)}, u32[]{:S(2)}) copy-start(f32[32,64,128]{2,1,0:T(8,128)} %get-tuple-element.98) | copy-start | bytes 3145732
  111.4 46.5 %collective-permute-start.10 = (f32[128,256]{0,1:T(8,128)}, f32[128,256]{0,1:T(8,128)}, u32[]{:S(2)}, u32[]{:S(2)}) collective-permute-start(f32[128,256]{0,1:T(8,128)} %get-tuple-element.59), channel_id=1, source_target_pairs={{4,0},{8,4},{12,8},{16,12},{20,16},{24,20},{28,24},{5,1},{9,5},{13... | collective-permute-start | bytes 393224 | tf_op jit(solution)/shard_map/ppermute | solution.py:15
  117.3 40.7 %collective-permute-start.11 = (f32[128,256]{0,1:T(8,128)}, f32[128,256]{0,1:T(8,128)}, u32[]{:S(2)}, u32[]{:S(2)}) collective-permute-start(f32[128,256]{0,1:T(8,128)} %get-tuple-element.60), channel_id=1, source_target_pairs={{8,0},{12,4},{16,8},{20,12},{24,16},{28,20},{9,1},{13,5},{17,9},{2... | collective-permute-start | bytes 393224 | tf_op jit(solution)/shard_map/ppermute | solution.py:15
  122.6 35.4 %copy-start.13 = (f32[384,128]{0,1:T(8,128)S(1)}, f32[384,128]{0,1:T(8,128)}, u32[]{:S(2)}) copy-start(f32[384,128]{0,1:T(8,128)} %copy-done.12) | copy-start | bytes 589828
  123.7 46.1 %collective-permute-start.7 = (f32[32,64,128]{2,1,0:T(8,128)S(1)}, f32[32,64,128]{2,1,0:T(8,128)}, u32[]{:S(2)}, u32[]{:S(2)}) collective-permute-start(f32[32,64,128]{2,1,0:T(8,128)S(1)} %copy-done.26), channel_id=1, source_target_pairs={{0,4},{4,8},{8,12},{12,16},{16,20},{20,24},{24,28},{1,5},{5,9},{9,... | collective-permute-start | bytes 3145736 | tf_op jit(solution)/shard_map/ppermute | solution.py:15
  162.1 1.0 copy-start.31
  164.6 1.0 copy-start.32
  167.1 1.0 copy-start.33
  169.7 1.0 copy-start.27
  172.2 1.0 copy-start.28
  174.7 1.0 copy-start.29
  177.2 1.0 copy-start.30
where the time goes:
time: 185 us; the launch traced here: 182 us
  waiting for transfers between devices  48.1 us (26%)
  starting transfers between devices  45.2 us (24%)
  matrix products  34.2 us (18%)
  local copies, waits for them, and re-layouts  27.7 us (15%)
  other arithmetic  23.5 us (13%)
  between operations  2.75 us (1%)
    ppermute x14, waiting for transfers between devices, passed_along(): return lax.ppermute(block, axis, route)  48.1 us
    ppermute x14, starting transfers between devices, passed_along(): return lax.ppermute(block, axis, route)  45.2 us
    unnamed x105, local copies, waits for them, and re-layouts  16.8 us
    dot_general x4, matrix products, shards(): jnp.einsum('hpn,hsn->shp', carry_out[low_head:high_head], write_w.astype(...  6.32 us
    dot_general x4, matrix products, shards(): jnp.einsum('hpn,htn->thp', carry_in[low_head:high_head], read_w.astype(jn...  6.24 us
    dot_general x2, matrix products, attn_grads(): jnp.einsum('its,tid->sd', score_gradient, query_grp, preferred_element_ty...  5.09 us
    add x2, other arithmetic, combine_carry(): nearer[0][:, None, None] * earlier[1] + nearer[1]  4.67 us
    dot_general x4, matrix products, shards(): jnp.einsum('hts,shp->thp', weights, inputs, preferred_element_type=jnp.fl...  3.95 us
  transfers between devices with their start and end apart: 14, of which 3 were waited for; matrix products, arithmetic and copies ran while one was open for 37% of the time, Pallas kernels for 0%

commit v1 on v0

v1 whole, which is shorter than its diff:
```python
import functools
import math

import jax
import jax.numpy as jnp
from jax import lax
from jax.experimental import pallas as pl
from jax.experimental.pallas import tpu as pltpu
from jax.sharding import PartitionSpec as P

HEAD_CHANNELS = 128
BF16 = jnp.bfloat16
F32 = jnp.float32
NT = (((1,), (1,)), ((), ()))
TN = (((0,), (0,)), ((), ()))


def passed_along(block, axis, distance):
    devices = range(lax.axis_size(axis))
    route = [(i - distance, i) for i in devices if i - distance in devices]
    return lax.ppermute(block, axis, route)


def dot(a, b, dims=(((1,), (0,)), ((), ()))):
    return lax.dot_general(a, b, dims, preferred_element_type=F32)


def iota(shape, dim):
    return lax.broadcasted_iota(jnp.int32, shape, dim)


def split3(v):
    hi = v.astype(BF16)
    rest = v - hi.astype(F32)
    mid = rest.astype(BF16)
    lo = (rest - mid.astype(F32)).astype(BF16)
    return hi, mid, lo


def aux_parts(aux, heads):
    wide = aux.astype(F32)
    lam = wide[:, :heads] + wide[:, heads : 2 * heads] + wide[:, 2 * heads : 3 * heads]
    return lam, wide[:, 3 * heads : 4 * heads]


def pack_kernel(heads, key_ref, value_ref, write_ref, read_ref, decay_ref, doc_ref, m_ref, n_ref):
    tokens = key_ref.shape[0]
    kv = key_ref.shape[1]
    tri = jnp.where(
        iota((tokens, tokens), 0) >= iota((tokens, tokens), 1), 1.0, 0.0
    ).astype(BF16)
    lam = sum(dot(tri, part) for part in split3(decay_ref[...]))
    docs = jnp.broadcast_to(doc_ref[...].astype(F32) + 1.0, (tokens, tokens)).T
    parts = [part.astype(F32) for part in split3(lam)] + [docs[:, :heads]]
    aux = jnp.concatenate(parts, axis=1).astype(BF16)
    state = write_ref.shape[1]
    m_ref[:, :kv] = key_ref[...]
    m_ref[:, kv : 2 * kv] = value_ref[...]
    m_ref[:, 2 * kv : 2 * kv + state] = write_ref[...]
    m_ref[:, 2 * kv + state :] = aux
    n_ref[:, :state] = read_ref[...]
    n_ref[:, state:] = aux


def attn_kernel(
    kv, docs_at, doc_ref, m0, m1, m2, q_ref, cot_ref, out_ref, own_ref, back1_ref, back2_ref
):
    tokens = m0.shape[0]
    group = q_ref.shape[1] // HEAD_CHANNELS
    inv_root = 1.0 / math.sqrt(HEAD_CHANNELS)
    width = HEAD_CHANNELS
    key_cols = pl.ds(pl.multiple_of(pl.program_id(0) * width, width), width)
    value_cols = pl.ds(pl.multiple_of(kv + pl.program_id(0) * width, width), width)
    tiles = (m2, m1, m0)
    keys = jnp.concatenate([tile[:, key_cols] for tile in tiles], axis=0)
    values = jnp.concatenate([tile[:, value_cols] for tile in tiles], axis=0)
    span = keys.shape[0]
    doc_s = jnp.concatenate(
        [tile[:, docs_at : docs_at + 1].astype(F32) for tile in tiles], axis=0
    )
    doc_t = doc_ref[...].astype(F32) + 1.0
    inside = (doc_s == doc_t) & (
        iota((span, tokens), 0) - (span - tokens) <= iota((span, tokens), 1)
    )
    inside = jnp.where(inside, 1.0, 0.0)
    inside = jnp.concatenate([inside] * group, axis=1) > 0.5
    query = jnp.concatenate(
        [q_ref[:, i * width : (i + 1) * width] for i in range(group)], axis=0
    )
    cot = jnp.concatenate(
        [cot_ref[:, i * width : (i + 1) * width] for i in range(group)], axis=0
    )
    score = jnp.where(inside, dot(keys, query, NT) * inv_root, -1e30)
    raised = jnp.exp(score - jnp.max(score, axis=0, keepdims=True))
    raised = jnp.where(inside, raised, 0.0)
    prob = (raised * (1.0 / jnp.sum(raised, axis=0, keepdims=True))).astype(BF16)
    out = dot(values, prob, TN).T
    for i in range(group):
        out_ref[:, i * width : (i + 1) * width] = out[i * tokens : (i + 1) * tokens].astype(BF16)
    prob_grad = dot(values, cot, NT)
    prob32 = prob.astype(F32)
    inner = jnp.sum(prob32 * prob_grad, axis=0, keepdims=True)
    score_grad = (prob32 * (prob_grad - inner) * inv_root).astype(BF16)
    key_grad = dot(score_grad, query)
    value_grad = dot(prob, cot)
    back2_ref[:, :width] = key_grad[:tokens].astype(BF16)
    back2_ref[:, width:] = value_grad[:tokens].astype(BF16)
    back1_ref[:, :width] = key_grad[tokens : 2 * tokens].astype(BF16)
    back1_ref[:, width:] = value_grad[tokens : 2 * tokens].astype(BF16)
    own_ref[:, :width] = key_grad[2 * tokens :]
    own_ref[:, width:] = value_grad[2 * tokens :]


def local_kernel(
    heads, head_width, write_at, doc_ref, m0, n0, x_ref, cot_ref, mixed_ref, grad_ref
):
    tokens = m0.shape[0]
    state = n0.shape[1] - 4 * heads
    cols = x_ref.shape[1]
    step_heads = cols // head_width
    lanes = 4 * heads
    aux = n0[:, state:]
    pick = (iota((lanes, lanes), 0) % heads) == (
        iota((lanes, lanes), 1) + pl.program_id(0) * step_heads
    )
    pick &= (iota((lanes, lanes), 0) < 3 * heads) & (iota((lanes, lanes), 1) < step_heads)
    lam = dot(aux, jnp.where(pick, 1.0, 0.0).astype(BF16))
    lam_t = lam.T
    doc_col = aux[:, 3 * heads : 3 * heads + 1].astype(F32)
    doc_row = doc_ref[...].astype(F32) + 1.0
    inside = (iota((tokens, tokens), 0) >= iota((tokens, tokens), 1)) & (doc_col == doc_row)
    score = dot(n0[:, :state], m0[:, write_at : write_at + state], NT)
    per = HEAD_CHANNELS // head_width
    lane_head = iota((tokens, HEAD_CHANNELS), 1) // head_width
    for pair in range(step_heads // per):
        at = slice(pair * HEAD_CHANNELS, (pair + 1) * HEAD_CHANNELS)
        x = x_ref[:, at]
        cot = cot_ref[:, at]
        mixed = grad = None
        for j in range(per):
            head = pair * per + j
            gap = lam[:, head : head + 1] - lam_t[head : head + 1, :]
            weights = (jnp.exp(jnp.where(inside, gap, -jnp.inf)) * score).astype(BF16)
            mixed_j = dot(weights, x)
            grad_j = dot(weights, cot, TN)
            mixed = mixed_j if j == 0 else jnp.where(lane_head == j, mixed_j, mixed)
            grad = grad_j if j == 0 else jnp.where(lane_head == j, grad_j, grad)
        mixed_ref[:, at] = mixed
        grad_ref[:, at] = grad


def final_kernel(
    heads,
    head_width,
    write_at,
    m0,
    m1,
    m2,
    n0,
    n1,
    n2,
    own_ref,
    r1_ref,
    r2_ref,
    x1_ref,
    x2_ref,
    c1_ref,
    c2_ref,
    mixed_ref,
    grad_ref,
    mixer_out_ref,
    grad_input_ref,
    grad_key_ref,
    grad_value_ref,
):
    tokens = m0.shape[0]
    state = n0.shape[1] - 4 * heads
    cols = x1_ref.shape[1]
    step_heads = cols // head_width

    @pl.when(pl.program_id(0) == 0)
    def _():
        total = own_ref[...] + r1_ref[...].astype(F32) + r2_ref[...].astype(F32)
        width = HEAD_CHANNELS
        for g in range(own_ref.shape[1] // (2 * width)):
            grad_key_ref[:, g * width : (g + 1) * width] = total[
                :, 2 * g * width : (2 * g + 1) * width
            ].astype(BF16)
            grad_value_ref[:, g * width : (g + 1) * width] = total[
                :, (2 * g + 1) * width : (2 * g + 2) * width
            ].astype(BF16)

    spread = (iota((heads, cols), 0) - pl.program_id(0) * step_heads) == (
        iota((heads, cols), 1) // head_width
    )
    spread = jnp.where(spread, 1.0, 0.0).astype(BF16)

    def widen(scale):
        return sum(dot(part, spread) for part in split3(scale))

    def same(a, b):
        return jnp.where(a == b, 1.0, 0.0)

    write_cols = slice(write_at, write_at + state)
    lam0, doc0 = aux_parts(n0[:, state:], heads)
    lam1, doc1 = aux_parts(m1[:, write_at + state :], heads)
    lam2, doc2 = aux_parts(m2[:, write_at + state :], heads)
    next1, next_doc1 = aux_parts(n1[:, state:], heads)
    next2, next_doc2 = aux_parts(n2[:, state:], heads)

    def last(v):
        return v[tokens - 1 : tokens]

    entry0 = jnp.exp(lam0) * same(doc0, last(doc1))
    exit1 = jnp.exp(last(lam1) - lam1) * same(doc1, last(doc1))
    gain1 = jnp.exp(last(lam1)) * same(last(doc1), last(doc2))
    exit2 = jnp.exp(last(lam2) - lam2) * same(doc2, last(doc2)) * gain1
    exit0 = jnp.exp(last(lam0) - lam0) * same(doc0, last(doc0))
    entry1 = jnp.exp(next1) * same(next_doc1, last(doc0))
    next_gain = jnp.exp(last(next1)) * same(last(next_doc1), last(doc0))
    entry2 = jnp.exp(next2) * same(next_doc2, last(next_doc1)) * next_gain

    read0 = n0[:, :state]
    write0 = m0[:, write_cols]
    score1 = dot(read0, m1[:, write_cols], NT).astype(BF16)
    score2 = dot(read0, m2[:, write_cols], NT).astype(BF16)
    back1 = dot(write0, n1[:, :state], NT).astype(BF16)
    back2 = dot(write0, n2[:, :state], NT).astype(BF16)

    def scaled(ref, scale):
        return (ref[...].astype(F32) * widen(scale)).astype(BF16)

    carried = dot(score1, scaled(x1_ref, exit1)) + dot(score2, scaled(x2_ref, exit2))
    mixer_out_ref[...] = (mixed_ref[...] + widen(entry0) * carried).astype(BF16)
    returned = dot(back1, scaled(c1_ref, entry1)) + dot(back2, scaled(c2_ref, entry2))
    grad_input_ref[...] = (grad_ref[...] + widen(exit0) * returned).astype(BF16)


def whole(shape):
    return pl.BlockSpec(shape, lambda i: (0, 0))


def columns(rows, cols):
    return pl.BlockSpec((rows, cols), lambda i: (0, i))


def shards(
    query_head_matrix,
    key_head_matrix,
    value_head_matrix,
    ssm_input,
    log_decay,
    state_write,
    state_read,
    document_ids,
    attention_output_gradient,
    cot_mixer,
):
    tokens, kv = key_head_matrix.shape
    kv_local = kv // HEAD_CHANNELS
    heads = log_decay.shape[1]
    state = state_write.shape[1]
    head_width = ssm_input.shape[1] // heads
    group_cols = query_head_matrix.shape[1] // kv_local
    write_at = 2 * kv
    doc_row = document_ids.reshape(1, tokens)
    aux = 4 * heads
    m_cols = 2 * kv + state + aux
    n_cols = state + aux
    step_cols = min(512, ssm_input.shape[1])
    steps = ssm_input.shape[1] // step_cols
    shape = jax.ShapeDtypeStruct
    params = pltpu.CompilerParams(vmem_limit_bytes=48 * 1024 * 1024)

    m0, n0 = pl.pallas_call(
        functools.partial(pack_kernel, heads),
        out_shape=(shape((tokens, m_cols), BF16), shape((tokens, n_cols), BF16)),
        compiler_params=params,
        name="pack",
    )(key_head_matrix, value_head_matrix, state_write, state_read, log_decay, doc_row)
    m1 = passed_along(m0, "ctx", 1)
    m2 = passed_along(m0, "ctx", 2)
    n1 = passed_along(n0, "ctx", -1)
    n2 = passed_along(n0, "ctx", -2)
    x1 = passed_along(ssm_input, "ctx", 1)
    c1 = passed_along(cot_mixer, "ctx", -1)
    x2 = passed_along(ssm_input, "ctx", 2)
    c2 = passed_along(cot_mixer, "ctx", -2)

    mixed, grad = pl.pallas_call(
        functools.partial(local_kernel, heads, head_width, write_at),
        grid=(steps,),
        in_specs=[
            whole((1, tokens)),
            whole((tokens, m_cols)),
            whole((tokens, n_cols)),
            columns(tokens, step_cols),
            columns(tokens, step_cols),
        ],
        out_specs=[columns(tokens, step_cols)] * 2,
        out_shape=(shape(ssm_input.shape, F32),) * 2,
        compiler_params=params,
        name="local_mixer",
    )(doc_row, m0, n0, ssm_input, cot_mixer)

    kv2 = 2 * HEAD_CHANNELS
    attention_out, own, back1, back2 = pl.pallas_call(
        functools.partial(attn_kernel, kv, 2 * kv + state + 3 * heads),
        grid=(kv_local,),
        in_specs=[whole((1, tokens))]
        + [whole((tokens, m_cols))] * 3
        + [columns(tokens, group_cols)] * 2,
        out_specs=[columns(tokens, group_cols)] + [columns(tokens, kv2)] * 3,
        out_shape=(
            shape(query_head_matrix.shape, BF16),
            shape((tokens, 2 * kv), F32),
            shape((tokens, 2 * kv), BF16),
            shape((tokens, 2 * kv), BF16),
        ),
        compiler_params=params,
        name="attention",
    )(doc_row, m0, m1, m2, query_head_matrix, attention_output_gradient)
    r1 = passed_along(back1, "ctx", -1)
    r2 = passed_along(back2, "ctx", -2)

    mixer_out, grad_input, grad_key, grad_value = pl.pallas_call(
        functools.partial(final_kernel, heads, head_width, write_at),
        grid=(steps,),
        in_specs=[whole((tokens, m_cols))] * 3
        + [whole((tokens, n_cols))] * 3
        + [whole((tokens, 2 * kv))] * 3
        + [columns(tokens, step_cols)] * 6,
        out_specs=[columns(tokens, step_cols)] * 2 + [whole((tokens, kv))] * 2,
        out_shape=(
            shape(ssm_input.shape, BF16),
            shape(cot_mixer.shape, BF16),
            shape(key_head_matrix.shape, BF16),
            shape(value_head_matrix.shape, BF16),
        ),
        compiler_params=params,
        name="final",
    )(m0, m1, m2, n0, n1, n2, own, r1, r2, x1, x2, c1, c2, mixed, grad)
    return (attention_out, mixer_out, grad_key, grad_value, grad_input)


def solution(mesh):
    return jax.shard_map(
        shards,
        mesh=mesh,
        in_specs=(
            P("ctx", "tp"),
            P("ctx", "tp"),
            P("ctx", "tp"),
            P("ctx", "tp"),
            P("ctx", "tp"),
            P("ctx", None),
            P("ctx", None),
            P("ctx"),
            P("ctx", "tp"),
            P("ctx", "tp"),
        ),
        out_specs=(P("ctx", "tp"), P("ctx", "tp"), P("ctx", "tp"), P("ctx", "tp"), P("ctx", "tp")),
        check_vma=False,
    )
```

time: 185 us -> 71.4 us (0.39); the launches traced: 182 us -> 70.8 us
  matrix products: 34.2 us -> 0 us
  waiting for transfers between devices: 48.1 us -> 23.8 us
  other arithmetic: 23.5 us -> 0 us
  local copies, waits for them, and re-layouts: 27.7 us -> 4.84 us
  starting transfers between devices: 45.2 us -> 28.3 us
  Pallas kernels: 0 us -> 13 us
  between operations: 2.75 us -> 0.86 us
    dot_general x33 -> x0, matrix products: 31.7 us -> none  [the longest x4 6.32 us: shards(): jnp.einsum('hpn,hsn->shp', carry_out[low_head:high_head], write_w.astype(...]
    ppermute x14 -> x10, waiting for transfers between devices: 48.1 us -> 23.8 us  [passed_along(): return lax.ppermute(block, axis, route)]
    ppermute x14 -> x10, starting transfers between devices: 45.2 us -> 28.3 us  [passed_along(): return lax.ppermute(block, axis, route)]
    pallas_call x0 -> x4, Pallas kernels: none -> 13 us  [the longest x1 6.35 us: shards(): pl.pallas_call(functools.partial(final_kernel, heads, head_width, write_a...]
    unnamed x105 -> x21, local copies, waits for them, and re-layouts: 16.8 us -> 4.84 us
    convert_element_type x10 -> x0, other arithmetic: 10.3 us -> none  [the longest x2 2.44 us: attn_probs(): (raised / jnp.sum(raised, axis=-1, keepdims=True)).astype(jnp.bfloat16)]
    slice x23 -> x0, local copies, waits for them, and re-layouts: 7.96 us -> none  [the longest x5 3.07 us: shards(): cot_mixer[:, low_col:high_col].reshape(tokens, head_block, head_width)]
    concatenate x7 -> x0, other arithmetic: 6.78 us -> none  [the longest x1 1.74 us: shards(): key_window = jnp.concatenate(key_cols, axis=1)]
  transfers between devices with their start and end apart: 14 -> 10, of which waited for: 3 -> 3; matrix products, arithmetic and copies ran while one was open for 37% -> 0% of each run, Pallas kernels for 0% -> 9%
where the time goes in v1:
time: 71.4 us; the launch traced here: 70.8 us
  starting transfers between devices  28.3 us (40%)
  waiting for transfers between devices  23.8 us (33%)
  Pallas kernels  13 us (18%)
  local copies, waits for them, and re-layouts  4.84 us (7%)
  between operations  0.86 us (1%)
    ppermute x10, starting transfers between devices, passed_along(): return lax.ppermute(block, axis, route)  28.3 us
    ppermute x10, waiting for transfers between devices, passed_along(): return lax.ppermute(block, axis, route)  23.8 us
    pallas_call x1, Pallas kernels, shards(): pl.pallas_call(functools.partial(final_kernel, heads, head_width, write_a...  6.35 us
    unnamed x21, local copies, waits for them, and re-layouts  4.84 us
    pallas_call x1, Pallas kernels, shards(): pl.pallas_call(functools.partial(attn_kernel, kv, 2 * kv + state + 3 * he...  3.21 us
    pallas_call x1, Pallas kernels, shards(): pl.pallas_call(functools.partial(local_kernel, heads, head_width, write_a...  3.14 us
  transfers between devices with their start and end apart: 10, of which 3 were waited for; matrix products, arithmetic and copies ran while one was open for 0% of the time, Pallas kernels for 9%

profile of v1, /device:TPU:14, one launch (start us, length us, event | category | flops | bytes accessed | tf_op | source)
XLA Modules:
  0.0 70.8 jit_solution(8017102031109533384)
XLA Ops:
  0.6 0.0 copy-start.4
  0.6 0.0 copy-start.2
  0.7 0.9 %copy.15.decay_ref = f32[128,32]{1,0:T(8,128)S(1)} copy(f32[128,32]{0,1:T(8,128)} %param.14) | data formatting | bytes 32768 | tf_op args[4]
  1.5 0.0 copy-done.4
  1.5 0.0 copy-start.5
  1.5 0.8 %copy-done.5 = bf16[128,256]{1,0:T(8,128)(2,1)S(1)} copy-done((bf16[128,256]{1,0:T(8,128)(2,1)S(1)}, bf16[128,256]{1,0:T(8,128)(2,1)}, u32[]{:S(2)}) %copy-start.5) | copy-done | bytes 65560
  2.4 0.0 copy-start.6
  2.4 0.8 %copy-done.6 = bf16[128,128]{1,0:T(8,128)(2,1)S(1)} copy-done((bf16[128,128]{1,0:T(8,128)(2,1)S(1)}, bf16[128,128]{1,0:T(8,128)(2,1)}, u32[]{:S(2)}) %copy-start.6) | copy-done | bytes 32792
  3.1 0.0 copy-start.7
  3.1 0.8 %copy-done.7 = bf16[128,128]{1,0:T(8,128)(2,1)S(1)} copy-done((bf16[128,128]{1,0:T(8,128)(2,1)S(1)}, bf16[128,128]{1,0:T(8,128)(2,1)}, u32[]{:S(2)}) %copy-start.7) | copy-done | bytes 32792
  3.9 0.0 copy-start.8
  3.9 0.7 copy-done.8
  4.5 0.3 pack.1
  4.8 0.0 copy-start.9
  4.8 3.5 %collective-permute-start.1 = (bf16[128,768]{1,0:T(8,128)(2,1)S(1)}, bf16[128,768]{1,0:T(8,128)(2,1)S(1)}, u32[]{:S(2)}, u32[]{:S(2)}) collective-permute-start(bf16[128,768]{1,0:T(8,128)(2,1)S(1)} %get-tuple-element.17.m0), channel_id=1, source_target_pairs={{0,8},{4,12},{8,16},{12,20},{16,24},{20,28},{1,9},{5,13},{9,17},{1... | collective-permute-start | bytes 589832 | tf_op jit(solution)/shard_map/ppermute | solution.py:21
  8.3 0.0 copy-start
  8.3 0.0 copy-start.1
  8.3 2.5 %collective-permute-start.3 = (bf16[128,256]{1,0:T(8,128)(2,1)S(1)}, bf16[128,256]{1,0:T(8,128)(2,1)S(1)}, u32[]{:S(2)}, u32[]{:S(2)}) collective-permute-start(bf16[128,256]{1,0:T(8,128)(2,1)S(1)} %get-tuple-element.19.n0), channel_id=1, source_target_pairs={{8,0},{12,4},{16,8},{20,12},{24,16},{28,20},{9,1},{13,5},{17,9},{2... | collective-permute-start | bytes 196616 | tf_op jit(solution)/shard_map/ppermute | solution.py:21
  10.8 3.4 %collective-permute-start = (bf16[128,768]{1,0:T(8,128)(2,1)S(1)}, bf16[128,768]{1,0:T(8,128)(2,1)S(1)}, u32[]{:S(2)}, u32[]{:S(2)}) collective-permute-start(bf16[128,768]{1,0:T(8,128)(2,1)S(1)} %get-tuple-element.17.m0), channel_id=1, source_target_pairs={{0,4},{4,8},{8,12},{12,16},{16,20},{20,24},{24,28},{1,5},{5,9},{9,... | collective-permute-start | bytes 589832 | tf_op jit(solution)/shard_map/ppermute | solution.py:21
  14.3 3.4 %collective-permute-start.6 = (bf16[128,2048]{1,0:T(8,128)(2,1)}, bf16[128,2048]{1,0:T(8,128)(2,1)S(1)}, u32[]{:S(2)}, u32[]{:S(2)}) collective-permute-start(bf16[128,2048]{1,0:T(8,128)(2,1)} %x_ref.1), channel_id=1, source_target_pairs={{0,4},{4,8},{8,12},{12,16},{16,20},{20,24},{24,28},{1,5},{5,9},{9,... | collective-permute-start | bytes 1572872 | tf_op jit(solution)/shard_map/ppermute | solution.py:21
  17.7 3.5 %collective-permute-start.7 = (bf16[128,2048]{1,0:T(8,128)(2,1)}, bf16[128,2048]{1,0:T(8,128)(2,1)S(1)}, u32[]{:S(2)}, u32[]{:S(2)}) collective-permute-start(bf16[128,2048]{1,0:T(8,128)(2,1)} %x_ref.1), channel_id=1, source_target_pairs={{0,8},{4,12},{8,16},{12,20},{16,24},{20,28},{1,9},{5,13},{9,17},{1... | collective-permute-start | bytes 1572872 | tf_op jit(solution)/shard_map/ppermute | solution.py:21
  21.2 0.0 collective-permute-done.3.n2
  21.2 2.4 %collective-permute-start.8 = (bf16[128,2048]{1,0:T(8,128)(2,1)}, bf16[128,2048]{1,0:T(8,128)(2,1)S(1)}, u32[]{:S(2)}, u32[]{:S(2)}) collective-permute-start(bf16[128,2048]{1,0:T(8,128)(2,1)} %cot_ref.3), channel_id=1, source_target_pairs={{4,0},{8,4},{12,8},{16,12},{20,16},{24,20},{28,24},{5,1},{9,5},{13... | collective-permute-start | bytes 1572872 | tf_op jit(solution)/shard_map/ppermute | solution.py:21
  23.7 0.0 collective-permute-done.1.m2
  23.7 2.4 %collective-permute-start.9 = (bf16[128,2048]{1,0:T(8,128)(2,1)}, bf16[128,2048]{1,0:T(8,128)(2,1)S(1)}, u32[]{:S(2)}, u32[]{:S(2)}) collective-permute-start(bf16[128,2048]{1,0:T(8,128)(2,1)} %cot_ref.3), channel_id=1, source_target_pairs={{8,0},{12,4},{16,8},{20,12},{24,16},{28,20},{9,1},{13,5},{17,9},{2... | collective-permute-start | bytes 1572872 | tf_op jit(solution)/shard_map/ppermute | solution.py:21
  26.1 0.0 collective-permute-done.m1
  26.1 2.8 %collective-permute-start.2 = (bf16[128,256]{1,0:T(8,128)(2,1)S(1)}, bf16[128,256]{1,0:T(8,128)(2,1)S(1)}, u32[]{:S(2)}, u32[]{:S(2)}) collective-permute-start(bf16[128,256]{1,0:T(8,128)(2,1)S(1)} %get-tuple-element.19.n0), channel_id=1, source_target_pairs={{4,0},{8,4},{12,8},{16,12},{20,16},{24,20},{28,24},{5,1},{9,5},{13... | collective-permute-start | bytes 196616 | tf_op jit(solution)/shard_map/ppermute | solution.py:21
  28.9 0.0 copy-done.2
  29.0 0.0 copy-done.9
  29.0 0.0 copy-start.3
  29.0 0.9 %copy-done.3 = bf16[128,1024]{1,0:T(8,128)(2,1)S(1)} copy-done((bf16[128,1024]{1,0:T(8,128)(2,1)S(1)}, bf16[128,1024]{1,0:T(8,128)(2,1)}, u32[]{:S(2)}) %copy-start.3) | copy-done | bytes 262168
  29.9 3.2 %attention.1 = (bf16[128,1024]{1,0:T(8,128)(2,1)}, f32[128,512]{1,0:T(8,128)S(1)}, bf16[128,512]{1,0:T(8,128)(2,1)S(1)}, bf16[128,512]{1,0:T(8,128)(2,1)S(1)}) custom-call(s32[1,128]{1,0:T(1,128)S(1)} %bitcast.2, bf16[128,768]{1,0:T(8,128)(2,1)S(1)} %get-tuple-element.17.m0, bf16[128,768]{1,0:T(8,128)(2,1)S(1)} %collective-permute-done.m1, ...), custom_call_target="tpu_custom_call" | custom-call | tf_op jit(solution)/shard_map/attention/pallas_call | solution.py:307
  33.1 16.0 %collective-permute-done.2.n1 = bf16[128,256]{1,0:T(8,128)(2,1)S(1)} collective-permute-done((bf16[128,256]{1,0:T(8,128)(2,1)S(1)}, bf16[128,256]{1,0:T(8,128)(2,1)S(1)}, u32[]{:S(2)}, u32[]{:S(2)}) %collective-permute-start.2) | collective-permute-done | bytes 65568 | tf_op jit(solution)/shard_map/ppermute | solution.py:21
  49.2 1.9 %collective-permute-start.4 = (bf16[128,512]{1,0:T(8,128)(2,1)S(1)}, bf16[128,512]{1,0:T(8,128)(2,1)S(1)}, u32[]{:S(2)}, u32[]{:S(2)}) collective-permute-start(bf16[128,512]{1,0:T(8,128)(2,1)S(1)} %get-tuple-element.21), channel_id=1, source_target_pairs={{4,0},{8,4},{12,8},{16,12},{20,16},{24,20},{28,24},{5,1},{9,5},{13... | collective-permute-start | bytes 393224 | tf_op jit(solution)/shard_map/ppermute | solution.py:21
  51.1 6.4 %collective-permute-done.4.r1_ref = bf16[128,512]{1,0:T(8,128)(2,1)S(1)} collective-permute-done((bf16[128,512]{1,0:T(8,128)(2,1)S(1)}, bf16[128,512]{1,0:T(8,128)(2,1)S(1)}, u32[]{:S(2)}, u32[]{:S(2)}) %collective-permute-start.4) | collective-permute-done | bytes 131104 | tf_op jit(solution)/shard_map/ppermute | solution.py:21
  57.5 2.4 %collective-permute-start.5 = (bf16[128,512]{1,0:T(8,128)(2,1)S(1)}, bf16[128,512]{1,0:T(8,128)(2,1)S(1)}, u32[]{:S(2)}, u32[]{:S(2)}) collective-permute-start(bf16[128,512]{1,0:T(8,128)(2,1)S(1)} %get-tuple-element.22), channel_id=1, source_target_pairs={{8,0},{12,4},{16,8},{20,12},{24,16},{28,20},{9,1},{13,5},{17,9},{2... | collective-permute-start | bytes 393224 | tf_op jit(solution)/shard_map/ppermute | solution.py:21
  59.9 0.0 copy-done
  59.9 0.0 copy-done.1
  59.9 3.1 %local_mixer.1 = (f32[128,2048]{1,0:T(8,128)S(1)}, f32[128,2048]{1,0:T(8,128)S(1)}) custom-call(s32[1,128]{1,0:T(1,128)S(1)} %bitcast.3, bf16[128,768]{1,0:T(8,128)(2,1)S(1)} %get-tuple-element.17.m0, bf16[128,256]{1,0:T(8,128)(2,1)S(1)} %get-tuple-element.19.n0, bf16[128,2048]{1,0:T(8,128)(2,1)S(1)} %copy-done, bf16[128,2048]{1,0:T(8,128)(2,1)S(1)} %copy-done.1), custom_call_target="tpu_custom_call" | custom-call | tf_op jit(solution)/shard_map/local_mixer/pallas_call | solution.py:290
  63.1 1.3 %collective-permute-done.5.r2_ref = bf16[128,512]{1,0:T(8,128)(2,1)S(1)} collective-permute-done((bf16[128,512]{1,0:T(8,128)(2,1)S(1)}, bf16[128,512]{1,0:T(8,128)(2,1)S(1)}, u32[]{:S(2)}, u32[]{:S(2)}) %collective-permute-start.5) | collective-permute-done | bytes 131104 | tf_op jit(solution)/shard_map/ppermute | solution.py:21
  64.4 0.0 collective-permute-done.6.x1_ref
  64.4 0.0 collective-permute-done.7.x2_ref
  64.4 0.0 collective-permute-done.8.c1_ref
  64.4 0.0 collective-permute-done.9.c2_ref
  64.4 6.3 %final.1 = (bf16[128,2048]{1,0:T(8,128)(2,1)}, bf16[128,2048]{1,0:T(8,128)(2,1)}, bf16[128,256]{1,0:T(8,128)(2,1)}, bf16[128,256]{1,0:T(8,128)(2,1)}) custom-call(bf16[128,768]{1,0:T(8,128)(2,1)S(1)} %get-tuple-element.17.m0, bf16[128,768]{1,0:T(8,128)(2,1)S(1)} %collective-permute-done.m1, bf16[128,768]{1,0:T(8,128)(2,1)S(1)} %collective-permute-done.1.m2, ...), custom_call_target="tpu_custom_call" | custom-call | tf_op jit(solution)/shard_map/final/pallas_call | solution.py:326
Async XLA Ops:
  0.6 0.9 %copy-start.4 = (bf16[128,256]{1,0:T(8,128)(2,1)S(1)}, bf16[128,256]{1,0:T(8,128)(2,1)}, u32[]{:S(2)}) copy-start(bf16[128,256]{1,0:T(8,128)(2,1)} %key_ref.1) | copy-start | bytes 196612
  0.6 28.3 %copy-start.2 = (bf16[128,1024]{1,0:T(8,128)(2,1)S(1)}, bf16[128,1024]{1,0:T(8,128)(2,1)}, u32[]{:S(2)}) copy-start(bf16[128,1024]{1,0:T(8,128)(2,1)} %q_ref.1) | copy-start | bytes 786436
  1.5 0.8 %copy-start.5 = (bf16[128,256]{1,0:T(8,128)(2,1)S(1)}, bf16[128,256]{1,0:T(8,128)(2,1)}, u32[]{:S(2)}) copy-start(bf16[128,256]{1,0:T(8,128)(2,1)} %value_ref.1) | copy-start | bytes 196612
  2.4 0.8 %copy-start.6 = (bf16[128,128]{1,0:T(8,128)(2,1)S(1)}, bf16[128,128]{1,0:T(8,128)(2,1)}, u32[]{:S(2)}) copy-start(bf16[128,128]{1,0:T(8,128)(2,1)} %write_ref.1) | copy-start | bytes 98308
  3.1 0.8 %copy-start.7 = (bf16[128,128]{1,0:T(8,128)(2,1)S(1)}, bf16[128,128]{1,0:T(8,128)(2,1)}, u32[]{:S(2)}) copy-start(bf16[128,128]{1,0:T(8,128)(2,1)} %read_ref.1) | copy-start | bytes 98308
  3.9 0.7 copy-start.8
  4.8 24.1 %copy-start.9 = (s32[128]{0:T(128)S(1)}, s32[128]{0:T(128)}, u32[]{:S(2)}) copy-start(s32[128]{0:T(128)} %param.17) | copy-start | bytes 1540
  4.8 18.8 %collective-permute-start.1 = (bf16[128,768]{1,0:T(8,128)(2,1)S(1)}, bf16[128,768]{1,0:T(8,128)(2,1)S(1)}, u32[]{:S(2)}, u32[]{:S(2)}) collective-permute-start(bf16[128,768]{1,0:T(8,128)(2,1)S(1)} %get-tuple-element.17.m0), channel_id=1, source_target_pairs={{0,8},{4,12},{8,16},{12,20},{16,24},{20,28},{1,9},{5,13},{9,17},{1... | collective-permute-start | bytes 589832 | tf_op jit(solution)/shard_map/ppermute | solution.py:21
  8.3 51.6 %copy-start = (bf16[128,2048]{1,0:T(8,128)(2,1)S(1)}, bf16[128,2048]{1,0:T(8,128)(2,1)}, u32[]{:S(2)}) copy-start(bf16[128,2048]{1,0:T(8,128)(2,1)} %x_ref.1) | copy-start | bytes 1572868
  8.3 51.6 %copy-start.1 = (bf16[128,2048]{1,0:T(8,128)(2,1)S(1)}, bf16[128,2048]{1,0:T(8,128)(2,1)}, u32[]{:S(2)}) copy-start(bf16[128,2048]{1,0:T(8,128)(2,1)} %cot_ref.3) | copy-start | bytes 1572868
  8.3 12.9 %collective-permute-start.3 = (bf16[128,256]{1,0:T(8,128)(2,1)S(1)}, bf16[128,256]{1,0:T(8,128)(2,1)S(1)}, u32[]{:S(2)}, u32[]{:S(2)}) collective-permute-start(bf16[128,256]{1,0:T(8,128)(2,1)S(1)} %get-tuple-element.19.n0), channel_id=1, source_target_pairs={{8,0},{12,4},{16,8},{20,12},{24,16},{28,20},{9,1},{13,5},{17,9},{2... | collective-permute-start | bytes 196616 | tf_op jit(solution)/shard_map/ppermute | solution.py:21
  10.8 15.2 %collective-permute-start = (bf16[128,768]{1,0:T(8,128)(2,1)S(1)}, bf16[128,768]{1,0:T(8,128)(2,1)S(1)}, u32[]{:S(2)}, u32[]{:S(2)}) collective-permute-start(bf16[128,768]{1,0:T(8,128)(2,1)S(1)} %get-tuple-element.17.m0), channel_id=1, source_target_pairs={{0,4},{4,8},{8,12},{12,16},{16,20},{20,24},{24,28},{1,5},{5,9},{9,... | collective-permute-start | bytes 589832 | tf_op jit(solution)/shard_map/ppermute | solution.py:21
  14.3 50.1 %collective-permute-start.6 = (bf16[128,2048]{1,0:T(8,128)(2,1)}, bf16[128,2048]{1,0:T(8,128)(2,1)S(1)}, u32[]{:S(2)}, u32[]{:S(2)}) collective-permute-start(bf16[128,2048]{1,0:T(8,128)(2,1)} %x_ref.1), channel_id=1, source_target_pairs={{0,4},{4,8},{8,12},{12,16},{16,20},{20,24},{24,28},{1,5},{5,9},{9,... | collective-permute-start | bytes 1572872 | tf_op jit(solution)/shard_map/ppermute | solution.py:21
  17.7 46.7 %collective-permute-start.7 = (bf16[128,2048]{1,0:T(8,128)(2,1)}, bf16[128,2048]{1,0:T(8,128)(2,1)S(1)}, u32[]{:S(2)}, u32[]{:S(2)}) collective-permute-start(bf16[128,2048]{1,0:T(8,128)(2,1)} %x_ref.1), channel_id=1, source_target_pairs={{0,8},{4,12},{8,16},{12,20},{16,24},{20,28},{1,9},{5,13},{9,17},{1... | collective-permute-start | bytes 1572872 | tf_op jit(solution)/shard_map/ppermute | solution.py:21
  21.2 43.2 %collective-permute-start.8 = (bf16[128,2048]{1,0:T(8,128)(2,1)}, bf16[128,2048]{1,0:T(8,128)(2,1)S(1)}, u32[]{:S(2)}, u32[]{:S(2)}) collective-permute-start(bf16[128,2048]{1,0:T(8,128)(2,1)} %cot_ref.3), channel_id=1, source_target_pairs={{4,0},{8,4},{12,8},{16,12},{20,16},{24,20},{28,24},{5,1},{9,5},{13... | collective-permute-start | bytes 1572872 | tf_op jit(solution)/shard_map/ppermute | solution.py:21
  23.7 40.7 %collective-permute-start.9 = (bf16[128,2048]{1,0:T(8,128)(2,1)}, bf16[128,2048]{1,0:T(8,128)(2,1)S(1)}, u32[]{:S(2)}, u32[]{:S(2)}) collective-permute-start(bf16[128,2048]{1,0:T(8,128)(2,1)} %cot_ref.3), channel_id=1, source_target_pairs={{8,0},{12,4},{16,8},{20,12},{24,16},{28,20},{9,1},{13,5},{17,9},{2... | collective-permute-start | bytes 1572872 | tf_op jit(solution)/shard_map/ppermute | solution.py:21
  26.1 23.1 %collective-permute-start.2 = (bf16[128,256]{1,0:T(8,128)(2,1)S(1)}, bf16[128,256]{1,0:T(8,128)(2,1)S(1)}, u32[]{:S(2)}, u32[]{:S(2)}) collective-permute-start(bf16[128,256]{1,0:T(8,128)(2,1)S(1)} %get-tuple-element.19.n0), channel_id=1, source_target_pairs={{4,0},{8,4},{12,8},{16,12},{20,16},{24,20},{28,24},{5,1},{9,5},{13... | collective-permute-start | bytes 196616 | tf_op jit(solution)/shard_map/ppermute | solution.py:21
  29.0 1.0 %copy-start.3 = (bf16[128,1024]{1,0:T(8,128)(2,1)S(1)}, bf16[128,1024]{1,0:T(8,128)(2,1)}, u32[]{:S(2)}) copy-start(bf16[128,1024]{1,0:T(8,128)(2,1)} %cot_ref.2) | copy-start | bytes 786436
  49.2 8.4 %collective-permute-start.4 = (bf16[128,512]{1,0:T(8,128)(2,1)S(1)}, bf16[128,512]{1,0:T(8,128)(2,1)S(1)}, u32[]{:S(2)}, u32[]{:S(2)}) collective-permute-start(bf16[128,512]{1,0:T(8,128)(2,1)S(1)} %get-tuple-element.21), channel_id=1, source_target_pairs={{4,0},{8,4},{12,8},{16,12},{20,16},{24,20},{28,24},{5,1},{9,5},{13... | collective-permute-start | bytes 393224 | tf_op jit(solution)/shard_map/ppermute | solution.py:21
  57.5 6.8 %collective-permute-start.5 = (bf16[128,512]{1,0:T(8,128)(2,1)S(1)}, bf16[128,512]{1,0:T(8,128)(2,1)S(1)}, u32[]{:S(2)}, u32[]{:S(2)}) collective-permute-start(bf16[128,512]{1,0:T(8,128)(2,1)S(1)} %get-tuple-element.22), channel_id=1, source_target_pairs={{8,0},{12,4},{16,8},{20,12},{24,16},{28,20},{9,1},{13,5},{17,9},{2... | collective-permute-start | bytes 393224 | tf_op jit(solution)/shard_map/ppermute | solution.py:21

commit v2 on v1

v2 whole, which is shorter than its diff:
```python
import functools
import math

import jax
import jax.numpy as jnp
from jax import lax
from jax.experimental import pallas as pl
from jax.experimental.pallas import tpu as pltpu
from jax.sharding import PartitionSpec as P

HEAD_CHANNELS = 128
BF16 = jnp.bfloat16
F32 = jnp.float32
VMEM_LIMIT = 32 * 1024 * 1024
PACK_LIMIT = 60 * 1024 * 1024
NT = (((1,), (1,)), ((), ()))
TN = (((0,), (0,)), ((), ()))


def passed_along(block, axis, distance):
    devices = range(lax.axis_size(axis))
    route = [(i - distance, i) for i in devices if i - distance in devices]
    return lax.ppermute(block, axis, route)


def dot(a, b, dims=(((1,), (0,)), ((), ()))):
    return lax.dot_general(a, b, dims, preferred_element_type=F32)


def iota(shape, dim):
    return lax.broadcasted_iota(jnp.int32, shape, dim)


def split3(v):
    hi = v.astype(BF16)
    rest = v - hi.astype(F32)
    mid = rest.astype(BF16)
    lo = (rest - mid.astype(F32)).astype(BF16)
    return hi, mid, lo


def cumulative(decay_t):
    tokens = decay_t.shape[1]
    tri = iota((tokens, tokens), 0) >= iota((tokens, tokens), 1)
    tri = jnp.where(tri, 1.0, 0.0).astype(BF16)
    return sum(dot(tri, part, NT) for part in split3(decay_t))


def thirds(v):
    return jnp.concatenate([part.astype(F32) for part in split3(v)], axis=1).astype(BF16)


def spread(heads, head_width, low, cols):
    offset = iota((heads, cols), 1) + low - iota((heads, cols), 0) * head_width
    match = jnp.where((offset >= 0) & (offset < head_width), 1.0, 0.0)
    return jnp.concatenate([match] * 3, axis=0).astype(BF16)


def aux_parts(aux, heads):
    wide = aux.astype(F32)
    lam = wide[:, :heads] + wide[:, heads : 2 * heads] + wide[:, 2 * heads : 3 * heads]
    return lam, wide[:, 3 * heads : 4 * heads]


def pack_kernel(key_ref, value_ref, write_ref, decay_ref, doc_ref, m_ref):
    tokens, kv = key_ref.shape
    heads = decay_ref.shape[0]
    state = write_ref.shape[1]
    lam = cumulative(decay_ref[...])
    docs = jnp.broadcast_to(doc_ref[...].astype(F32) + 1.0, (tokens, tokens)).T[:, :heads]
    aux = jnp.concatenate([p.astype(F32) for p in split3(lam)] + [docs], axis=1).astype(BF16)
    m_ref[:, :kv] = key_ref[...]
    m_ref[:, kv : 2 * kv] = value_ref[...]
    m_ref[:, 2 * kv : 2 * kv + state] = write_ref[...]
    m_ref[:, 2 * kv + state :] = aux


def attn_kernel(
    kv,
    docs_at,
    doc_ref,
    read_ref,
    m0,
    m1,
    m2,
    q_ref,
    cot_ref,
    out_ref,
    own_ref,
    back1_ref,
    back2_ref,
):
    tokens = m0.shape[0]
    group = q_ref.shape[1] // HEAD_CHANNELS
    inv_root = 1.0 / math.sqrt(HEAD_CHANNELS)
    width = HEAD_CHANNELS
    tiles = (m2, m1, m0)
    key_cols = pl.ds(pl.multiple_of(pl.program_id(0) * width, width), width)
    value_cols = pl.ds(pl.multiple_of(kv + pl.program_id(0) * width, width), width)
    keys = jnp.concatenate([tile[:, key_cols] for tile in tiles], axis=0)
    values = jnp.concatenate([tile[:, value_cols] for tile in tiles], axis=0)
    span = keys.shape[0]
    doc_s = jnp.concatenate(
        [tile[:, docs_at : docs_at + 1].astype(F32) for tile in tiles], axis=0
    )
    doc_t = doc_ref[...].astype(F32) + 1.0
    inside = (doc_s == doc_t) & (
        iota((span, tokens), 0) - (span - tokens) <= iota((span, tokens), 1)
    )
    inside = jnp.where(inside, 1.0, 0.0)
    inside = jnp.concatenate([inside] * group, axis=1) > 0.5
    query = jnp.concatenate(
        [q_ref[:, i * width : (i + 1) * width] for i in range(group)], axis=0
    )
    cot = jnp.concatenate(
        [cot_ref[:, i * width : (i + 1) * width] for i in range(group)], axis=0
    )
    score = jnp.where(inside, dot(keys, query, NT) * inv_root, -1e30)
    raised = jnp.exp(score - jnp.max(score, axis=0, keepdims=True))
    raised = jnp.where(inside, raised, 0.0)
    prob = (raised * (1.0 / jnp.sum(raised, axis=0, keepdims=True))).astype(BF16)
    out = dot(values, prob, TN).T
    for i in range(group):
        out_ref[:, i * width : (i + 1) * width] = out[i * tokens : (i + 1) * tokens].astype(BF16)
    prob_grad = dot(values, cot, NT)
    prob32 = prob.astype(F32)
    inner = jnp.sum(prob32 * prob_grad, axis=0, keepdims=True)
    score_grad = (prob32 * (prob_grad - inner) * inv_root).astype(BF16)
    key_grad = dot(score_grad, query)
    value_grad = dot(prob, cot)
    low = pl.multiple_of(pl.program_id(0) * 2 * width, 2 * width)
    key_at = pl.ds(low, width)
    value_at = pl.ds(pl.multiple_of(low + width, width), width)
    back2_ref[:, key_at] = key_grad[:tokens].astype(BF16)
    back2_ref[:, value_at] = value_grad[:tokens].astype(BF16)
    back1_ref[:, key_at] = key_grad[tokens : 2 * tokens].astype(BF16)
    back1_ref[:, value_at] = value_grad[tokens : 2 * tokens].astype(BF16)
    own_ref[:, key_at] = key_grad[2 * tokens :]
    own_ref[:, value_at] = value_grad[2 * tokens :]

    @pl.when(pl.program_id(0) == 0)
    def _():
        state = read_ref.shape[1]
        aux = m0[:, 2 * kv + state :]
        for back_ref in (back1_ref, back2_ref):
            back_ref[:, 2 * kv : 2 * kv + state] = read_ref[...]
            back_ref[:, 2 * kv + state :] = aux


def local_kernel(
    head_width, doc_ref, write_ref, read_ref, decay_ref, x_ref, cot_ref, mixed_ref, grad_ref
):
    tokens, cols = x_ref.shape
    step_heads = cols // head_width
    lam = cumulative(decay_ref[...])
    upper = iota((tokens, tokens), 0) <= iota((tokens, tokens), 1)
    upper = jnp.where(upper, 1.0, 0.0).astype(BF16)
    lam_t = sum(dot(part, upper) for part in split3(decay_ref[...]))
    doc_row = doc_ref[...].astype(F32)
    doc_col = jnp.broadcast_to(doc_row, (tokens, tokens)).T
    inside = (iota((tokens, tokens), 0) >= iota((tokens, tokens), 1)) & (doc_col == doc_row)
    score = dot(read_ref[...], write_ref[...], NT)
    per = HEAD_CHANNELS // head_width
    lane_head = iota((tokens, HEAD_CHANNELS), 1) // head_width
    for pair in range(step_heads // per):
        at = slice(pair * HEAD_CHANNELS, (pair + 1) * HEAD_CHANNELS)
        x = x_ref[:, at]
        cot = cot_ref[:, at]
        mixed = grad = None
        for j in range(per):
            head = pair * per + j
            gap = lam[:, head : head + 1] - lam_t[head : head + 1, :]
            weights = (jnp.exp(jnp.where(inside, gap, -jnp.inf)) * score).astype(BF16)
            mixed_j = dot(weights, x)
            grad_j = dot(weights, cot, TN)
            mixed = mixed_j if j == 0 else jnp.where(lane_head == j, mixed_j, mixed)
            grad = grad_j if j == 0 else jnp.where(lane_head == j, grad_j, grad)
        mixed_ref[:, at] = mixed
        grad_ref[:, at] = grad


def same(a, b):
    return jnp.where(a == b, 1.0, 0.0)


def carried_kernel(
    head_width,
    decay_ref,
    doc_ref,
    read_ref,
    write1_ref,
    aux1_ref,
    write2_ref,
    aux2_ref,
    x1_ref,
    x2_ref,
    mixed_ref,
    out_ref,
):
    tokens, cols = x1_ref.shape
    heads = decay_ref.shape[0]
    lam = cumulative(decay_ref[...])
    docs = jnp.broadcast_to(doc_ref[...].astype(F32) + 1.0, (tokens, tokens)).T[:, :heads]
    lam1, doc1 = aux_parts(aux1_ref[...], heads)
    lam2, doc2 = aux_parts(aux2_ref[...], heads)

    def last(v):
        return v[tokens - 1 :]

    entry = thirds(jnp.exp(lam) * same(docs, last(doc1)))
    gain = jnp.exp(last(lam1)) * same(last(doc1), last(doc2))
    exit1 = thirds(jnp.exp(last(lam1) - lam1) * same(doc1, last(doc1)))
    exit2 = thirds(jnp.exp(last(lam2) - lam2) * same(doc2, last(doc2)) * gain)
    score1 = dot(read_ref[...], write1_ref[...], NT).astype(BF16)
    score2 = dot(read_ref[...], write2_ref[...], NT).astype(BF16)
    step = min(cols, 512)
    for low in range(0, cols, step):
        at = slice(low, low + step)
        to_cols = spread(heads, head_width, low, step)
        x1 = (x1_ref[:, at].astype(F32) * dot(exit1, to_cols)).astype(BF16)
        x2 = (x2_ref[:, at].astype(F32) * dot(exit2, to_cols)).astype(BF16)
        carried = (dot(score1, x1) + dot(score2, x2)) * dot(entry, to_cols)
        out_ref[:, at] = (mixed_ref[:, at] + carried).astype(BF16)


def returned_kernel(
    head_width,
    decay_ref,
    doc_ref,
    write_ref,
    r1_ref,
    r2_ref,
    own_ref,
    c1_ref,
    c2_ref,
    grad_ref,
    out_ref,
    grad_key_ref,
    grad_value_ref,
):
    tokens, cols = c1_ref.shape
    heads = decay_ref.shape[0]
    state = write_ref.shape[1]
    width = HEAD_CHANNELS
    kv2 = own_ref.shape[1]
    total = own_ref[...] + r1_ref[:, :kv2].astype(F32) + r2_ref[:, :kv2].astype(F32)
    for g in range(kv2 // (2 * width)):
        at = slice(g * width, (g + 1) * width)
        low = 2 * g * width
        grad_key_ref[:, at] = total[:, low : low + width].astype(BF16)
        grad_value_ref[:, at] = total[:, low + width : low + 2 * width].astype(BF16)

    def last(v):
        return v[tokens - 1 :]

    lam = cumulative(decay_ref[...])
    docs = jnp.broadcast_to(doc_ref[...].astype(F32) + 1.0, (tokens, tokens)).T[:, :heads]
    lam1, doc1 = aux_parts(r1_ref[:, kv2 + state :], heads)
    lam2, doc2 = aux_parts(r2_ref[:, kv2 + state :], heads)
    exit_w = thirds(jnp.exp(last(lam) - lam) * same(docs, last(docs)))
    gain = jnp.exp(last(lam1)) * same(last(doc1), last(docs))
    entry1 = thirds(jnp.exp(lam1) * same(doc1, last(docs)))
    entry2 = thirds(jnp.exp(lam2) * same(doc2, last(doc1)) * gain)
    score1 = dot(write_ref[...], r1_ref[:, kv2 : kv2 + state], NT).astype(BF16)
    score2 = dot(write_ref[...], r2_ref[:, kv2 : kv2 + state], NT).astype(BF16)
    step = min(cols, 512)
    for low in range(0, cols, step):
        at = slice(low, low + step)
        to_cols = spread(heads, head_width, low, step)
        c1 = (c1_ref[:, at].astype(F32) * dot(entry1, to_cols)).astype(BF16)
        c2 = (c2_ref[:, at].astype(F32) * dot(entry2, to_cols)).astype(BF16)
        returned = (dot(score1, c1) + dot(score2, c2)) * dot(exit_w, to_cols)
        out_ref[:, at] = (grad_ref[:, at] + returned).astype(BF16)


def whole(shape):
    return pl.BlockSpec(shape, lambda i: (0, 0))


def columns(rows, cols):
    return pl.BlockSpec((rows, cols), lambda i: (0, i))


def part(rows, width, low):
    return pl.BlockSpec((rows, width), lambda i: (0, low // width))


def shards(
    query_head_matrix,
    key_head_matrix,
    value_head_matrix,
    ssm_input,
    log_decay,
    state_write,
    state_read,
    document_ids,
    attention_output_gradient,
    cot_mixer,
):
    tokens, kv = key_head_matrix.shape
    kv_local = kv // HEAD_CHANNELS
    heads = log_decay.shape[1]
    state = state_write.shape[1]
    cols = ssm_input.shape[1]
    head_width = cols // heads
    group_cols = query_head_matrix.shape[1] // kv_local
    doc_row = document_ids.reshape(1, tokens)
    decay_t = log_decay.T
    aux = 4 * heads
    m_cols = 2 * kv + state + aux
    step_cols = min(512, cols)
    steps = cols // step_cols
    shape = jax.ShapeDtypeStruct
    params = pltpu.CompilerParams(vmem_limit_bytes=VMEM_LIMIT)

    x1 = passed_along(ssm_input, "ctx", 1)
    c2 = passed_along(cot_mixer, "ctx", -2)
    m0 = pl.pallas_call(
        pack_kernel,
        out_shape=shape((tokens, m_cols), BF16),
        compiler_params=pltpu.CompilerParams(vmem_limit_bytes=PACK_LIMIT),
        name="pack",
    )(key_head_matrix, value_head_matrix, state_write, decay_t, doc_row)
    m1 = passed_along(m0, "ctx", 1)
    m2 = passed_along(m0, "ctx", 2)
    c1 = passed_along(cot_mixer, "ctx", -1)
    decay_local, m1, m2 = lax.optimization_barrier((decay_t, m1, m2))
    mixed, grad = pl.pallas_call(
        functools.partial(local_kernel, head_width),
        grid=(steps,),
        in_specs=[
            whole((1, tokens)),
            whole((tokens, state)),
            whole((tokens, state)),
            pl.BlockSpec((heads // steps, tokens), lambda i: (i, 0)),
            columns(tokens, step_cols),
            columns(tokens, step_cols),
        ],
        out_specs=[columns(tokens, step_cols)] * 2,
        out_shape=(shape(ssm_input.shape, F32),) * 2,
        compiler_params=params,
        name="local_mixer",
    )(doc_row, state_write, state_read, decay_local, ssm_input, cot_mixer)

    mixed, grad, x0 = lax.optimization_barrier((mixed, grad, ssm_input))
    x2 = passed_along(x0, "ctx", 2)
    attention_out, own, back1, back2 = pl.pallas_call(
        functools.partial(attn_kernel, kv, 2 * kv + state + 3 * heads),
        grid=(kv_local,),
        in_specs=[whole((1, tokens)), whole((tokens, state))]
        + [whole((tokens, m_cols))] * 3
        + [columns(tokens, group_cols)] * 2,
        out_specs=[columns(tokens, group_cols), whole((tokens, 2 * kv))]
        + [whole((tokens, m_cols))] * 2,
        out_shape=(
            shape(query_head_matrix.shape, BF16),
            shape((tokens, 2 * kv), F32),
            shape((tokens, m_cols), BF16),
            shape((tokens, m_cols), BF16),
        ),
        compiler_params=params,
        name="attention",
    )(doc_row, state_read, m0, m1, m2, query_head_matrix, attention_output_gradient)
    r1 = passed_along(back1, "ctx", -1)
    back2, c1 = lax.optimization_barrier((back2, c1))
    r2 = passed_along(back2, "ctx", -2)


    write_at = 2 * kv
    mixer_out = pl.pallas_call(
        functools.partial(carried_kernel, head_width),
        grid=(1,),
        in_specs=[
            whole((heads, tokens)),
            whole((1, tokens)),
            whole((tokens, state)),
            part(tokens, state, write_at),
            part(tokens, aux, write_at + state),
            part(tokens, state, write_at),
            part(tokens, aux, write_at + state),
            whole((tokens, cols)),
            whole((tokens, cols)),
            whole((tokens, cols)),
        ],
        out_specs=whole((tokens, cols)),
        out_shape=shape(ssm_input.shape, BF16),
        compiler_params=params,
        name="carried",
    )(decay_t, doc_row, state_read, m1, m1, m2, m2, x1, x2, mixed)

    own, mixer_out = lax.optimization_barrier((own, mixer_out))
    grad_input, grad_key, grad_value = pl.pallas_call(
        functools.partial(returned_kernel, head_width),
        grid=(1,),
        in_specs=[
            whole((heads, tokens)),
            whole((1, tokens)),
            whole((tokens, state)),
            whole((tokens, m_cols)),
            whole((tokens, m_cols)),
            whole((tokens, 2 * kv)),
            whole((tokens, cols)),
            whole((tokens, cols)),
            whole((tokens, cols)),
        ],
        out_specs=[whole((tokens, cols))] + [whole((tokens, kv))] * 2,
        out_shape=(
            shape(cot_mixer.shape, BF16),
            shape(key_head_matrix.shape, BF16),
            shape(value_head_matrix.shape, BF16),
        ),
        compiler_params=params,
        name="returned",
    )(decay_t, doc_row, state_write, r1, r2, own, c1, c2, grad)
    return (attention_out, mixer_out, grad_key, grad_value, grad_input)


def solution(mesh):
    return jax.shard_map(
        shards,
        mesh=mesh,
        in_specs=(
            P("ctx", "tp"),
            P("ctx", "tp"),
            P("ctx", "tp"),
            P("ctx", "tp"),
            P("ctx", "tp"),
            P("ctx", None),
            P("ctx", None),
            P("ctx"),
            P("ctx", "tp"),
            P("ctx", "tp"),
        ),
        out_specs=(P("ctx", "tp"), P("ctx", "tp"), P("ctx", "tp"), P("ctx", "tp"), P("ctx", "tp")),
        check_vma=False,
    )
```

time: 71.4 us -> 50.4 us (0.71)
  the two profiles are of different devices: /device:TPU:14 before, /device:TPU:0 now
where the time goes in v2:
time: 50.4 us; the launch traced here: 50 us
  starting transfers between devices  21.7 us (43%)
  Pallas kernels  14.3 us (28%)
  waiting for transfers between devices  13.2 us (26%)
  between operations  0.82 us (2%)
    ppermute x8, starting transfers between devices, passed_along(): return lax.ppermute(block, axis, route)  21.7 us
    ppermute x8, waiting for transfers between devices, passed_along(): return lax.ppermute(block, axis, route)  13.2 us
    pallas_call x1, Pallas kernels, shards(): pl.pallas_call(functools.partial(local_kernel, head_width), grid=(steps,)...  4.23 us
    pallas_call x1, Pallas kernels, shards(): pl.pallas_call(functools.partial(attn_kernel, kv, 2 * kv + state + 3 * he...  3.28 us
    pallas_call x1, Pallas kernels, shards(): pl.pallas_call(functools.partial(returned_kernel, head_width), grid=(1,),...  2.54 us
    pallas_call x1, Pallas kernels, shards(): pl.pallas_call(functools.partial(carried_kernel, head_width), grid=(1,),...  2.38 us
    pallas_call x1, Pallas kernels, shards(): pl.pallas_call(pack_kernel, out_shape=shape((tokens, m_cols), BF16), comp...  1.85 us
  transfers between devices with their start and end apart: 8, of which 2 were waited for; matrix products, arithmetic and copies ran while one was open for 0% of the time, Pallas kernels for 20%

profile of v2, /device:TPU:0, one launch (start us, length us, event | category | flops | bytes accessed | tf_op | source)
XLA Modules:
  0.0 50.0 jit_solution(3638077637170041317)
XLA Ops:
  0.6 0.0 copy-start.1
  0.6 0.0 copy-start.2
  0.7 0.0 copy-start.3
  0.7 0.0 copy-start.6
  0.7 1.8 %pack.1.m0 = bf16[128,768]{1,0:T(8,128)(2,1)} custom-call(bf16[128,256]{1,0:T(8,128)(2,1)} %key_ref.1, bf16[128,256]{1,0:T(8,128)(2,1)} %value_ref.1, bf16[128,128]{1,0:T(8,128)(2,1)} %write_ref.5, f32[32,128]{1,0:T(8,128)} %bitcast.2, s32[1,128]{1,0:T(1,128)} %bitcast.6), custom_call_target="tpu_custom_call" | custom-call | tf_op jit(solution)/shard_map/pack/pallas_call | solution.py:318
  2.5 0.0 copy-start
  2.5 0.0 copy-start.4
  2.5 0.0 copy-start.5
  2.5 5.0 %collective-permute-start = (bf16[128,768]{1,0:T(8,128)(2,1)}, bf16[128,768]{1,0:T(8,128)(2,1)S(1)}, u32[]{:S(2)}, u32[]{:S(2)}) collective-permute-start(bf16[128,768]{1,0:T(8,128)(2,1)} %pack.1.m0), channel_id=1, source_target_pairs={{0,4},{4,8},{8,12},{12,16},{16,20},{20,24},{24,28},{1,5},{5,9},{9,... | collective-permute-start | bytes 589832 | tf_op jit(solution)/shard_map/ppermute | solution.py:23
  7.5 3.5 %collective-permute-start.1 = (bf16[128,768]{1,0:T(8,128)(2,1)}, bf16[128,768]{1,0:T(8,128)(2,1)S(1)}, u32[]{:S(2)}, u32[]{:S(2)}) collective-permute-start(bf16[128,768]{1,0:T(8,128)(2,1)} %pack.1.m0), channel_id=1, source_target_pairs={{0,8},{4,12},{8,16},{12,20},{16,24},{20,28},{1,9},{5,13},{9,17},{1... | collective-permute-start | bytes 589832 | tf_op jit(solution)/shard_map/ppermute | solution.py:23
  11.0 1.3 %collective-permute-start.5 = (bf16[128,2048]{1,0:T(8,128)(2,1)}, bf16[128,2048]{1,0:T(8,128)(2,1)S(1)}, u32[]{:S(2)}, u32[]{:S(2)}) collective-permute-start(bf16[128,2048]{1,0:T(8,128)(2,1)} %cot_ref.3), channel_id=1, source_target_pairs={{4,0},{8,4},{12,8},{16,12},{20,16},{24,20},{28,24},{5,1},{9,5},{13... | collective-permute-start | bytes 1572872 | tf_op jit(solution)/shard_map/ppermute | solution.py:23
  12.3 4.6 %collective-permute-start.2 = (bf16[128,2048]{1,0:T(8,128)(2,1)}, bf16[128,2048]{1,0:T(8,128)(2,1)S(1)}, u32[]{:S(2)}, u32[]{:S(2)}) collective-permute-start(bf16[128,2048]{1,0:T(8,128)(2,1)} %x_ref.1), channel_id=1, source_target_pairs={{0,4},{4,8},{8,12},{12,16},{16,20},{20,24},{24,28},{1,5},{5,9},{9,... | collective-permute-start | bytes 1572872 | tf_op jit(solution)/shard_map/ppermute | solution.py:23
  16.9 0.0 collective-permute-done.m1.write1_ref.aux1_ref
  16.9 0.0 collective-permute-done.1.m2.write2_ref.aux2_ref
  16.9 0.0 copy-done.1
  16.9 0.0 copy-done.2
  16.9 0.0 copy-done.3
  16.9 0.0 copy-done.6
  17.0 4.2 %local_mixer.1 = (f32[128,2048]{1,0:T(8,128)S(1)}, f32[128,2048]{1,0:T(8,128)S(1)}) custom-call(s32[1,128]{1,0:T(1,128)S(1)} %bitcast.7, bf16[128,128]{1,0:T(8,128)(2,1)S(1)} %copy-done.2, bf16[128,128]{1,0:T(8,128)(2,1)S(1)} %copy-done.1, f32[32,128]{1,0:T(8,128)S(1)} %bitcast.3, bf16[128,2048]{1,0:T(8,128)(2,1)} %x_ref.1, bf16[128,2048]{1,0:T(8,128)(2,1)} %cot_ref.3), custom_call_target="tpu_custom_call" | custom-call | tf_op jit(solution)/shard_map/local_mixer/pallas_call | solution.py:328
  21.2 3.5 %collective-permute-start.3 = (bf16[128,2048]{1,0:T(8,128)(2,1)}, bf16[128,2048]{1,0:T(8,128)(2,1)S(1)}, u32[]{:S(2)}, u32[]{:S(2)}) collective-permute-start(bf16[128,2048]{1,0:T(8,128)(2,1)} %x_ref.1), channel_id=1, source_target_pairs={{0,8},{4,12},{8,16},{12,20},{16,24},{20,28},{1,9},{5,13},{9,17},{1... | collective-permute-start | bytes 1572872 | tf_op jit(solution)/shard_map/ppermute | solution.py:23
  24.7 1.3 %collective-permute-start.7 = (bf16[128,2048]{1,0:T(8,128)(2,1)}, bf16[128,2048]{1,0:T(8,128)(2,1)S(1)}, u32[]{:S(2)}, u32[]{:S(2)}) collective-permute-start(bf16[128,2048]{1,0:T(8,128)(2,1)} %cot_ref.3), channel_id=1, source_target_pairs={{8,0},{12,4},{16,8},{20,12},{24,16},{28,20},{9,1},{13,5},{17,9},{2... | collective-permute-start | bytes 1572872 | tf_op jit(solution)/shard_map/ppermute | solution.py:23
  26.0 0.0 copy-done
  26.0 0.0 copy-done.4
  26.0 0.0 copy-done.5
  26.0 3.3 %attention.1 = (bf16[128,1024]{1,0:T(8,128)(2,1)}, f32[128,512]{1,0:T(8,128)S(1)}, bf16[128,768]{1,0:T(8,128)(2,1)S(1)}, bf16[128,768]{1,0:T(8,128)(2,1)S(1)}) custom-call(s32[1,128]{1,0:T(1,128)S(1)} %bitcast.8, bf16[128,128]{1,0:T(8,128)(2,1)S(1)} %copy-done.1, bf16[128,768]{1,0:T(8,128)(2,1)S(1)} %copy-done, ...), custom_call_target="tpu_custom_call" | custom-call | tf_op jit(solution)/shard_map/attention/pallas_call | solution.py:347
  29.3 1.3 %collective-permute-start.4 = (bf16[128,768]{1,0:T(8,128)(2,1)S(1)}, bf16[128,768]{1,0:T(8,128)(2,1)S(1)}, u32[]{:S(2)}, u32[]{:S(2)}) collective-permute-start(bf16[128,768]{1,0:T(8,128)(2,1)S(1)} %get-tuple-element.34), channel_id=1, source_target_pairs={{4,0},{8,4},{12,8},{16,12},{20,16},{24,20},{28,24},{5,1},{9,5},{13... | collective-permute-start | bytes 589832 | tf_op jit(solution)/shard_map/ppermute | solution.py:23
  30.6 0.0 collective-permute-done.5.c1_ref
  30.6 1.3 %collective-permute-start.6 = (bf16[128,768]{1,0:T(8,128)(2,1)S(1)}, bf16[128,768]{1,0:T(8,128)(2,1)S(1)}, u32[]{:S(2)}, u32[]{:S(2)}) collective-permute-start(bf16[128,768]{1,0:T(8,128)(2,1)S(1)} %get-tuple-element.36), channel_id=1, source_target_pairs={{8,0},{12,4},{16,8},{20,12},{24,16},{28,20},{9,1},{13,5},{17,9},{2... | collective-permute-start | bytes 589832 | tf_op jit(solution)/shard_map/ppermute | solution.py:23
  31.9 7.5 %collective-permute-done.2.x1_ref = bf16[128,2048]{1,0:T(8,128)(2,1)S(1)} collective-permute-done((bf16[128,2048]{1,0:T(8,128)(2,1)}, bf16[128,2048]{1,0:T(8,128)(2,1)S(1)}, u32[]{:S(2)}, u32[]{:S(2)}) %collective-permute-start.2) | collective-permute-done | bytes 524320 | tf_op jit(solution)/shard_map/ppermute | solution.py:23
  39.4 0.0 collective-permute-done.3.x2_ref
  39.4 2.4 %carried.1 = bf16[128,2048]{1,0:T(8,128)(2,1)} custom-call(f32[32,128]{1,0:T(8,128)S(1)} %bitcast.4, s32[1,128]{1,0:T(1,128)S(1)} %bitcast.9, bf16[128,128]{1,0:T(8,128)(2,1)S(1)} %copy-done.1, bf16[128,768]{1,0:T(8,128)(2,1)S(1)} %collective-permute-done.m1.write1_ref.aux1_ref, bf16[128,768]{1,0:T(8,128)(2,1)S(1)} %collective-permute-done.m1.write1_ref.aux1_ref, ...), custom_call_target="tpu_custom_call" | custom-call | tf_op jit(solution)/shard_map/carried/pallas_call | solution.py:370
  41.7 0.0 collective-permute-done.4.r1_ref
  41.7 0.0 collective-permute-done.7.c2_ref
  41.7 5.7 %collective-permute-done.6.r2_ref = bf16[128,768]{1,0:T(8,128)(2,1)S(1)} collective-permute-done((bf16[128,768]{1,0:T(8,128)(2,1)S(1)}, bf16[128,768]{1,0:T(8,128)(2,1)S(1)}, u32[]{:S(2)}, u32[]{:S(2)}) %collective-permute-start.6) | collective-permute-done | bytes 196640 | tf_op jit(solution)/shard_map/ppermute | solution.py:23
  47.5 2.5 %returned.1 = (bf16[128,2048]{1,0:T(8,128)(2,1)}, bf16[128,256]{1,0:T(8,128)(2,1)}, bf16[128,256]{1,0:T(8,128)(2,1)}) custom-call(f32[32,128]{1,0:T(8,128)S(1)} %bitcast.5, s32[1,128]{1,0:T(1,128)S(1)} %bitcast.10, bf16[128,128]{1,0:T(8,128)(2,1)S(1)} %copy-done.2, bf16[128,768]{1,0:T(8,128)(2,1)S(1)} %collective-permute-done.4.r1_ref, ...), custom_call_target="tpu_custom_call" | custom-call | tf_op jit(solution)/shard_map/returned/pallas_call | solution.py:392
Async XLA Ops:
  0.6 16.3 %copy-start.1 = (bf16[128,128]{1,0:T(8,128)(2,1)S(1)}, bf16[128,128]{1,0:T(8,128)(2,1)}, u32[]{:S(2)}) copy-start(bf16[128,128]{1,0:T(8,128)(2,1)} %read_ref.5) | copy-start | bytes 98308
  0.6 16.3 %copy-start.2 = (bf16[128,128]{1,0:T(8,128)(2,1)S(1)}, bf16[128,128]{1,0:T(8,128)(2,1)}, u32[]{:S(2)}) copy-start(bf16[128,128]{1,0:T(8,128)(2,1)} %write_ref.5) | copy-start | bytes 98308
  0.7 16.3 %copy-start.3 = (f32[128,32]{0,1:T(8,128)S(1)}, f32[128,32]{0,1:T(8,128)}, u32[]{:S(2)}) copy-start(f32[128,32]{0,1:T(8,128)} %param.14) | copy-start | bytes 49156
  0.7 16.3 %copy-start.6 = (s32[128]{0:T(128)S(1)}, s32[128]{0:T(128)}, u32[]{:S(2)}) copy-start(s32[128]{0:T(128)} %param.17) | copy-start | bytes 1540
  2.5 23.5 %copy-start = (bf16[128,768]{1,0:T(8,128)(2,1)S(1)}, bf16[128,768]{1,0:T(8,128)(2,1)}, u32[]{:S(2)}) copy-start(bf16[128,768]{1,0:T(8,128)(2,1)} %pack.1.m0) | copy-start | bytes 589828
  2.5 23.5 %copy-start.4 = (bf16[128,1024]{1,0:T(8,128)(2,1)S(1)}, bf16[128,1024]{1,0:T(8,128)(2,1)}, u32[]{:S(2)}) copy-start(bf16[128,1024]{1,0:T(8,128)(2,1)} %q_ref.1) | copy-start | bytes 786436
  2.5 23.5 %copy-start.5 = (bf16[128,1024]{1,0:T(8,128)(2,1)S(1)}, bf16[128,1024]{1,0:T(8,128)(2,1)}, u32[]{:S(2)}) copy-start(bf16[128,1024]{1,0:T(8,128)(2,1)} %cot_ref.2) | copy-start | bytes 786436
  2.5 14.4 %collective-permute-start = (bf16[128,768]{1,0:T(8,128)(2,1)}, bf16[128,768]{1,0:T(8,128)(2,1)S(1)}, u32[]{:S(2)}, u32[]{:S(2)}) collective-permute-start(bf16[128,768]{1,0:T(8,128)(2,1)} %pack.1.m0), channel_id=1, source_target_pairs={{0,4},{4,8},{8,12},{12,16},{16,20},{20,24},{24,28},{1,5},{5,9},{9,... | collective-permute-start | bytes 589832 | tf_op jit(solution)/shard_map/ppermute | solution.py:23
  7.5 9.4 %collective-permute-start.1 = (bf16[128,768]{1,0:T(8,128)(2,1)}, bf16[128,768]{1,0:T(8,128)(2,1)S(1)}, u32[]{:S(2)}, u32[]{:S(2)}) collective-permute-start(bf16[128,768]{1,0:T(8,128)(2,1)} %pack.1.m0), channel_id=1, source_target_pairs={{0,8},{4,12},{8,16},{12,20},{16,24},{20,28},{1,9},{5,13},{9,17},{1... | collective-permute-start | bytes 589832 | tf_op jit(solution)/shard_map/ppermute | solution.py:23
  11.0 19.6 %collective-permute-start.5 = (bf16[128,2048]{1,0:T(8,128)(2,1)}, bf16[128,2048]{1,0:T(8,128)(2,1)S(1)}, u32[]{:S(2)}, u32[]{:S(2)}) collective-permute-start(bf16[128,2048]{1,0:T(8,128)(2,1)} %cot_ref.3), channel_id=1, source_target_pairs={{4,0},{8,4},{12,8},{16,12},{20,16},{24,20},{28,24},{5,1},{9,5},{13... | collective-permute-start | bytes 1572872 | tf_op jit(solution)/shard_map/ppermute | solution.py:23
  12.3 27.0 %collective-permute-start.2 = (bf16[128,2048]{1,0:T(8,128)(2,1)}, bf16[128,2048]{1,0:T(8,128)(2,1)S(1)}, u32[]{:S(2)}, u32[]{:S(2)}) collective-permute-start(bf16[128,2048]{1,0:T(8,128)(2,1)} %x_ref.1), channel_id=1, source_target_pairs={{0,4},{4,8},{8,12},{12,16},{16,20},{20,24},{24,28},{1,5},{5,9},{9,... | collective-permute-start | bytes 1572872 | tf_op jit(solution)/shard_map/ppermute | solution.py:23
  21.2 18.2 %collective-permute-start.3 = (bf16[128,2048]{1,0:T(8,128)(2,1)}, bf16[128,2048]{1,0:T(8,128)(2,1)S(1)}, u32[]{:S(2)}, u32[]{:S(2)}) collective-permute-start(bf16[128,2048]{1,0:T(8,128)(2,1)} %x_ref.1), channel_id=1, source_target_pairs={{0,8},{4,12},{8,16},{12,20},{16,24},{20,28},{1,9},{5,13},{9,17},{1... | collective-permute-start | bytes 1572872 | tf_op jit(solution)/shard_map/ppermute | solution.py:23
  24.7 17.1 %collective-permute-start.7 = (bf16[128,2048]{1,0:T(8,128)(2,1)}, bf16[128,2048]{1,0:T(8,128)(2,1)S(1)}, u32[]{:S(2)}, u32[]{:S(2)}) collective-permute-start(bf16[128,2048]{1,0:T(8,128)(2,1)} %cot_ref.3), channel_id=1, source_target_pairs={{8,0},{12,4},{16,8},{20,12},{24,16},{28,20},{9,1},{13,5},{17,9},{2... | collective-permute-start | bytes 1572872 | tf_op jit(solution)/shard_map/ppermute | solution.py:23
  29.3 12.4 %collective-permute-start.4 = (bf16[128,768]{1,0:T(8,128)(2,1)S(1)}, bf16[128,768]{1,0:T(8,128)(2,1)S(1)}, u32[]{:S(2)}, u32[]{:S(2)}) collective-permute-start(bf16[128,768]{1,0:T(8,128)(2,1)S(1)} %get-tuple-element.34), channel_id=1, source_target_pairs={{4,0},{8,4},{12,8},{16,12},{20,16},{24,20},{28,24},{5,1},{9,5},{13... | collective-permute-start | bytes 589832 | tf_op jit(solution)/shard_map/ppermute | solution.py:23
  30.6 16.9 %collective-permute-start.6 = (bf16[128,768]{1,0:T(8,128)(2,1)S(1)}, bf16[128,768]{1,0:T(8,128)(2,1)S(1)}, u32[]{:S(2)}, u32[]{:S(2)}) collective-permute-start(bf16[128,768]{1,0:T(8,128)(2,1)S(1)} %get-tuple-element.36), channel_id=1, source_target_pairs={{8,0},{12,4},{16,8},{20,12},{24,16},{28,20},{9,1},{13,5},{17,9},{2... | collective-permute-start | bytes 589832 | tf_op jit(solution)/shard_map/ppermute | solution.py:23

commit v3 on v2

--- a/solution.py
+++ b/solution.py
@@ -23,6 +23,14 @@
     return lax.ppermute(block, axis, route)
 
 
+def exchanged(block, axis, first):
+    count = lax.axis_size(axis)
+    route = []
+    for i in range(first, count - 1, 2):
+        route += [(i, i + 1), (i + 1, i)]
+    return lax.ppermute(block, axis, route)
+
+
 def dot(a, b, dims=(((1,), (0,)), ((), ()))):
     return lax.dot_general(a, b, dims, preferred_element_type=F32)
 
@@ -62,7 +70,9 @@
     return lam, wide[:, 3 * heads : 4 * heads]
 
 
-def pack_kernel(key_ref, value_ref, write_ref, decay_ref, doc_ref, m_ref):
+def pack_kernel(
+    key_ref, value_ref, write_ref, read_ref, decay_ref, doc_ref, m_ref, n_ref
+):
     tokens, kv = key_ref.shape
     heads = decay_ref.shape[0]
     state = write_ref.shape[1]
@@ -73,6 +83,8 @@
     m_ref[:, kv : 2 * kv] = value_ref[...]
     m_ref[:, 2 * kv : 2 * kv + state] = write_ref[...]
     m_ref[:, 2 * kv + state :] = aux
+    n_ref[:, :state] = read_ref[...]
+    n_ref[:, state:] = jnp.zeros((tokens, n_ref.shape[1] - state), BF16)
 
 
 def attn_kernel(
@@ -85,6 +97,7 @@
     m2,
     q_ref,
     cot_ref,
+    far_ref,
     out_ref,
     own_ref,
     back1_ref,
@@ -141,10 +154,9 @@
     @pl.when(pl.program_id(0) == 0)
     def _():
         state = read_ref.shape[1]
-        aux = m0[:, 2 * kv + state :]
-        for back_ref in (back1_ref, back2_ref):
-            back_ref[:, 2 * kv : 2 * kv + state] = read_ref[...]
-            back_ref[:, 2 * kv + state :] = aux
+        back1_ref[:, 2 * kv : 2 * kv + state] = read_ref[...]
+        back1_ref[:, 2 * kv + state :] = m0[:, 2 * kv + state :]
+        back2_ref[:, 2 * kv :] = far_ref[...]
 
 
 def local_kernel(
@@ -183,6 +195,69 @@
     return jnp.where(a == b, 1.0, 0.0)
 
 
+def last(v):
+    return v[v.shape[0] - 1 :]
+
+
+def tail_is_long(docs):
+    count = jnp.sum(same(docs[:, :1], last(docs)[:, :1]), axis=0, keepdims=True)
+    return count > docs.shape[0] // 2
+
+
+def choose(flag, a, b):
+    return jnp.where(jnp.broadcast_to(jnp.where(flag, 1.0, 0.0), a.shape) > 0.5, a, b)
+
+
+def own_numbers(decay_ref, doc_ref):
+    heads, tokens = decay_ref.shape
+    docs = jnp.broadcast_to(doc_ref[...].astype(F32) + 1.0, (tokens, tokens)).T
+    return cumulative(decay_ref[...]), docs[:, :heads]
+
+
+def far_kernel(
+    head_width,
+    decay_ref,
+    doc_ref,
+    read_ref,
+    write_ref,
+    read2_ref,
+    aux1_ref,
+    write2_ref,
+    aux2_ref,
+    x_ref,
+    cot_ref,
+    ahead_ref,
+    behind_ref,
+):
+    tokens, cols = x_ref.shape
+    heads = decay_ref.shape[0]
+    half = tokens // 2
+    lam, docs = own_numbers(decay_ref, doc_ref)
+    lam1, doc1 = aux_parts(aux1_ref[...], heads)
+    _, doc2 = aux_parts(aux2_ref[...], heads)
+    gain = jnp.exp(last(lam1)) * same(last(doc1), last(doc2))
+    exit_w = thirds(jnp.exp(last(lam) - lam) * same(docs, last(docs)))
+    entry = thirds(jnp.exp(lam) * same(docs, last(doc1)) * gain)
+    ahead_score = dot(read2_ref[:half], write_ref[...], NT).astype(BF16)
+    behind_score = dot(write2_ref[half:], read_ref[...], NT).astype(BF16)
+    ahead_sums = tail_is_long(docs)
+    behind_rows = tail_is_long(doc2)
+    step = min(cols // 2, 512)
+    for low in range(0, cols, step):
+        at = slice(low, low + step)
+        to_cols = spread(heads, head_width, low, step)
+        x = (x_ref[:, at].astype(F32) * dot(exit_w, to_cols)).astype(BF16)
+        sums = dot(ahead_score, x)
+        ahead_ref[:, at] = choose(ahead_sums, sums, x[half:].astype(F32)).astype(BF16)
+        cot = (cot_ref[:, at].astype(F32) * dot(entry, to_cols)).astype(BF16)
+        sums = dot(behind_score, cot)
+        row = low // (cols // 2) * half
+        col = low % (cols // 2)
+        behind_ref[row : row + half, col : col + step] = choose(
+            behind_rows, cot[:half].astype(F32), sums
+        ).astype(BF16)
+
+
 def carried_kernel(
     head_width,
     decay_ref,
@@ -192,34 +267,36 @@
     aux1_ref,
     write2_ref,
     aux2_ref,
-    x1_ref,
+    odd_ref,
+    first_ref,
+    then_ref,
     x2_ref,
     mixed_ref,
     out_ref,
 ):
-    tokens, cols = x1_ref.shape
+    tokens, cols = first_ref.shape
+    odd = odd_ref[0, 0] == 1
     heads = decay_ref.shape[0]
-    lam = cumulative(decay_ref[...])
-    docs = jnp.broadcast_to(doc_ref[...].astype(F32) + 1.0, (tokens, tokens)).T[:, :heads]
+    half = tokens // 2
+    lam, docs = own_numbers(decay_ref, doc_ref)
     lam1, doc1 = aux_parts(aux1_ref[...], heads)
-    lam2, doc2 = aux_parts(aux2_ref[...], heads)
-
-    def last(v):
-        return v[tokens - 1 :]
-
+    _, doc2 = aux_parts(aux2_ref[...], heads)
     entry = thirds(jnp.exp(lam) * same(docs, last(doc1)))
     gain = jnp.exp(last(lam1)) * same(last(doc1), last(doc2))
+    gain = thirds(jnp.broadcast_to(gain, (16, heads)))
     exit1 = thirds(jnp.exp(last(lam1) - lam1) * same(doc1, last(doc1)))
-    exit2 = thirds(jnp.exp(last(lam2) - lam2) * same(doc2, last(doc2)) * gain)
     score1 = dot(read_ref[...], write1_ref[...], NT).astype(BF16)
-    score2 = dot(read_ref[...], write2_ref[...], NT).astype(BF16)
+    take = jnp.where(iota((tokens, half), 0) == iota((tokens, half), 1), 1.0, 0.0)
+    score2 = dot(read_ref[...], write2_ref[half:], NT)
+    score2 = choose(tail_is_long(doc2), take, score2).astype(BF16)
     step = min(cols, 512)
     for low in range(0, cols, step):
         at = slice(low, low + step)
         to_cols = spread(heads, head_width, low, step)
-        x1 = (x1_ref[:, at].astype(F32) * dot(exit1, to_cols)).astype(BF16)
-        x2 = (x2_ref[:, at].astype(F32) * dot(exit2, to_cols)).astype(BF16)
-        carried = (dot(score1, x1) + dot(score2, x2)) * dot(entry, to_cols)
+        x1 = jnp.where(odd, first_ref[:, at], then_ref[:, at])
+        x1 = (x1.astype(F32) * dot(exit1, to_cols)).astype(BF16)
+        carried = dot(score2, x2_ref[:, at]) * dot(gain, to_cols)[:1]
+        carried = (carried + dot(score1, x1)) * dot(entry, to_cols)
         out_ref[:, at] = (mixed_ref[:, at] + carried).astype(BF16)
 
 
@@ -228,19 +305,23 @@
     decay_ref,
     doc_ref,
     write_ref,
+    read2_ref,
     r1_ref,
     r2_ref,
     own_ref,
-    c1_ref,
-    c2_ref,
+    odd_ref,
+    first_ref,
+    then_ref,
     grad_ref,
     out_ref,
     grad_key_ref,
     grad_value_ref,
 ):
-    tokens, cols = c1_ref.shape
+    tokens, cols = first_ref.shape
+    odd = odd_ref[0, 0] == 1
     heads = decay_ref.shape[0]
     state = write_ref.shape[1]
+    half = tokens // 2
     width = HEAD_CHANNELS
     kv2 = own_ref.shape[1]
     total = own_ref[...] + r1_ref[:, :kv2].astype(F32) + r2_ref[:, :kv2].astype(F32)
@@ -249,27 +330,24 @@
         low = 2 * g * width
         grad_key_ref[:, at] = total[:, low : low + width].astype(BF16)
         grad_value_ref[:, at] = total[:, low + width : low + 2 * width].astype(BF16)
-
-    def last(v):
-        return v[tokens - 1 :]
-
-    lam = cumulative(decay_ref[...])
-    docs = jnp.broadcast_to(doc_ref[...].astype(F32) + 1.0, (tokens, tokens)).T[:, :heads]
+    lam, docs = own_numbers(decay_ref, doc_ref)
     lam1, doc1 = aux_parts(r1_ref[:, kv2 + state :], heads)
-    lam2, doc2 = aux_parts(r2_ref[:, kv2 + state :], heads)
     exit_w = thirds(jnp.exp(last(lam) - lam) * same(docs, last(docs)))
-    gain = jnp.exp(last(lam1)) * same(last(doc1), last(docs))
     entry1 = thirds(jnp.exp(lam1) * same(doc1, last(docs)))
-    entry2 = thirds(jnp.exp(lam2) * same(doc2, last(doc1)) * gain)
     score1 = dot(write_ref[...], r1_ref[:, kv2 : kv2 + state], NT).astype(BF16)
-    score2 = dot(write_ref[...], r2_ref[:, kv2 : kv2 + state], NT).astype(BF16)
-    step = min(cols, 512)
+    take = jnp.where(iota((tokens, half), 0) == iota((tokens, half), 1) + half, 1.0, 0.0)
+    score2 = dot(write_ref[...], read2_ref[:half], NT)
+    score2 = choose(tail_is_long(docs), score2, take).astype(BF16)
+    step = min(cols // 2, 512)
     for low in range(0, cols, step):
         at = slice(low, low + step)
         to_cols = spread(heads, head_width, low, step)
-        c1 = (c1_ref[:, at].astype(F32) * dot(entry1, to_cols)).astype(BF16)
-        c2 = (c2_ref[:, at].astype(F32) * dot(entry2, to_cols)).astype(BF16)
-        returned = (dot(score1, c1) + dot(score2, c2)) * dot(exit_w, to_cols)
+        c1 = jnp.where(odd, then_ref[:, at], first_ref[:, at])
+        c1 = (c1.astype(F32) * dot(entry1, to_cols)).astype(BF16)
+        row = low // (cols // 2) * half
+        col = kv2 + low % (cols // 2)
+        far = r2_ref[row : row + half, col : col + step]
+        returned = (dot(score1, c1) + dot(score2, far)) * dot(exit_w, to_cols)
         out_ref[:, at] = (grad_ref[:, at] + returned).astype(BF16)
 
 
@@ -313,18 +391,22 @@
     shape = jax.ShapeDtypeStruct
     params = pltpu.CompilerParams(vmem_limit_bytes=VMEM_LIMIT)
 
-    x1 = passed_along(ssm_input, "ctx", 1)
-    c2 = passed_along(cot_mixer, "ctx", -2)
-    m0 = pl.pallas_call(
+    odd = lax.axis_index("ctx") % 2
+    first_sent = jnp.where(odd == 0, ssm_input, cot_mixer)
+    then_sent = jnp.where(odd == 0, cot_mixer, ssm_input)
+    odd = odd.reshape(1, 1)
+    first = exchanged(first_sent, "ctx", 0)
+    m0, n0 = pl.pallas_call(
         pack_kernel,
-        out_shape=shape((tokens, m_cols), BF16),
+        out_shape=(shape((tokens, m_cols), BF16),) * 2,
         compiler_params=pltpu.CompilerParams(vmem_limit_bytes=PACK_LIMIT),
         name="pack",
-    )(key_head_matrix, value_head_matrix, state_write, decay_t, doc_row)
+    )(key_head_matrix, value_head_matrix, state_write, state_read, decay_t, doc_row)
     m1 = passed_along(m0, "ctx", 1)
     m2 = passed_along(m0, "ctx", 2)
-    c1 = passed_along(cot_mixer, "ctx", -1)
-    decay_local, m1, m2 = lax.optimization_barrier((decay_t, m1, m2))
+    read2 = passed_along(n0, "ctx", -2)
+    then = exchanged(then_sent, "ctx", 1)
+    decay_local, m1, m2, read2 = lax.optimization_barrier((decay_t, m1, m2, read2))
     mixed, grad = pl.pallas_call(
         functools.partial(local_kernel, head_width),
         grid=(steps,),
@@ -342,31 +424,57 @@
         name="local_mixer",
     )(doc_row, state_write, state_read, decay_local, ssm_input, cot_mixer)
 
-    mixed, grad, x0 = lax.optimization_barrier((mixed, grad, ssm_input))
-    x2 = passed_along(x0, "ctx", 2)
+    write_at = 2 * kv
+    ahead, behind = pl.pallas_call(
+        functools.partial(far_kernel, head_width),
+        grid=(1,),
+        in_specs=[
+            whole((heads, tokens)),
+            whole((1, tokens)),
+            whole((tokens, state)),
+            whole((tokens, state)),
+            part(tokens, state, 0),
+            part(tokens, aux, write_at + state),
+            part(tokens, state, write_at),
+            part(tokens, aux, write_at + state),
+            whole((tokens, cols)),
+            whole((tokens, cols)),
+        ],
+        out_specs=[whole((tokens // 2, cols)), whole((tokens, cols // 2))],
+        out_shape=(
+            shape((tokens // 2, cols), BF16),
+            shape((tokens, cols // 2), BF16),
+        ),
+        compiler_params=params,
+        name="far",
+    )(decay_t, doc_row, state_read, state_write, read2, m1, m2, m2, ssm_input, cot_mixer)
+    x2 = passed_along(ahead, "ctx", 2)
     attention_out, own, back1, back2 = pl.pallas_call(
         functools.partial(attn_kernel, kv, 2 * kv + state + 3 * heads),
         grid=(kv_local,),
         in_specs=[whole((1, tokens)), whole((tokens, state))]
         + [whole((tokens, m_cols))] * 3
-        + [columns(tokens, group_cols)] * 2,
-        out_specs=[columns(tokens, group_cols), whole((tokens, 2 * kv))]
-        + [whole((tokens, m_cols))] * 2,
+        + [columns(tokens, group_cols)] * 2
+        + [whole((tokens, cols // 2))],
+        out_specs=[
+            columns(tokens, group_cols),
+            whole((tokens, 2 * kv)),
+            whole((tokens, m_cols)),
+            whole((tokens, 2 * kv + cols // 2)),
+        ],
         out_shape=(
             shape(query_head_matrix.shape, BF16),
             shape((tokens, 2 * kv), F32),
             shape((tokens, m_cols), BF16),
-            shape((tokens, m_cols), BF16),
+            shape((tokens, 2 * kv + cols // 2), BF16),
         ),
         compiler_params=params,
         name="attention",
-    )(doc_row, state_read, m0, m1, m2, query_head_matrix, attention_output_gradient)
+    )(doc_row, state_read, m0, m1, m2, query_head_matrix, attention_output_gradient, behind)
     r1 = passed_along(back1, "ctx", -1)
-    back2, c1 = lax.optimization_barrier((back2, c1))
     r2 = passed_along(back2, "ctx", -2)
 
 
-    write_at = 2 * kv
     mixer_out = pl.pallas_call(
         functools.partial(carried_kernel, head_width),
         grid=(1,),
@@ -378,15 +486,17 @@
             part(tokens, aux, write_at + state),
             part(tokens, state, write_at),
             part(tokens, aux, write_at + state),
-            whole((tokens, cols)),
-            whole((tokens, cols)),
+            pl.BlockSpec(memory_space=pltpu.SMEM),
+            whole((tokens, cols)),
+            whole((tokens, cols)),
+            whole((tokens // 2, cols)),
             whole((tokens, cols)),
         ],
         out_specs=whole((tokens, cols)),
         out_shape=shape(ssm_input.shape, BF16),
         compiler_params=params,
         name="carried",
-    )(decay_t, doc_row, state_read, m1, m1, m2, m2, x1, x2, mixed)
+    )(decay_t, doc_row, state_read, m1, m1, m2, m2, odd, first, then, x2, mixed)
 
     own, mixer_out = lax.optimization_barrier((own, mixer_out))
     grad_input, grad_key, grad_value = pl.pallas_call(
@@ -396,9 +506,11 @@
             whole((heads, tokens)),
             whole((1, tokens)),
             whole((tokens, state)),
+            part(tokens, state, 0),
             whole((tokens, m_cols)),
-            whole((tokens, m_cols)),
+            whole((tokens, 2 * kv + cols // 2)),
             whole((tokens, 2 * kv)),
+            pl.BlockSpec(memory_space=pltpu.SMEM),
             whole((tokens, cols)),
             whole((tokens, cols)),
             whole((tokens, cols)),
@@ -411,7 +523,7 @@
         ),
         compiler_params=params,
         name="returned",
-    )(decay_t, doc_row, state_write, r1, r2, own, c1, c2, grad)
+    )(decay_t, doc_row, state_write, read2, r1, r2, own, odd, first, then, grad)
     return (attention_out, mixer_out, grad_key, grad_value, grad_input)
 
 

time: 50.4 us -> 44.5 us (0.88)
  the two profiles are of different devices: /device:TPU:0 before, /device:TPU:14 now
where the time goes in v3:
time: 44.5 us; the launch traced here: 44.2 us
  starting transfers between devices  22.2 us (50%)
  Pallas kernels  14.4 us (32%)
  waiting for transfers between devices  5.32 us (12%)
  other arithmetic  1.35 us (3%)
  between operations  0.87 us (2%)
    ppermute x6, starting transfers between devices, passed_along(): return lax.ppermute(block, axis, route)  17 us
    ppermute x2, starting transfers between devices, exchanged(): return lax.ppermute(block, axis, route)  5.12 us
    ppermute x2, waiting for transfers between devices, exchanged(): return lax.ppermute(block, axis, route)  4.28 us
    pallas_call x1, Pallas kernels, shards(): pl.pallas_call(functools.partial(attn_kernel, kv, 2 * kv + state + 3 * he...  3.29 us
    pallas_call x1, Pallas kernels, shards(): pl.pallas_call(functools.partial(local_kernel, head_width), grid=(steps,)...  3.12 us
    pallas_call x1, Pallas kernels, shards(): pl.pallas_call(functools.partial(returned_kernel, head_width), grid=(1,),...  2.25 us
    pallas_call x1, Pallas kernels, shards(): pl.pallas_call(functools.partial(carried_kernel, head_width), grid=(1,),...  2.15 us
    pallas_call x1, Pallas kernels, shards(): pl.pallas_call(pack_kernel, out_shape=(shape((tokens, m_cols), BF16),) *...  1.83 us
  transfers between devices with their start and end apart: 8, of which 3 were waited for; matrix products, arithmetic and copies ran while one was open for 3% of the time, Pallas kernels for 23%

profile of v3, /device:TPU:14, one launch (start us, length us, event | category | flops | bytes accessed | tf_op | source)
XLA Modules:
  0.0 44.2 jit_solution(15349311162462082367)
XLA Ops:
  0.6 1.8 %pack.1 = (bf16[128,768]{1,0:T(8,128)(2,1)}, bf16[128,768]{1,0:T(8,128)(2,1)}) custom-call(bf16[128,256]{1,0:T(8,128)(2,1)} %key_ref.1, bf16[128,256]{1,0:T(8,128)(2,1)} %value_ref.1, bf16[128,128]{1,0:T(8,128)(2,1)} %write_ref.7, bf16[128,128]{1,0:T(8,128)(2,1)} %read_ref.9, f32[32,128]{1,0:T(8,128)} %bitcast.3, s32[1,128]{1,0:T(1,128)} %bitcast.8), custom_call_target="tpu_custom_call" | custom-call | tf_op jit(solution)/shard_map/pack/pallas_call | solution.py:399
  2.5 3.4 %collective-permute-start = (bf16[128,768]{1,0:T(8,128)(2,1)}, bf16[128,768]{1,0:T(8,128)(2,1)S(1)}, u32[]{:S(2)}, u32[]{:S(2)}) collective-permute-start(bf16[128,768]{1,0:T(8,128)(2,1)} %get-tuple-element.24.m0), channel_id=1, source_target_pairs={{0,4},{4,8},{8,12},{12,16},{16,20},{20,24},{24,28},{1,5},{5,9},{9,... | collective-permute-start | bytes 589832 | tf_op jit(solution)/shard_map/ppermute | solution.py:23
  5.9 3.5 %collective-permute-start.1 = (bf16[128,768]{1,0:T(8,128)(2,1)}, bf16[128,768]{1,0:T(8,128)(2,1)S(1)}, u32[]{:S(2)}, u32[]{:S(2)}) collective-permute-start(bf16[128,768]{1,0:T(8,128)(2,1)} %get-tuple-element.24.m0), channel_id=1, source_target_pairs={{0,8},{4,12},{8,16},{12,20},{16,24},{20,28},{1,9},{5,13},{9,17},{1... | collective-permute-start | bytes 589832 | tf_op jit(solution)/shard_map/ppermute | solution.py:23
  9.4 2.4 %collective-permute-start.2 = (bf16[128,768]{1,0:T(8,128)(2,1)}, bf16[128,768]{1,0:T(8,128)(2,1)S(1)}, u32[]{:S(2)}, u32[]{:S(2)}) collective-permute-start(bf16[128,768]{1,0:T(8,128)(2,1)} %get-tuple-element.25), channel_id=1, source_target_pairs={{8,0},{12,4},{16,8},{20,12},{24,16},{28,20},{9,1},{13,5},{17,9},{2... | collective-permute-start | bytes 589832 | tf_op jit(solution)/shard_map/ppermute | solution.py:23
  11.8 0.0 copy-start
  11.8 0.0 copy-start.1
  11.8 0.0 copy-start.2
  11.8 0.0 copy-start.3
  11.8 0.0 copy-start.4
  11.9 1.4 %broadcast_select_fusion = (bf16[128,2048]{1,0:T(8,128)(2,1)S(1)}, bf16[128,2048]{1,0:T(8,128)(2,1)S(1)}) fusion(bf16[128,2048]{1,0:T(8,128)(2,1)} %cot_ref.5, bf16[128,2048]{1,0:T(8,128)(2,1)} %x_ref.3, pred[]{:T(512)S(6)} %eq.6), kind=kLoop, calls=%fused_computation | loop fusion | flops 524288 | bytes 2097153 | tf_op jit(solution)/shard_map/jit(_where)/select_n | solution.py:396
  13.2 0.0 copy-start.8
  13.2 0.5 %collective-permute-start.3 = (bf16[128,2048]{1,0:T(8,128)(2,1)S(1)}, bf16[128,2048]{1,0:T(8,128)(2,1)S(1)}, u32[]{:S(2)}, u32[]{:S(2)}) collective-permute-start(bf16[128,2048]{1,0:T(8,128)(2,1)S(1)} %get-tuple-element.44), channel_id=1, source_target_pairs={{0,4},{4,0},{8,12},{12,8},{16,20},{20,16},{24,28},{28,24},{1,5},{5... | collective-permute-start | bytes 1572872 | tf_op jit(solution)/shard_map/ppermute | solution.py:31
  13.8 0.0 copy-start.5
  13.8 0.0 copy-start.6
  13.8 0.0 copy-start.7
  13.8 4.6 %collective-permute-start.4 = (bf16[128,2048]{1,0:T(8,128)(2,1)S(1)}, bf16[128,2048]{1,0:T(8,128)(2,1)S(1)}, u32[]{:S(2)}, u32[]{:S(2)}) collective-permute-start(bf16[128,2048]{1,0:T(8,128)(2,1)S(1)} %get-tuple-element.43), channel_id=1, source_target_pairs={{4,8},{8,4},{12,16},{16,12},{20,24},{24,20},{5,9},{9,5},{13,17},{1... | collective-permute-start | bytes 1572872 | tf_op jit(solution)/shard_map/ppermute | solution.py:31
  18.4 0.0 collective-permute-done.aux1_ref.m1.write1_ref
  18.4 0.0 collective-permute-done.1.write2_ref.aux2_ref.m2
  18.4 0.0 collective-permute-done.2.read2_ref
  18.4 0.0 copy-done
  18.4 0.0 copy-done.1
  18.4 0.0 copy-done.2
  18.4 0.0 copy-done.3
  18.4 0.0 copy-done.4
  18.4 0.0 copy-done.8
  18.5 1.8 %far.1 = (bf16[64,2048]{1,0:T(8,128)(2,1)S(1)}, bf16[128,1024]{1,0:T(8,128)(2,1)S(1)}) custom-call(f32[32,128]{1,0:T(8,128)S(1)} %bitcast.4, s32[1,128]{1,0:T(1,128)S(1)} %bitcast.9, bf16[128,128]{1,0:T(8,128)(2,1)S(1)} %copy-done.2, bf16[128,128]{1,0:T(8,128)(2,1)S(1)} %copy-done.3, bf16[128,768]{1,0:T(8,128)(2,1)S(1)} %collective-permute-done.2.read2_ref, ...), custom_call_target="tpu_custom_call" | custom-call | tf_op jit(solution)/shard_map/far/pallas_call | solution.py:428
  20.2 0.0 copy-done.5
  20.2 0.0 copy-done.6
  20.2 0.0 copy-done.7
  20.3 3.3 %attention.1 = (bf16[128,1024]{1,0:T(8,128)(2,1)}, f32[128,512]{1,0:T(8,128)S(1)}, bf16[128,768]{1,0:T(8,128)(2,1)S(1)}, bf16[128,1536]{1,0:T(8,128)(2,1)S(1)}) custom-call(s32[1,128]{1,0:T(1,128)S(1)} %bitcast.10, bf16[128,128]{1,0:T(8,128)(2,1)S(1)} %copy-done.2, bf16[128,768]{1,0:T(8,128)(2,1)S(1)} %copy-done.7, ...), custom_call_target="tpu_custom_call" | custom-call | tf_op jit(solution)/shard_map/attention/pallas_call | solution.py:452
  23.6 2.4 %collective-permute-start.7 = (bf16[128,1536]{1,0:T(8,128)(2,1)S(1)}, bf16[128,1536]{1,0:T(8,128)(2,1)S(1)}, u32[]{:S(2)}, u32[]{:S(2)}) collective-permute-start(bf16[128,1536]{1,0:T(8,128)(2,1)S(1)} %get-tuple-element.37), channel_id=1, source_target_pairs={{8,0},{12,4},{16,8},{20,12},{24,16},{28,20},{9,1},{13,5},{17,9},{2... | collective-permute-start | bytes 1179656 | tf_op jit(solution)/shard_map/ppermute | solution.py:23
  25.9 3.5 %collective-permute-start.5 = (bf16[64,2048]{1,0:T(8,128)(2,1)S(1)}, bf16[64,2048]{1,0:T(8,128)(2,1)S(1)}, u32[]{:S(2)}, u32[]{:S(2)}) collective-permute-start(bf16[64,2048]{1,0:T(8,128)(2,1)S(1)} %get-tuple-element.32), channel_id=1, source_target_pairs={{0,8},{4,12},{8,16},{12,20},{16,24},{20,28},{1,9},{5,13},{9,17},{1... | collective-permute-start | bytes 786440 | tf_op jit(solution)/shard_map/ppermute | solution.py:23
  29.4 1.9 %collective-permute-start.6 = (bf16[128,768]{1,0:T(8,128)(2,1)S(1)}, bf16[128,768]{1,0:T(8,128)(2,1)S(1)}, u32[]{:S(2)}, u32[]{:S(2)}) collective-permute-start(bf16[128,768]{1,0:T(8,128)(2,1)S(1)} %get-tuple-element.36), channel_id=1, source_target_pairs={{4,0},{8,4},{12,8},{16,12},{20,16},{24,20},{28,24},{5,1},{9,5},{13... | collective-permute-start | bytes 589832 | tf_op jit(solution)/shard_map/ppermute | solution.py:23
  31.3 3.1 %local_mixer.1 = (f32[128,2048]{1,0:T(8,128)S(1)}, f32[128,2048]{1,0:T(8,128)S(1)}) custom-call(s32[1,128]{1,0:T(1,128)S(1)} %bitcast.11, bf16[128,128]{1,0:T(8,128)(2,1)S(1)} %copy-done.3, bf16[128,128]{1,0:T(8,128)(2,1)S(1)} %copy-done.2, f32[32,128]{1,0:T(8,128)S(1)} %bitcast.5, bf16[128,2048]{1,0:T(8,128)(2,1)S(1)} %copy-done, ...), custom_call_target="tpu_custom_call" | custom-call | tf_op jit(solution)/shard_map/local_mixer/pallas_call | solution.py:410
  34.5 0.5 %collective-permute-done.5.x2_ref = bf16[64,2048]{1,0:T(8,128)(2,1)S(1)} collective-permute-done((bf16[64,2048]{1,0:T(8,128)(2,1)S(1)}, bf16[64,2048]{1,0:T(8,128)(2,1)S(1)}, u32[]{:S(2)}, u32[]{:S(2)}) %collective-permute-start.5) | collective-permute-done | bytes 262176 | tf_op jit(solution)/shard_map/ppermute | solution.py:23
  35.0 4.3 %collective-permute-done.3.first_ref = bf16[128,2048]{1,0:T(8,128)(2,1)S(1)} collective-permute-done((bf16[128,2048]{1,0:T(8,128)(2,1)S(1)}, bf16[128,2048]{1,0:T(8,128)(2,1)S(1)}, u32[]{:S(2)}, u32[]{:S(2)}) %collective-permute-start.3) | collective-permute-done | bytes 524320 | tf_op jit(solution)/shard_map/ppermute | solution.py:31
  39.3 0.0 collective-permute-done.4.then_ref
  39.3 2.2 %carried.1 = bf16[128,2048]{1,0:T(8,128)(2,1)} custom-call(f32[32,128]{1,0:T(8,128)S(1)} %bitcast.6, s32[1,128]{1,0:T(1,128)S(1)} %bitcast.12, bf16[128,128]{1,0:T(8,128)(2,1)S(1)} %copy-done.2, bf16[128,768]{1,0:T(8,128)(2,1)S(1)} %collective-permute-done.aux1_ref.m1.write1_ref, bf16[128,768]{1,0:T(8,128)(2,1)S(1)} %collective-permute-done.aux1_ref.m1.write1_ref, ...), custom_call_target="tpu_custom_call" | custom-call | tf_op jit(solution)/shard_map/carried/pallas_call | solution.py:478
  41.4 0.5 %collective-permute-done.6.r1_ref = bf16[128,768]{1,0:T(8,128)(2,1)S(1)} collective-permute-done((bf16[128,768]{1,0:T(8,128)(2,1)S(1)}, bf16[128,768]{1,0:T(8,128)(2,1)S(1)}, u32[]{:S(2)}, u32[]{:S(2)}) %collective-permute-start.6) | collective-permute-done | bytes 196640 | tf_op jit(solution)/shard_map/ppermute | solution.py:23
  41.9 0.0 collective-permute-done.7.r2_ref
  41.9 2.2 %returned.1 = (bf16[128,2048]{1,0:T(8,128)(2,1)}, bf16[128,256]{1,0:T(8,128)(2,1)}, bf16[128,256]{1,0:T(8,128)(2,1)}) custom-call(f32[32,128]{1,0:T(8,128)S(1)} %bitcast.7, s32[1,128]{1,0:T(1,128)S(1)} %bitcast.13, bf16[128,128]{1,0:T(8,128)(2,1)S(1)} %copy-done.3, bf16[128,768]{1,0:T(8,128)(2,1)S(1)} %collective-permute-done.2.read2_ref, ...), custom_call_target="tpu_custom_call" | custom-call | tf_op jit(solution)/shard_map/returned/pallas_call | solution.py:502
Async XLA Ops:
  2.5 15.9 %collective-permute-start = (bf16[128,768]{1,0:T(8,128)(2,1)}, bf16[128,768]{1,0:T(8,128)(2,1)S(1)}, u32[]{:S(2)}, u32[]{:S(2)}) collective-permute-start(bf16[128,768]{1,0:T(8,128)(2,1)} %get-tuple-element.24.m0), channel_id=1, source_target_pairs={{0,4},{4,8},{8,12},{12,16},{16,20},{20,24},{24,28},{1,5},{5,9},{9,... | collective-permute-start | bytes 589832 | tf_op jit(solution)/shard_map/ppermute | solution.py:23
  5.9 12.5 %collective-permute-start.1 = (bf16[128,768]{1,0:T(8,128)(2,1)}, bf16[128,768]{1,0:T(8,128)(2,1)S(1)}, u32[]{:S(2)}, u32[]{:S(2)}) collective-permute-start(bf16[128,768]{1,0:T(8,128)(2,1)} %get-tuple-element.24.m0), channel_id=1, source_target_pairs={{0,8},{4,12},{8,16},{12,20},{16,24},{20,28},{1,9},{5,13},{9,17},{1... | collective-permute-start | bytes 589832 | tf_op jit(solution)/shard_map/ppermute | solution.py:23
  9.4 9.0 %collective-permute-start.2 = (bf16[128,768]{1,0:T(8,128)(2,1)}, bf16[128,768]{1,0:T(8,128)(2,1)S(1)}, u32[]{:S(2)}, u32[]{:S(2)}) collective-permute-start(bf16[128,768]{1,0:T(8,128)(2,1)} %get-tuple-element.25), channel_id=1, source_target_pairs={{8,0},{12,4},{16,8},{20,12},{24,16},{28,20},{9,1},{13,5},{17,9},{2... | collective-permute-start | bytes 589832 | tf_op jit(solution)/shard_map/ppermute | solution.py:23
  11.8 6.6 %copy-start = (bf16[128,2048]{1,0:T(8,128)(2,1)S(1)}, bf16[128,2048]{1,0:T(8,128)(2,1)}, u32[]{:S(2)}) copy-start(bf16[128,2048]{1,0:T(8,128)(2,1)} %x_ref.3) | copy-start | bytes 1572868
  11.8 6.6 %copy-start.1 = (bf16[128,2048]{1,0:T(8,128)(2,1)S(1)}, bf16[128,2048]{1,0:T(8,128)(2,1)}, u32[]{:S(2)}) copy-start(bf16[128,2048]{1,0:T(8,128)(2,1)} %cot_ref.5) | copy-start | bytes 1572868
  11.8 6.6 %copy-start.2 = (bf16[128,128]{1,0:T(8,128)(2,1)S(1)}, bf16[128,128]{1,0:T(8,128)(2,1)}, u32[]{:S(2)}) copy-start(bf16[128,128]{1,0:T(8,128)(2,1)} %read_ref.9) | copy-start | bytes 98308
  11.8 6.6 %copy-start.3 = (bf16[128,128]{1,0:T(8,128)(2,1)S(1)}, bf16[128,128]{1,0:T(8,128)(2,1)}, u32[]{:S(2)}) copy-start(bf16[128,128]{1,0:T(8,128)(2,1)} %write_ref.7) | copy-start | bytes 98308
  11.8 6.6 %copy-start.4 = (f32[128,32]{0,1:T(8,128)S(1)}, f32[128,32]{0,1:T(8,128)}, u32[]{:S(2)}) copy-start(f32[128,32]{0,1:T(8,128)} %param.14) | copy-start | bytes 49156
  13.2 5.2 %copy-start.8 = (s32[128]{0:T(128)S(1)}, s32[128]{0:T(128)}, u32[]{:S(2)}) copy-start(s32[128]{0:T(128)} %param.17) | copy-start | bytes 1540
  13.2 26.0 %collective-permute-start.3 = (bf16[128,2048]{1,0:T(8,128)(2,1)S(1)}, bf16[128,2048]{1,0:T(8,128)(2,1)S(1)}, u32[]{:S(2)}, u32[]{:S(2)}) collective-permute-start(bf16[128,2048]{1,0:T(8,128)(2,1)S(1)} %get-tuple-element.44), channel_id=1, source_target_pairs={{0,4},{4,0},{8,12},{12,8},{16,20},{20,16},{24,28},{28,24},{1,5},{5... | collective-permute-start | bytes 1572872 | tf_op jit(solution)/shard_map/ppermute | solution.py:31
  13.8 6.5 %copy-start.5 = (bf16[128,1024]{1,0:T(8,128)(2,1)S(1)}, bf16[128,1024]{1,0:T(8,128)(2,1)}, u32[]{:S(2)}) copy-start(bf16[128,1024]{1,0:T(8,128)(2,1)} %q_ref.1) | copy-start | bytes 786436
  13.8 6.5 %copy-start.6 = (bf16[128,1024]{1,0:T(8,128)(2,1)S(1)}, bf16[128,1024]{1,0:T(8,128)(2,1)}, u32[]{:S(2)}) copy-start(bf16[128,1024]{1,0:T(8,128)(2,1)} %cot_ref.4) | copy-start | bytes 786436
  13.8 6.5 %copy-start.7 = (bf16[128,768]{1,0:T(8,128)(2,1)S(1)}, bf16[128,768]{1,0:T(8,128)(2,1)}, u32[]{:S(2)}) copy-start(bf16[128,768]{1,0:T(8,128)(2,1)} %get-tuple-element.24.m0) | copy-start | bytes 589828
  13.8 25.5 %collective-permute-start.4 = (bf16[128,2048]{1,0:T(8,128)(2,1)S(1)}, bf16[128,2048]{1,0:T(8,128)(2,1)S(1)}, u32[]{:S(2)}, u32[]{:S(2)}) collective-permute-start(bf16[128,2048]{1,0:T(8,128)(2,1)S(1)} %get-tuple-element.43), channel_id=1, source_target_pairs={{4,8},{8,4},{12,16},{16,12},{20,24},{24,20},{5,9},{9,5},{13,17},{1... | collective-permute-start | bytes 1572872 | tf_op jit(solution)/shard_map/ppermute | solution.py:31
  23.6 18.4 %collective-permute-start.7 = (bf16[128,1536]{1,0:T(8,128)(2,1)S(1)}, bf16[128,1536]{1,0:T(8,128)(2,1)S(1)}, u32[]{:S(2)}, u32[]{:S(2)}) collective-permute-start(bf16[128,1536]{1,0:T(8,128)(2,1)S(1)} %get-tuple-element.37), channel_id=1, source_target_pairs={{8,0},{12,4},{16,8},{20,12},{24,16},{28,20},{9,1},{13,5},{17,9},{2... | collective-permute-start | bytes 1179656 | tf_op jit(solution)/shard_map/ppermute | solution.py:23
  25.9 9.1 %collective-permute-start.5 = (bf16[64,2048]{1,0:T(8,128)(2,1)S(1)}, bf16[64,2048]{1,0:T(8,128)(2,1)S(1)}, u32[]{:S(2)}, u32[]{:S(2)}) collective-permute-start(bf16[64,2048]{1,0:T(8,128)(2,1)S(1)} %get-tuple-element.32), channel_id=1, source_target_pairs={{0,8},{4,12},{8,16},{12,20},{16,24},{20,28},{1,9},{5,13},{9,17},{1... | collective-permute-start | bytes 786440 | tf_op jit(solution)/shard_map/ppermute | solution.py:23
  29.4 12.5 %collective-permute-start.6 = (bf16[128,768]{1,0:T(8,128)(2,1)S(1)}, bf16[128,768]{1,0:T(8,128)(2,1)S(1)}, u32[]{:S(2)}, u32[]{:S(2)}) collective-permute-start(bf16[128,768]{1,0:T(8,128)(2,1)S(1)} %get-tuple-element.36), channel_id=1, source_target_pairs={{4,0},{8,4},{12,8},{16,12},{20,16},{24,20},{28,24},{5,1},{9,5},{13... | collective-permute-start | bytes 589832 | tf_op jit(solution)/shard_map/ppermute | solution.py:23

commit v4 on v3

--- a/solution.py
+++ b/solution.py
@@ -11,7 +11,7 @@
 HEAD_CHANNELS = 128
 BF16 = jnp.bfloat16
 F32 = jnp.float32
-VMEM_LIMIT = 32 * 1024 * 1024
+VMEM_LIMIT = 20 * 1024 * 1024
 PACK_LIMIT = 60 * 1024 * 1024
 NT = (((1,), (1,)), ((), ()))
 TN = (((0,), (0,)), ((), ()))
@@ -70,9 +70,7 @@
     return lam, wide[:, 3 * heads : 4 * heads]
 
 
-def pack_kernel(
-    key_ref, value_ref, write_ref, read_ref, decay_ref, doc_ref, m_ref, n_ref
-):
+def pack_kernel(key_ref, value_ref, write_ref, decay_ref, doc_ref, m_ref):
     tokens, kv = key_ref.shape
     heads = decay_ref.shape[0]
     state = write_ref.shape[1]
@@ -83,8 +81,6 @@
     m_ref[:, kv : 2 * kv] = value_ref[...]
     m_ref[:, 2 * kv : 2 * kv + state] = write_ref[...]
     m_ref[:, 2 * kv + state :] = aux
-    n_ref[:, :state] = read_ref[...]
-    n_ref[:, state:] = jnp.zeros((tokens, n_ref.shape[1] - state), BF16)
 
 
 def attn_kernel(
@@ -98,6 +94,7 @@
     q_ref,
     cot_ref,
     far_ref,
+    entry_ref,
     out_ref,
     own_ref,
     back1_ref,
@@ -130,7 +127,6 @@
     )
     score = jnp.where(inside, dot(keys, query, NT) * inv_root, -1e30)
     raised = jnp.exp(score - jnp.max(score, axis=0, keepdims=True))
-    raised = jnp.where(inside, raised, 0.0)
     prob = (raised * (1.0 / jnp.sum(raised, axis=0, keepdims=True))).astype(BF16)
     out = dot(values, prob, TN).T
     for i in range(group):
@@ -155,12 +151,27 @@
     def _():
         state = read_ref.shape[1]
         back1_ref[:, 2 * kv : 2 * kv + state] = read_ref[...]
-        back1_ref[:, 2 * kv + state :] = m0[:, 2 * kv + state :]
+        back1_ref[:, 2 * kv + state :] = entry_ref[...]
         back2_ref[:, 2 * kv :] = far_ref[...]
 
 
 def local_kernel(
-    head_width, doc_ref, write_ref, read_ref, decay_ref, x_ref, cot_ref, mixed_ref, grad_ref
+    heads,
+    head_width,
+    doc_ref,
+    write_ref,
+    read_ref,
+    decay_ref,
+    aux1_ref,
+    aux2_ref,
+    x_ref,
+    cot_ref,
+    mixed_ref,
+    grad_ref,
+    entry_ref,
+    exit_ref,
+    exit1_ref,
+    gain_ref,
 ):
     tokens, cols = x_ref.shape
     step_heads = cols // head_width
@@ -172,6 +183,20 @@
     doc_col = jnp.broadcast_to(doc_row, (tokens, tokens)).T
     inside = (iota((tokens, tokens), 0) >= iota((tokens, tokens), 1)) & (doc_col == doc_row)
     score = dot(read_ref[...], write_ref[...], NT)
+    lam1, doc1 = aux_parts(aux1_ref[...], heads)
+    _, doc2 = aux_parts(aux2_ref[...], heads)
+    docs = doc_col[:, :step_heads] + 1.0
+    entry = jnp.exp(lam) * same(docs, last(doc1)[:, :1])
+    exit_w = jnp.exp(last(lam) - lam) * same(docs, last(docs))
+    to_cols = spread(step_heads, head_width, 0, cols)
+    entry_ref[...] = dot(thirds(entry), to_cols)
+    exit_ref[...] = dot(thirds(exit_w), to_cols)
+    exit1 = jnp.exp(last(lam1) - lam1) * same(doc1, last(doc1))
+    gain = jnp.exp(last(lam1)) * same(last(doc1), last(doc2))
+    gain = thirds(jnp.broadcast_to(gain, (16, heads)))
+    to_cols = spread(heads, head_width, pl.program_id(0) * cols, cols)
+    exit1_ref[...] = dot(thirds(exit1), to_cols)
+    gain_ref[...] = dot(gain, to_cols)[:8]
     per = HEAD_CHANNELS // head_width
     lane_head = iota((tokens, HEAD_CHANNELS), 1) // head_width
     for pair in range(step_heads // per):
@@ -228,6 +253,8 @@
     cot_ref,
     ahead_ref,
     behind_ref,
+    entry_ref,
+    take_ref,
 ):
     tokens, cols = x_ref.shape
     heads = decay_ref.shape[0]
@@ -237,7 +264,13 @@
     _, doc2 = aux_parts(aux2_ref[...], heads)
     gain = jnp.exp(last(lam1)) * same(last(doc1), last(doc2))
     exit_w = thirds(jnp.exp(last(lam) - lam) * same(docs, last(docs)))
-    entry = thirds(jnp.exp(lam) * same(docs, last(doc1)) * gain)
+    entry = jnp.exp(lam) * same(docs, last(doc1))
+    parts = [p.astype(F32) for p in split3(entry)] + [jnp.zeros_like(entry)]
+    entry_ref[...] = jnp.concatenate(parts, axis=1).astype(BF16)
+    entry = thirds(entry * gain)
+    take = jnp.where(iota((tokens, half), 0) == iota((tokens, half), 1) + half, 1.0, 0.0)
+    sums = dot(write_ref[...], read2_ref[:half], NT)
+    take_ref[...] = choose(tail_is_long(docs), sums, take).astype(BF16)
     ahead_score = dot(read2_ref[:half], write_ref[...], NT).astype(BF16)
     behind_score = dot(write2_ref[half:], read_ref[...], NT).astype(BF16)
     ahead_sums = tail_is_long(docs)
@@ -258,13 +291,23 @@
         ).astype(BF16)
 
 
+def in_steps(cols, step, out_ref, held_ref, sems, columns_of):
+    copies = []
+    for place, low in enumerate(range(0, cols, step)):
+        at = slice(low, low + step)
+        held_ref[:, at] = columns_of(low, at)
+        copies.append(
+            pltpu.make_async_copy(held_ref.at[:, at], out_ref.at[:, at], sems.at[place])
+        )
+        copies[-1].start()
+    for copy in copies:
+        copy.wait()
+
+
 def carried_kernel(
-    head_width,
-    decay_ref,
-    doc_ref,
+    step,
     read_ref,
     write1_ref,
-    aux1_ref,
     write2_ref,
     aux2_ref,
     odd_ref,
@@ -272,40 +315,37 @@
     then_ref,
     x2_ref,
     mixed_ref,
+    entry_ref,
+    exit1_ref,
+    gain_ref,
     out_ref,
+    held_ref,
+    sems,
 ):
     tokens, cols = first_ref.shape
+    half = tokens // 2
     odd = odd_ref[0, 0] == 1
-    heads = decay_ref.shape[0]
-    half = tokens // 2
-    lam, docs = own_numbers(decay_ref, doc_ref)
-    lam1, doc1 = aux_parts(aux1_ref[...], heads)
-    _, doc2 = aux_parts(aux2_ref[...], heads)
-    entry = thirds(jnp.exp(lam) * same(docs, last(doc1)))
-    gain = jnp.exp(last(lam1)) * same(last(doc1), last(doc2))
-    gain = thirds(jnp.broadcast_to(gain, (16, heads)))
-    exit1 = thirds(jnp.exp(last(lam1) - lam1) * same(doc1, last(doc1)))
+    _, doc2 = aux_parts(aux2_ref[...], aux2_ref.shape[1] // 4)
     score1 = dot(read_ref[...], write1_ref[...], NT).astype(BF16)
     take = jnp.where(iota((tokens, half), 0) == iota((tokens, half), 1), 1.0, 0.0)
     score2 = dot(read_ref[...], write2_ref[half:], NT)
     score2 = choose(tail_is_long(doc2), take, score2).astype(BF16)
-    step = min(cols, 512)
-    for low in range(0, cols, step):
-        at = slice(low, low + step)
-        to_cols = spread(heads, head_width, low, step)
+
+    def columns_of(low, at):
         x1 = jnp.where(odd, first_ref[:, at], then_ref[:, at])
-        x1 = (x1.astype(F32) * dot(exit1, to_cols)).astype(BF16)
-        carried = dot(score2, x2_ref[:, at]) * dot(gain, to_cols)[:1]
-        carried = (carried + dot(score1, x1)) * dot(entry, to_cols)
-        out_ref[:, at] = (mixed_ref[:, at] + carried).astype(BF16)
+        x1 = (x1.astype(F32) * exit1_ref[:, at]).astype(BF16)
+        carried = dot(score2, x2_ref[:, at]) * gain_ref[:1, at] + dot(score1, x1)
+        return (mixed_ref[:, at] + carried * entry_ref[:, at]).astype(BF16)
+
+    in_steps(cols, step, out_ref, held_ref, sems, columns_of)
 
 
 def returned_kernel(
+    heads,
     head_width,
-    decay_ref,
-    doc_ref,
+    step,
     write_ref,
-    read2_ref,
+    take_ref,
     r1_ref,
     r2_ref,
     own_ref,
@@ -313,43 +353,39 @@
     first_ref,
     then_ref,
     grad_ref,
+    exit_ref,
     out_ref,
     grad_key_ref,
     grad_value_ref,
 ):
-    tokens, cols = first_ref.shape
+    cols = first_ref.shape[1]
+    state = write_ref.shape[1]
+    half = take_ref.shape[1]
     odd = odd_ref[0, 0] == 1
-    heads = decay_ref.shape[0]
-    state = write_ref.shape[1]
-    half = tokens // 2
     width = HEAD_CHANNELS
     kv2 = own_ref.shape[1]
+    score1 = dot(write_ref[...], r1_ref[:, kv2 : kv2 + state], NT).astype(BF16)
+    entry1 = r1_ref[:, kv2 + state : kv2 + state + 3 * heads]
     total = own_ref[...] + r1_ref[:, :kv2].astype(F32) + r2_ref[:, :kv2].astype(F32)
     for g in range(kv2 // (2 * width)):
         at = slice(g * width, (g + 1) * width)
         low = 2 * g * width
         grad_key_ref[:, at] = total[:, low : low + width].astype(BF16)
         grad_value_ref[:, at] = total[:, low + width : low + 2 * width].astype(BF16)
-    lam, docs = own_numbers(decay_ref, doc_ref)
-    lam1, doc1 = aux_parts(r1_ref[:, kv2 + state :], heads)
-    exit_w = thirds(jnp.exp(last(lam) - lam) * same(docs, last(docs)))
-    entry1 = thirds(jnp.exp(lam1) * same(doc1, last(docs)))
-    score1 = dot(write_ref[...], r1_ref[:, kv2 : kv2 + state], NT).astype(BF16)
-    take = jnp.where(iota((tokens, half), 0) == iota((tokens, half), 1) + half, 1.0, 0.0)
-    score2 = dot(write_ref[...], read2_ref[:half], NT)
-    score2 = choose(tail_is_long(docs), score2, take).astype(BF16)
-    step = min(cols // 2, 512)
-    for low in range(0, cols, step):
-        at = slice(low, low + step)
-        to_cols = spread(heads, head_width, low, step)
+
+    def columns_of(low, at):
         c1 = jnp.where(odd, then_ref[:, at], first_ref[:, at])
-        c1 = (c1.astype(F32) * dot(entry1, to_cols)).astype(BF16)
+        entry = dot(entry1, spread(heads, head_width, low, step))
+        c1 = (c1.astype(F32) * entry).astype(BF16)
         row = low // (cols // 2) * half
         col = kv2 + low % (cols // 2)
         far = r2_ref[row : row + half, col : col + step]
-        returned = (dot(score1, c1) + dot(score2, far)) * dot(exit_w, to_cols)
-        out_ref[:, at] = (grad_ref[:, at] + returned).astype(BF16)
-
+        returned = dot(score1, c1) + dot(take_ref[...], far)
+        return (grad_ref[:, at] + returned * exit_ref[:, at]).astype(BF16)
+
+    for low in range(0, cols, step):
+        at = slice(low, low + step)
+        out_ref[:, at] = columns_of(low, at)
 
 def whole(shape):
     return pl.BlockSpec(shape, lambda i: (0, 0))
@@ -392,40 +428,43 @@
     params = pltpu.CompilerParams(vmem_limit_bytes=VMEM_LIMIT)
 
     odd = lax.axis_index("ctx") % 2
-    first_sent = jnp.where(odd == 0, ssm_input, cot_mixer)
-    then_sent = jnp.where(odd == 0, cot_mixer, ssm_input)
+    read2 = passed_along(state_read, "ctx", -2)
+    m0 = pl.pallas_call(
+        pack_kernel,
+        out_shape=shape((tokens, m_cols), BF16),
+        compiler_params=pltpu.CompilerParams(vmem_limit_bytes=PACK_LIMIT),
+        name="pack",
+    )(key_head_matrix, value_head_matrix, state_write, decay_t, doc_row)
+    m1 = passed_along(m0, "ctx", 1)
+    m2 = passed_along(m0, "ctx", 2)
+    x0, cot0, read2 = lax.optimization_barrier((ssm_input, cot_mixer, read2))
+    first_sent = jnp.where(odd == 0, x0, cot0)
+    then_sent = jnp.where(odd == 0, cot0, x0)
     odd = odd.reshape(1, 1)
     first = exchanged(first_sent, "ctx", 0)
-    m0, n0 = pl.pallas_call(
-        pack_kernel,
-        out_shape=(shape((tokens, m_cols), BF16),) * 2,
-        compiler_params=pltpu.CompilerParams(vmem_limit_bytes=PACK_LIMIT),
-        name="pack",
-    )(key_head_matrix, value_head_matrix, state_write, state_read, decay_t, doc_row)
-    m1 = passed_along(m0, "ctx", 1)
-    m2 = passed_along(m0, "ctx", 2)
-    read2 = passed_along(n0, "ctx", -2)
     then = exchanged(then_sent, "ctx", 1)
     decay_local, m1, m2, read2 = lax.optimization_barrier((decay_t, m1, m2, read2))
-    mixed, grad = pl.pallas_call(
-        functools.partial(local_kernel, head_width),
+    write_at = 2 * kv
+    mixed, grad, entry_w, exit_w, exit1_w, gain_w = pl.pallas_call(
+        functools.partial(local_kernel, heads, head_width),
         grid=(steps,),
         in_specs=[
             whole((1, tokens)),
             whole((tokens, state)),
             whole((tokens, state)),
             pl.BlockSpec((heads // steps, tokens), lambda i: (i, 0)),
+            part(tokens, aux, write_at + state),
+            part(tokens, aux, write_at + state),
             columns(tokens, step_cols),
             columns(tokens, step_cols),
         ],
-        out_specs=[columns(tokens, step_cols)] * 2,
-        out_shape=(shape(ssm_input.shape, F32),) * 2,
+        out_specs=[columns(tokens, step_cols)] * 5 + [columns(8, step_cols)],
+        out_shape=(shape(ssm_input.shape, F32),) * 5 + (shape((8, cols), F32),),
         compiler_params=params,
         name="local_mixer",
-    )(doc_row, state_write, state_read, decay_local, ssm_input, cot_mixer)
-
-    write_at = 2 * kv
-    ahead, behind = pl.pallas_call(
+    )(doc_row, state_write, state_read, decay_local, m1, m2, ssm_input, cot_mixer)
+
+    ahead, behind, entry_parts, take2 = pl.pallas_call(
         functools.partial(far_kernel, head_width),
         grid=(1,),
         in_specs=[
@@ -433,17 +472,24 @@
             whole((1, tokens)),
             whole((tokens, state)),
             whole((tokens, state)),
-            part(tokens, state, 0),
+            whole((tokens, state)),
             part(tokens, aux, write_at + state),
             part(tokens, state, write_at),
             part(tokens, aux, write_at + state),
             whole((tokens, cols)),
             whole((tokens, cols)),
         ],
-        out_specs=[whole((tokens // 2, cols)), whole((tokens, cols // 2))],
+        out_specs=[
+            whole((tokens // 2, cols)),
+            whole((tokens, cols // 2)),
+            whole((tokens, aux)),
+            whole((tokens, tokens // 2)),
+        ],
         out_shape=(
             shape((tokens // 2, cols), BF16),
             shape((tokens, cols // 2), BF16),
+            shape((tokens, aux), BF16),
+            shape((tokens, tokens // 2), BF16),
         ),
         compiler_params=params,
         name="far",
@@ -455,7 +501,7 @@
         in_specs=[whole((1, tokens)), whole((tokens, state))]
         + [whole((tokens, m_cols))] * 3
         + [columns(tokens, group_cols)] * 2
-        + [whole((tokens, cols // 2))],
+        + [whole((tokens, cols // 2)), whole((tokens, aux))],
         out_specs=[
             columns(tokens, group_cols),
             whole((tokens, 2 * kv)),
@@ -470,51 +516,52 @@
         ),
         compiler_params=params,
         name="attention",
-    )(doc_row, state_read, m0, m1, m2, query_head_matrix, attention_output_gradient, behind)
+    )(doc_row, state_read, m0, m1, m2, query_head_matrix, attention_output_gradient, behind, entry_parts)
     r1 = passed_along(back1, "ctx", -1)
     r2 = passed_along(back2, "ctx", -2)
 
 
+    smem = pl.BlockSpec(memory_space=pltpu.SMEM)
+    half_step = min(step_cols, cols // 2)
+    held = [
+        pltpu.VMEM((tokens, cols), BF16),
+        pltpu.SemaphoreType.DMA((cols // half_step,)),
+    ]
     mixer_out = pl.pallas_call(
-        functools.partial(carried_kernel, head_width),
+        functools.partial(carried_kernel, half_step),
         grid=(1,),
         in_specs=[
-            whole((heads, tokens)),
-            whole((1, tokens)),
-            whole((tokens, state)),
+            whole((tokens, state)),
+            part(tokens, state, write_at),
             part(tokens, state, write_at),
             part(tokens, aux, write_at + state),
-            part(tokens, state, write_at),
-            part(tokens, aux, write_at + state),
-            pl.BlockSpec(memory_space=pltpu.SMEM),
+            smem,
             whole((tokens, cols)),
             whole((tokens, cols)),
             whole((tokens // 2, cols)),
-            whole((tokens, cols)),
-        ],
-        out_specs=whole((tokens, cols)),
+        ]
+        + [whole((tokens, cols))] * 3
+        + [whole((8, cols))],
+        out_specs=pl.BlockSpec(memory_space=pl.ANY),
         out_shape=shape(ssm_input.shape, BF16),
+        scratch_shapes=held,
         compiler_params=params,
         name="carried",
-    )(decay_t, doc_row, state_read, m1, m1, m2, m2, odd, first, then, x2, mixed)
+    )(state_read, m1, m2, m2, odd, first, then, x2, mixed, entry_w, exit1_w, gain_w)
 
     own, mixer_out = lax.optimization_barrier((own, mixer_out))
     grad_input, grad_key, grad_value = pl.pallas_call(
-        functools.partial(returned_kernel, head_width),
+        functools.partial(returned_kernel, heads, head_width, half_step),
         grid=(1,),
         in_specs=[
-            whole((heads, tokens)),
-            whole((1, tokens)),
-            whole((tokens, state)),
-            part(tokens, state, 0),
+            whole((tokens, state)),
+            whole((tokens, tokens // 2)),
             whole((tokens, m_cols)),
             whole((tokens, 2 * kv + cols // 2)),
             whole((tokens, 2 * kv)),
-            pl.BlockSpec(memory_space=pltpu.SMEM),
-            whole((tokens, cols)),
-            whole((tokens, cols)),
-            whole((tokens, cols)),
-        ],
+            smem,
+        ]
+        + [whole((tokens, cols))] * 4,
         out_specs=[whole((tokens, cols))] + [whole((tokens, kv))] * 2,
         out_shape=(
             shape(cot_mixer.shape, BF16),
@@ -523,7 +570,7 @@
         ),
         compiler_params=params,
         name="returned",
-    )(decay_t, doc_row, state_write, read2, r1, r2, own, odd, first, then, grad)
+    )(state_write, take2, r1, r2, own, odd, first, then, grad, exit_w)
     return (attention_out, mixer_out, grad_key, grad_value, grad_input)
 
 

time: 44.5 us -> 44.1 us (level)
  waiting for transfers between devices: 5.32 us -> 7.04 us
  starting transfers between devices: 22.2 us -> 21 us
  Pallas kernels: 14.4 us -> 13.5 us
    ppermute x6, waiting for transfers between devices: 1.03 us -> 2.75 us  [passed_along(): return lax.ppermute(block, axis, route)]
    ppermute x2, starting transfers between devices: 5.12 us -> 3.64 us  [exchanged(): return lax.ppermute(block, axis, route)]
    pallas_call x4, Pallas kernels: 9.36 us -> 8.46 us  [the longest x1 3.54 us: shards(): pl.pallas_call(functools.partial(local_kernel, heads, head_width), grid=(...]
  transfers between devices with their start and end apart: 8 -> 8, of which waited for: 3 -> 4; matrix products, arithmetic and copies ran while one was open for 3% -> 3% of each run, Pallas kernels for 23% -> 27%
where the time goes in v4:
time: 44.1 us; the launch traced here: 43.7 us
  starting transfers between devices  21 us (48%)
  Pallas kernels  13.5 us (31%)
  waiting for transfers between devices  7.04 us (16%)
  other arithmetic  1.35 us (3%)
  between operations  0.85 us (2%)
    ppermute x6, starting transfers between devices, passed_along(): return lax.ppermute(block, axis, route)  17.3 us
    ppermute x2, waiting for transfers between devices, exchanged(): return lax.ppermute(block, axis, route)  4.29 us
    ppermute x2, starting transfers between devices, exchanged(): return lax.ppermute(block, axis, route)  3.64 us
    pallas_call x1, Pallas kernels, shards(): pl.pallas_call(functools.partial(local_kernel, heads, head_width), grid=(...  3.54 us
    pallas_call x1, Pallas kernels, shards(): pl.pallas_call(functools.partial(attn_kernel, kv, 2 * kv + state + 3 * he...  3.23 us
    ppermute x6, waiting for transfers between devices, passed_along(): return lax.ppermute(block, axis, route)  2.75 us
    pallas_call x1, Pallas kernels, shards(): pl.pallas_call(pack_kernel, out_shape=shape((tokens, m_cols), BF16), comp...  1.83 us
    pallas_call x1, Pallas kernels, shards(): pl.pallas_call(functools.partial(returned_kernel, heads, head_width, half...  1.8 us
  transfers between devices with their start and end apart: 8, of which 4 were waited for; matrix products, arithmetic and copies ran while one was open for 3% of the time, Pallas kernels for 27%

profile of v4, /device:TPU:14, one launch (start us, length us, event | category | flops | bytes accessed | tf_op | source)
XLA Modules:
  0.0 43.7 jit_solution(4538288897175099720)
XLA Ops:
  0.6 2.4 %collective-permute-start.2 = (bf16[128,128]{1,0:T(8,128)(2,1)}, bf16[128,128]{1,0:T(8,128)(2,1)S(1)}, u32[]{:S(2)}, u32[]{:S(2)}) collective-permute-start(bf16[128,128]{1,0:T(8,128)(2,1)} %read_ref.7), channel_id=1, source_target_pairs={{8,0},{12,4},{16,8},{20,12},{24,16},{28,20},{9,1},{13,5},{17,9},{2... | collective-permute-start | bytes 98312 | tf_op jit(solution)/shard_map/ppermute | solution.py:23
  3.0 1.8 %pack.1.m0 = bf16[128,768]{1,0:T(8,128)(2,1)} custom-call(bf16[128,256]{1,0:T(8,128)(2,1)} %key_ref.1, bf16[128,256]{1,0:T(8,128)(2,1)} %value_ref.1, bf16[128,128]{1,0:T(8,128)(2,1)} %write_ref.7, f32[32,128]{1,0:T(8,128)} %bitcast.3, s32[1,128]{1,0:T(1,128)} %bitcast.6), custom_call_target="tpu_custom_call" | custom-call | tf_op jit(solution)/shard_map/pack/pallas_call | solution.py:432
  4.8 3.4 %collective-permute-start = (bf16[128,768]{1,0:T(8,128)(2,1)}, bf16[128,768]{1,0:T(8,128)(2,1)S(1)}, u32[]{:S(2)}, u32[]{:S(2)}) collective-permute-start(bf16[128,768]{1,0:T(8,128)(2,1)} %pack.1.m0), channel_id=1, source_target_pairs={{0,4},{4,8},{8,12},{12,16},{16,20},{20,24},{24,28},{1,5},{5,9},{9,... | collective-permute-start | bytes 589832 | tf_op jit(solution)/shard_map/ppermute | solution.py:23
  8.3 3.5 %collective-permute-start.1 = (bf16[128,768]{1,0:T(8,128)(2,1)}, bf16[128,768]{1,0:T(8,128)(2,1)S(1)}, u32[]{:S(2)}, u32[]{:S(2)}) collective-permute-start(bf16[128,768]{1,0:T(8,128)(2,1)} %pack.1.m0), channel_id=1, source_target_pairs={{0,8},{4,12},{8,16},{12,20},{16,24},{20,28},{1,9},{5,13},{9,17},{1... | collective-permute-start | bytes 589832 | tf_op jit(solution)/shard_map/ppermute | solution.py:23
  11.8 0.0 copy-start
  11.8 0.0 copy-start.1
  11.8 0.0 copy-start.3
  11.8 0.0 copy-start.4
  11.8 0.0 copy-start.7
  11.8 0.0 collective-permute-done.2.read2_ref
  11.9 1.3 %broadcast_select_fusion = (bf16[128,2048]{1,0:T(8,128)(2,1)S(1)}, bf16[128,2048]{1,0:T(8,128)(2,1)S(1)}) fusion(bf16[128,2048]{1,0:T(8,128)(2,1)} %cot_ref.5, bf16[128,2048]{1,0:T(8,128)(2,1)} %x_ref.3, pred[]{:T(512)S(6)} %eq.6), kind=kLoop, calls=%fused_computation | loop fusion | flops 524288 | bytes 2097153 | tf_op jit(solution)/shard_map/jit(_where)/select_n | solution.py:442
  13.2 0.0 copy-start.8
  13.2 0.5 %collective-permute-start.3 = (bf16[128,2048]{1,0:T(8,128)(2,1)S(1)}, bf16[128,2048]{1,0:T(8,128)(2,1)S(1)}, u32[]{:S(2)}, u32[]{:S(2)}) collective-permute-start(bf16[128,2048]{1,0:T(8,128)(2,1)S(1)} %get-tuple-element.58), channel_id=1, source_target_pairs={{0,4},{4,0},{8,12},{12,8},{16,20},{20,16},{24,28},{28,24},{1,5},{5... | collective-permute-start | bytes 1572872 | tf_op jit(solution)/shard_map/ppermute | solution.py:31
  13.8 0.0 copy-start.2
  13.8 0.0 copy-start.5
  13.8 0.0 copy-start.6
  13.8 3.1 %collective-permute-start.4 = (bf16[128,2048]{1,0:T(8,128)(2,1)S(1)}, bf16[128,2048]{1,0:T(8,128)(2,1)S(1)}, u32[]{:S(2)}, u32[]{:S(2)}) collective-permute-start(bf16[128,2048]{1,0:T(8,128)(2,1)S(1)} %get-tuple-element.57), channel_id=1, source_target_pairs={{4,8},{8,4},{12,16},{16,12},{20,24},{24,20},{5,9},{9,5},{13,17},{1... | collective-permute-start | bytes 1572872 | tf_op jit(solution)/shard_map/ppermute | solution.py:31
  16.9 0.0 collective-permute-done.aux1_ref.m1.write1_ref
  16.9 0.6 %collective-permute-done.1.write2_ref.aux2_ref.m2 = bf16[128,768]{1,0:T(8,128)(2,1)S(1)} collective-permute-done((bf16[128,768]{1,0:T(8,128)(2,1)}, bf16[128,768]{1,0:T(8,128)(2,1)S(1)}, u32[]{:S(2)}, u32[]{:S(2)}) %collective-permute-start.1) | collective-permute-done | bytes 196640 | tf_op jit(solution)/shard_map/ppermute | solution.py:23
  17.5 0.0 copy-done
  17.5 0.0 copy-done.1
  17.5 0.0 copy-done.3
  17.5 0.0 copy-done.4
  17.5 0.0 copy-done.7
  17.5 0.0 copy-done.8
  17.5 1.8 %far.1 = (bf16[64,2048]{1,0:T(8,128)(2,1)S(1)}, bf16[128,1024]{1,0:T(8,128)(2,1)S(1)}, bf16[128,128]{1,0:T(8,128)(2,1)S(1)}, bf16[128,64]{1,0:T(8,128)(2,1)S(1)}) custom-call(f32[32,128]{1,0:T(8,128)S(1)} %bitcast.4, s32[1,128]{1,0:T(1,128)S(1)} %bitcast.7, bf16[128,128]{1,0:T(8,128)(2,1)S(1)} %copy-done.4, bf16[128,128]{1,0:T(8,128)(2,1)S(1)} %copy-done.3, ...), custom_call_target="tpu_custom_call" | custom-call | tf_op jit(solution)/shard_map/far/pallas_call | solution.py:467
  19.3 0.0 copy-done.2
  19.3 0.0 copy-done.5
  19.3 0.0 copy-done.6
  19.3 3.2 %attention.1 = (bf16[128,1024]{1,0:T(8,128)(2,1)}, f32[128,512]{1,0:T(8,128)S(1)}, bf16[128,768]{1,0:T(8,128)(2,1)S(1)}, bf16[128,1536]{1,0:T(8,128)(2,1)S(1)}) custom-call(s32[1,128]{1,0:T(1,128)S(1)} %bitcast.8, bf16[128,128]{1,0:T(8,128)(2,1)S(1)} %copy-done.4, bf16[128,768]{1,0:T(8,128)(2,1)S(1)} %copy-done.2, ...), custom_call_target="tpu_custom_call" | custom-call | tf_op jit(solution)/shard_map/attention/pallas_call | solution.py:498
  22.6 3.3 %collective-permute-start.7 = (bf16[128,1536]{1,0:T(8,128)(2,1)S(1)}, bf16[128,1536]{1,0:T(8,128)(2,1)S(1)}, u32[]{:S(2)}, u32[]{:S(2)}) collective-permute-start(bf16[128,1536]{1,0:T(8,128)(2,1)S(1)} %get-tuple-element.50), channel_id=1, source_target_pairs={{8,0},{12,4},{16,8},{20,12},{24,16},{28,20},{9,1},{13,5},{17,9},{2... | collective-permute-start | bytes 1179656 | tf_op jit(solution)/shard_map/ppermute | solution.py:23
  25.9 2.8 %collective-permute-start.5 = (bf16[64,2048]{1,0:T(8,128)(2,1)S(1)}, bf16[64,2048]{1,0:T(8,128)(2,1)S(1)}, u32[]{:S(2)}, u32[]{:S(2)}) collective-permute-start(bf16[64,2048]{1,0:T(8,128)(2,1)S(1)} %get-tuple-element.41), channel_id=1, source_target_pairs={{0,8},{4,12},{8,16},{12,20},{16,24},{20,28},{1,9},{5,13},{9,17},{1... | collective-permute-start | bytes 786440 | tf_op jit(solution)/shard_map/ppermute | solution.py:23
  28.6 2.0 %collective-permute-start.6 = (bf16[128,768]{1,0:T(8,128)(2,1)S(1)}, bf16[128,768]{1,0:T(8,128)(2,1)S(1)}, u32[]{:S(2)}, u32[]{:S(2)}) collective-permute-start(bf16[128,768]{1,0:T(8,128)(2,1)S(1)} %get-tuple-element.49), channel_id=1, source_target_pairs={{4,0},{8,4},{12,8},{16,12},{20,16},{24,20},{28,24},{5,1},{9,5},{13... | collective-permute-start | bytes 589832 | tf_op jit(solution)/shard_map/ppermute | solution.py:23
  30.6 3.5 %local_mixer.1 = (f32[128,2048]{1,0:T(8,128)S(1)}, f32[128,2048]{1,0:T(8,128)S(1)}, f32[128,2048]{1,0:T(8,128)S(1)}, f32[128,2048]{1,0:T(8,128)S(1)}, f32[128,2048]{1,0:T(8,128)S(1)}, /*index=5*/f32[8,2048]{1,0:T(8,128)S(1)}) custom-call(s32[1,128]{1,0:T(1,128)S(1)} %bitcast.9, bf16[128,128]{1,0:T(8,128)(2,1)S(1)} %copy-done.3, ...), custom_call_target="tpu_custom_call" | custom-call | tf_op jit(solution)/shard_map/local_mixer/pallas_call | solution.py:448
  34.2 0.8 %collective-permute-done.5.x2_ref = bf16[64,2048]{1,0:T(8,128)(2,1)S(1)} collective-permute-done((bf16[64,2048]{1,0:T(8,128)(2,1)S(1)}, bf16[64,2048]{1,0:T(8,128)(2,1)S(1)}, u32[]{:S(2)}, u32[]{:S(2)}) %collective-permute-start.5) | collective-permute-done | bytes 262176 | tf_op jit(solution)/shard_map/ppermute | solution.py:23
  35.0 4.3 %collective-permute-done.3.first_ref = bf16[128,2048]{1,0:T(8,128)(2,1)S(1)} collective-permute-done((bf16[128,2048]{1,0:T(8,128)(2,1)S(1)}, bf16[128,2048]{1,0:T(8,128)(2,1)S(1)}, u32[]{:S(2)}, u32[]{:S(2)}) %collective-permute-start.3) | collective-permute-done | bytes 524320 | tf_op jit(solution)/shard_map/ppermute | solution.py:31
  39.3 0.0 collective-permute-done.4.then_ref
  39.3 1.3 %carried.1 = bf16[128,2048]{1,0:T(8,128)(2,1)} custom-call(bf16[128,128]{1,0:T(8,128)(2,1)S(1)} %copy-done.4, bf16[128,768]{1,0:T(8,128)(2,1)S(1)} %collective-permute-done.aux1_ref.m1.write1_ref, bf16[128,768]{1,0:T(8,128)(2,1)S(1)} %collective-permute-done.1.write2_ref.aux2_ref.m2, bf16[128,768]{1,0:T(8,128)(2,1)S(1)} %collective-permute-done.1.write2_ref.aux2_ref.m2, ...), custom_call_target="tpu_custom_call" | custom-call | tf_op jit(solution)/shard_map/carried/pallas_call | solution.py:530
  40.6 1.4 %collective-permute-done.6.r1_ref = bf16[128,768]{1,0:T(8,128)(2,1)S(1)} collective-permute-done((bf16[128,768]{1,0:T(8,128)(2,1)S(1)}, bf16[128,768]{1,0:T(8,128)(2,1)S(1)}, u32[]{:S(2)}, u32[]{:S(2)}) %collective-permute-start.6) | collective-permute-done | bytes 196640 | tf_op jit(solution)/shard_map/ppermute | solution.py:23
  41.9 0.0 collective-permute-done.7.r2_ref
  41.9 1.8 %returned.1 = (bf16[128,2048]{1,0:T(8,128)(2,1)}, bf16[128,256]{1,0:T(8,128)(2,1)}, bf16[128,256]{1,0:T(8,128)(2,1)}) custom-call(bf16[128,128]{1,0:T(8,128)(2,1)S(1)} %copy-done.3, bf16[128,64]{1,0:T(8,128)(2,1)S(1)} %get-tuple-element.48.take_ref, bf16[128,768]{1,0:T(8,128)(2,1)S(1)} %collective-permute-done.6.r1_ref, ...), custom_call_target="tpu_custom_call" | custom-call | tf_op jit(solution)/shard_map/returned/pallas_call | solution.py:553
Async XLA Ops:
  0.6 11.2 %collective-permute-start.2 = (bf16[128,128]{1,0:T(8,128)(2,1)}, bf16[128,128]{1,0:T(8,128)(2,1)S(1)}, u32[]{:S(2)}, u32[]{:S(2)}) collective-permute-start(bf16[128,128]{1,0:T(8,128)(2,1)} %read_ref.7), channel_id=1, source_target_pairs={{8,0},{12,4},{16,8},{20,12},{24,16},{28,20},{9,1},{13,5},{17,9},{2... | collective-permute-start | bytes 98312 | tf_op jit(solution)/shard_map/ppermute | solution.py:23
  4.8 12.0 %collective-permute-start = (bf16[128,768]{1,0:T(8,128)(2,1)}, bf16[128,768]{1,0:T(8,128)(2,1)S(1)}, u32[]{:S(2)}, u32[]{:S(2)}) collective-permute-start(bf16[128,768]{1,0:T(8,128)(2,1)} %pack.1.m0), channel_id=1, source_target_pairs={{0,4},{4,8},{8,12},{12,16},{16,20},{20,24},{24,28},{1,5},{5,9},{9,... | collective-permute-start | bytes 589832 | tf_op jit(solution)/shard_map/ppermute | solution.py:23
  8.3 9.2 %collective-permute-start.1 = (bf16[128,768]{1,0:T(8,128)(2,1)}, bf16[128,768]{1,0:T(8,128)(2,1)S(1)}, u32[]{:S(2)}, u32[]{:S(2)}) collective-permute-start(bf16[128,768]{1,0:T(8,128)(2,1)} %pack.1.m0), channel_id=1, source_target_pairs={{0,8},{4,12},{8,16},{12,20},{16,24},{20,28},{1,9},{5,13},{9,17},{1... | collective-permute-start | bytes 589832 | tf_op jit(solution)/shard_map/ppermute | solution.py:23
  11.8 5.7 %copy-start = (bf16[128,2048]{1,0:T(8,128)(2,1)S(1)}, bf16[128,2048]{1,0:T(8,128)(2,1)}, u32[]{:S(2)}) copy-start(bf16[128,2048]{1,0:T(8,128)(2,1)} %x_ref.3) | copy-start | bytes 1572868
  11.8 5.7 %copy-start.1 = (bf16[128,2048]{1,0:T(8,128)(2,1)S(1)}, bf16[128,2048]{1,0:T(8,128)(2,1)}, u32[]{:S(2)}) copy-start(bf16[128,2048]{1,0:T(8,128)(2,1)} %cot_ref.5) | copy-start | bytes 1572868
  11.8 5.7 %copy-start.3 = (bf16[128,128]{1,0:T(8,128)(2,1)S(1)}, bf16[128,128]{1,0:T(8,128)(2,1)}, u32[]{:S(2)}) copy-start(bf16[128,128]{1,0:T(8,128)(2,1)} %write_ref.7) | copy-start | bytes 98308
  11.8 5.7 %copy-start.4 = (bf16[128,128]{1,0:T(8,128)(2,1)S(1)}, bf16[128,128]{1,0:T(8,128)(2,1)}, u32[]{:S(2)}) copy-start(bf16[128,128]{1,0:T(8,128)(2,1)} %read_ref.7) | copy-start | bytes 98308
  11.8 5.7 %copy-start.7 = (f32[128,32]{0,1:T(8,128)S(1)}, f32[128,32]{0,1:T(8,128)}, u32[]{:S(2)}) copy-start(f32[128,32]{0,1:T(8,128)} %param.14) | copy-start | bytes 49156
  13.2 4.3 %copy-start.8 = (s32[128]{0:T(128)S(1)}, s32[128]{0:T(128)}, u32[]{:S(2)}) copy-start(s32[128]{0:T(128)} %param.17) | copy-start | bytes 1540
  13.2 26.0 %collective-permute-start.3 = (bf16[128,2048]{1,0:T(8,128)(2,1)S(1)}, bf16[128,2048]{1,0:T(8,128)(2,1)S(1)}, u32[]{:S(2)}, u32[]{:S(2)}) collective-permute-start(bf16[128,2048]{1,0:T(8,128)(2,1)S(1)} %get-tuple-element.58), channel_id=1, source_target_pairs={{0,4},{4,0},{8,12},{12,8},{16,20},{20,16},{24,28},{28,24},{1,5},{5... | collective-permute-start | bytes 1572872 | tf_op jit(solution)/shard_map/ppermute | solution.py:31
  13.8 5.5 %copy-start.2 = (bf16[128,768]{1,0:T(8,128)(2,1)S(1)}, bf16[128,768]{1,0:T(8,128)(2,1)}, u32[]{:S(2)}) copy-start(bf16[128,768]{1,0:T(8,128)(2,1)} %pack.1.m0) | copy-start | bytes 589828
  13.8 5.5 %copy-start.5 = (bf16[128,1024]{1,0:T(8,128)(2,1)S(1)}, bf16[128,1024]{1,0:T(8,128)(2,1)}, u32[]{:S(2)}) copy-start(bf16[128,1024]{1,0:T(8,128)(2,1)} %q_ref.1) | copy-start | bytes 786436
  13.8 5.5 %copy-start.6 = (bf16[128,1024]{1,0:T(8,128)(2,1)S(1)}, bf16[128,1024]{1,0:T(8,128)(2,1)}, u32[]{:S(2)}) copy-start(bf16[128,1024]{1,0:T(8,128)(2,1)} %cot_ref.4) | copy-start | bytes 786436
  13.8 25.5 %collective-permute-start.4 = (bf16[128,2048]{1,0:T(8,128)(2,1)S(1)}, bf16[128,2048]{1,0:T(8,128)(2,1)S(1)}, u32[]{:S(2)}, u32[]{:S(2)}) collective-permute-start(bf16[128,2048]{1,0:T(8,128)(2,1)S(1)} %get-tuple-element.57), channel_id=1, source_target_pairs={{4,8},{8,4},{12,16},{16,12},{20,24},{24,20},{5,9},{9,5},{13,17},{1... | collective-permute-start | bytes 1572872 | tf_op jit(solution)/shard_map/ppermute | solution.py:31
  22.6 19.4 %collective-permute-start.7 = (bf16[128,1536]{1,0:T(8,128)(2,1)S(1)}, bf16[128,1536]{1,0:T(8,128)(2,1)S(1)}, u32[]{:S(2)}, u32[]{:S(2)}) collective-permute-start(bf16[128,1536]{1,0:T(8,128)(2,1)S(1)} %get-tuple-element.50), channel_id=1, source_target_pairs={{8,0},{12,4},{16,8},{20,12},{24,16},{28,20},{9,1},{13,5},{17,9},{2... | collective-permute-start | bytes 1179656 | tf_op jit(solution)/shard_map/ppermute | solution.py:23
  25.9 9.1 %collective-permute-start.5 = (bf16[64,2048]{1,0:T(8,128)(2,1)S(1)}, bf16[64,2048]{1,0:T(8,128)(2,1)S(1)}, u32[]{:S(2)}, u32[]{:S(2)}) collective-permute-start(bf16[64,2048]{1,0:T(8,128)(2,1)S(1)} %get-tuple-element.41), channel_id=1, source_target_pairs={{0,8},{4,12},{8,16},{12,20},{16,24},{20,28},{1,9},{5,13},{9,17},{1... | collective-permute-start | bytes 786440 | tf_op jit(solution)/shard_map/ppermute | solution.py:23
  28.6 13.3 %collective-permute-start.6 = (bf16[128,768]{1,0:T(8,128)(2,1)S(1)}, bf16[128,768]{1,0:T(8,128)(2,1)S(1)}, u32[]{:S(2)}, u32[]{:S(2)}) collective-permute-start(bf16[128,768]{1,0:T(8,128)(2,1)S(1)} %get-tuple-element.49), channel_id=1, source_target_pairs={{4,0},{8,4},{12,8},{16,12},{20,16},{24,20},{28,24},{5,1},{9,5},{13... | collective-permute-start | bytes 589832 | tf_op jit(solution)/shard_map/ppermute | solution.py:23

commit v5 on v4

--- a/solution.py
+++ b/solution.py
@@ -152,7 +152,9 @@
         state = read_ref.shape[1]
         back1_ref[:, 2 * kv : 2 * kv + state] = read_ref[...]
         back1_ref[:, 2 * kv + state :] = entry_ref[...]
-        back2_ref[:, 2 * kv :] = far_ref[...]
+        far_cols = far_ref.shape[1]
+        back2_ref[:, 2 * kv : 2 * kv + far_cols] = far_ref[...]
+        back2_ref[:, 2 * kv + far_cols :] = read_ref[...]
 
 
 def local_kernel(
@@ -171,7 +173,7 @@
     entry_ref,
     exit_ref,
     exit1_ref,
-    gain_ref,
+    exit2_ref,
 ):
     tokens, cols = x_ref.shape
     step_heads = cols // head_width
@@ -184,7 +186,7 @@
     inside = (iota((tokens, tokens), 0) >= iota((tokens, tokens), 1)) & (doc_col == doc_row)
     score = dot(read_ref[...], write_ref[...], NT)
     lam1, doc1 = aux_parts(aux1_ref[...], heads)
-    _, doc2 = aux_parts(aux2_ref[...], heads)
+    lam2, doc2 = aux_parts(aux2_ref[...], heads)
     docs = doc_col[:, :step_heads] + 1.0
     entry = jnp.exp(lam) * same(docs, last(doc1)[:, :1])
     exit_w = jnp.exp(last(lam) - lam) * same(docs, last(docs))
@@ -193,10 +195,10 @@
     exit_ref[...] = dot(thirds(exit_w), to_cols)
     exit1 = jnp.exp(last(lam1) - lam1) * same(doc1, last(doc1))
     gain = jnp.exp(last(lam1)) * same(last(doc1), last(doc2))
-    gain = thirds(jnp.broadcast_to(gain, (16, heads)))
+    exit2 = jnp.exp(last(lam2) - lam2) * same(doc2, last(doc2)) * gain
     to_cols = spread(heads, head_width, pl.program_id(0) * cols, cols)
     exit1_ref[...] = dot(thirds(exit1), to_cols)
-    gain_ref[...] = dot(gain, to_cols)[:8]
+    exit2_ref[...] = dot(thirds(exit2), to_cols)
     per = HEAD_CHANNELS // head_width
     lane_head = iota((tokens, HEAD_CHANNELS), 1) // head_width
     for pair in range(step_heads // per):
@@ -244,50 +246,37 @@
     decay_ref,
     doc_ref,
     read_ref,
-    write_ref,
-    read2_ref,
     aux1_ref,
     write2_ref,
     aux2_ref,
-    x_ref,
     cot_ref,
-    ahead_ref,
     behind_ref,
     entry_ref,
-    take_ref,
+    long_ref,
 ):
-    tokens, cols = x_ref.shape
+    tokens, cols = cot_ref.shape
     heads = decay_ref.shape[0]
     half = tokens // 2
     lam, docs = own_numbers(decay_ref, doc_ref)
     lam1, doc1 = aux_parts(aux1_ref[...], heads)
     _, doc2 = aux_parts(aux2_ref[...], heads)
     gain = jnp.exp(last(lam1)) * same(last(doc1), last(doc2))
-    exit_w = thirds(jnp.exp(last(lam) - lam) * same(docs, last(docs)))
     entry = jnp.exp(lam) * same(docs, last(doc1))
     parts = [p.astype(F32) for p in split3(entry)] + [jnp.zeros_like(entry)]
     entry_ref[...] = jnp.concatenate(parts, axis=1).astype(BF16)
     entry = thirds(entry * gain)
-    take = jnp.where(iota((tokens, half), 0) == iota((tokens, half), 1) + half, 1.0, 0.0)
-    sums = dot(write_ref[...], read2_ref[:half], NT)
-    take_ref[...] = choose(tail_is_long(docs), sums, take).astype(BF16)
-    ahead_score = dot(read2_ref[:half], write_ref[...], NT).astype(BF16)
-    behind_score = dot(write2_ref[half:], read_ref[...], NT).astype(BF16)
-    ahead_sums = tail_is_long(docs)
-    behind_rows = tail_is_long(doc2)
+    long_ref[...] = jnp.broadcast_to(jnp.where(tail_is_long(docs), 1.0, 0.0), long_ref.shape)
+    score = dot(write2_ref[half:], read_ref[...], NT).astype(BF16)
+    send_rows = tail_is_long(doc2)
     step = min(cols // 2, 512)
     for low in range(0, cols, step):
         at = slice(low, low + step)
         to_cols = spread(heads, head_width, low, step)
-        x = (x_ref[:, at].astype(F32) * dot(exit_w, to_cols)).astype(BF16)
-        sums = dot(ahead_score, x)
-        ahead_ref[:, at] = choose(ahead_sums, sums, x[half:].astype(F32)).astype(BF16)
         cot = (cot_ref[:, at].astype(F32) * dot(entry, to_cols)).astype(BF16)
-        sums = dot(behind_score, cot)
         row = low // (cols // 2) * half
         col = low % (cols // 2)
         behind_ref[row : row + half, col : col + step] = choose(
-            behind_rows, cot[:half].astype(F32), sums
+            send_rows, cot[:half].astype(F32), dot(score, cot)
         ).astype(BF16)
 
 
@@ -309,7 +298,6 @@
     read_ref,
     write1_ref,
     write2_ref,
-    aux2_ref,
     odd_ref,
     first_ref,
     then_ref,
@@ -317,24 +305,21 @@
     mixed_ref,
     entry_ref,
     exit1_ref,
-    gain_ref,
+    exit2_ref,
     out_ref,
     held_ref,
     sems,
 ):
-    tokens, cols = first_ref.shape
-    half = tokens // 2
+    cols = first_ref.shape[1]
     odd = odd_ref[0, 0] == 1
-    _, doc2 = aux_parts(aux2_ref[...], aux2_ref.shape[1] // 4)
     score1 = dot(read_ref[...], write1_ref[...], NT).astype(BF16)
-    take = jnp.where(iota((tokens, half), 0) == iota((tokens, half), 1), 1.0, 0.0)
-    score2 = dot(read_ref[...], write2_ref[half:], NT)
-    score2 = choose(tail_is_long(doc2), take, score2).astype(BF16)
+    score2 = dot(read_ref[...], write2_ref[...], NT).astype(BF16)
 
     def columns_of(low, at):
         x1 = jnp.where(odd, first_ref[:, at], then_ref[:, at])
         x1 = (x1.astype(F32) * exit1_ref[:, at]).astype(BF16)
-        carried = dot(score2, x2_ref[:, at]) * gain_ref[:1, at] + dot(score1, x1)
+        x2 = (x2_ref[:, at].astype(F32) * exit2_ref[:, at]).astype(BF16)
+        carried = dot(score2, x2) + dot(score1, x1)
         return (mixed_ref[:, at] + carried * entry_ref[:, at]).astype(BF16)
 
     in_steps(cols, step, out_ref, held_ref, sems, columns_of)
@@ -345,7 +330,7 @@
     head_width,
     step,
     write_ref,
-    take_ref,
+    long_ref,
     r1_ref,
     r2_ref,
     own_ref,
@@ -358,14 +343,17 @@
     grad_key_ref,
     grad_value_ref,
 ):
-    cols = first_ref.shape[1]
+    tokens, cols = first_ref.shape
     state = write_ref.shape[1]
-    half = take_ref.shape[1]
+    half = tokens // 2
     odd = odd_ref[0, 0] == 1
     width = HEAD_CHANNELS
     kv2 = own_ref.shape[1]
     score1 = dot(write_ref[...], r1_ref[:, kv2 : kv2 + state], NT).astype(BF16)
     entry1 = r1_ref[:, kv2 + state : kv2 + state + 3 * heads]
+    sums = dot(write_ref[...], r2_ref[:half, kv2 + cols // 2 :], NT)
+    take = jnp.where(iota((tokens, half), 0) == iota((tokens, half), 1) + half, 1.0, 0.0)
+    score2 = choose(long_ref[:1, :1] > 0.5, sums, take).astype(BF16)
     total = own_ref[...] + r1_ref[:, :kv2].astype(F32) + r2_ref[:, :kv2].astype(F32)
     for g in range(kv2 // (2 * width)):
         at = slice(g * width, (g + 1) * width)
@@ -380,7 +368,7 @@
         row = low // (cols // 2) * half
         col = kv2 + low % (cols // 2)
         far = r2_ref[row : row + half, col : col + step]
-        returned = dot(score1, c1) + dot(take_ref[...], far)
+        returned = dot(score1, c1) + dot(score2, far)
         return (grad_ref[:, at] + returned * exit_ref[:, at]).astype(BF16)
 
     for low in range(0, cols, step):
@@ -428,7 +416,6 @@
     params = pltpu.CompilerParams(vmem_limit_bytes=VMEM_LIMIT)
 
     odd = lax.axis_index("ctx") % 2
-    read2 = passed_along(state_read, "ctx", -2)
     m0 = pl.pallas_call(
         pack_kernel,
         out_shape=shape((tokens, m_cols), BF16),
@@ -437,15 +424,14 @@
     )(key_head_matrix, value_head_matrix, state_write, decay_t, doc_row)
     m1 = passed_along(m0, "ctx", 1)
     m2 = passed_along(m0, "ctx", 2)
-    x0, cot0, read2 = lax.optimization_barrier((ssm_input, cot_mixer, read2))
-    first_sent = jnp.where(odd == 0, x0, cot0)
-    then_sent = jnp.where(odd == 0, cot0, x0)
+    first_sent = jnp.where(odd == 0, ssm_input, cot_mixer)
+    then_sent = jnp.where(odd == 0, cot_mixer, ssm_input)
     odd = odd.reshape(1, 1)
     first = exchanged(first_sent, "ctx", 0)
     then = exchanged(then_sent, "ctx", 1)
-    decay_local, m1, m2, read2 = lax.optimization_barrier((decay_t, m1, m2, read2))
+    decay_local, m1, m2 = lax.optimization_barrier((decay_t, m1, m2))
     write_at = 2 * kv
-    mixed, grad, entry_w, exit_w, exit1_w, gain_w = pl.pallas_call(
+    mixed, grad, entry_w, exit_w, exit1_w, exit2_w = pl.pallas_call(
         functools.partial(local_kernel, heads, head_width),
         grid=(steps,),
         in_specs=[
@@ -458,43 +444,33 @@
             columns(tokens, step_cols),
             columns(tokens, step_cols),
         ],
-        out_specs=[columns(tokens, step_cols)] * 5 + [columns(8, step_cols)],
-        out_shape=(shape(ssm_input.shape, F32),) * 5 + (shape((8, cols), F32),),
+        out_specs=[columns(tokens, step_cols)] * 6,
+        out_shape=(shape(ssm_input.shape, F32),) * 6,
         compiler_params=params,
         name="local_mixer",
     )(doc_row, state_write, state_read, decay_local, m1, m2, ssm_input, cot_mixer)
 
-    ahead, behind, entry_parts, take2 = pl.pallas_call(
+    behind, entry_parts, long_tail = pl.pallas_call(
         functools.partial(far_kernel, head_width),
         grid=(1,),
         in_specs=[
             whole((heads, tokens)),
             whole((1, tokens)),
             whole((tokens, state)),
-            whole((tokens, state)),
-            whole((tokens, state)),
             part(tokens, aux, write_at + state),
             part(tokens, state, write_at),
             part(tokens, aux, write_at + state),
             whole((tokens, cols)),
-            whole((tokens, cols)),
         ],
-        out_specs=[
-            whole((tokens // 2, cols)),
-            whole((tokens, cols // 2)),
-            whole((tokens, aux)),
-            whole((tokens, tokens // 2)),
-        ],
+        out_specs=[whole((tokens, cols // 2)), whole((tokens, aux)), whole((8, 128))],
         out_shape=(
-            shape((tokens // 2, cols), BF16),
             shape((tokens, cols // 2), BF16),
             shape((tokens, aux), BF16),
-            shape((tokens, tokens // 2), BF16),
+            shape((8, 128), F32),
         ),
         compiler_params=params,
         name="far",
-    )(decay_t, doc_row, state_read, state_write, read2, m1, m2, m2, ssm_input, cot_mixer)
-    x2 = passed_along(ahead, "ctx", 2)
+    )(decay_t, doc_row, state_read, m1, m2, m2, cot_mixer)
     attention_out, own, back1, back2 = pl.pallas_call(
         functools.partial(attn_kernel, kv, 2 * kv + state + 3 * heads),
         grid=(kv_local,),
@@ -506,19 +482,21 @@
             columns(tokens, group_cols),
             whole((tokens, 2 * kv)),
             whole((tokens, m_cols)),
-            whole((tokens, 2 * kv + cols // 2)),
+            whole((tokens, 2 * kv + cols // 2 + state)),
         ],
         out_shape=(
             shape(query_head_matrix.shape, BF16),
             shape((tokens, 2 * kv), F32),
             shape((tokens, m_cols), BF16),
-            shape((tokens, 2 * kv + cols // 2), BF16),
+            shape((tokens, 2 * kv + cols // 2 + state), BF16),
         ),
         compiler_params=params,
         name="attention",
     )(doc_row, state_read, m0, m1, m2, query_head_matrix, attention_output_gradient, behind, entry_parts)
     r1 = passed_along(back1, "ctx", -1)
     r2 = passed_along(back2, "ctx", -2)
+    x0, behind = lax.optimization_barrier((ssm_input, behind))
+    x2 = passed_along(x0, "ctx", 2)
 
 
     smem = pl.BlockSpec(memory_space=pltpu.SMEM)
@@ -534,20 +512,15 @@
             whole((tokens, state)),
             part(tokens, state, write_at),
             part(tokens, state, write_at),
-            part(tokens, aux, write_at + state),
             smem,
-            whole((tokens, cols)),
-            whole((tokens, cols)),
-            whole((tokens // 2, cols)),
         ]
-        + [whole((tokens, cols))] * 3
-        + [whole((8, cols))],
+        + [whole((tokens, cols))] * 7,
         out_specs=pl.BlockSpec(memory_space=pl.ANY),
         out_shape=shape(ssm_input.shape, BF16),
         scratch_shapes=held,
         compiler_params=params,
         name="carried",
-    )(state_read, m1, m2, m2, odd, first, then, x2, mixed, entry_w, exit1_w, gain_w)
+    )(state_read, m1, m2, odd, first, then, x2, mixed, entry_w, exit1_w, exit2_w)
 
     own, mixer_out = lax.optimization_barrier((own, mixer_out))
     grad_input, grad_key, grad_value = pl.pallas_call(
@@ -555,9 +528,9 @@
         grid=(1,),
         in_specs=[
             whole((tokens, state)),
-            whole((tokens, tokens // 2)),
+            whole((8, 128)),
             whole((tokens, m_cols)),
-            whole((tokens, 2 * kv + cols // 2)),
+            whole((tokens, 2 * kv + cols // 2 + state)),
             whole((tokens, 2 * kv)),
             smem,
         ]
@@ -570,7 +543,7 @@
         ),
         compiler_params=params,
         name="returned",
-    )(state_write, take2, r1, r2, own, odd, first, then, grad, exit_w)
+    )(state_write, long_tail, r1, r2, own, odd, first, then, grad, exit_w)
     return (attention_out, mixer_out, grad_key, grad_value, grad_input)
 
 

time: 44.1 us -> 42.6 us (0.966)
  starting transfers between devices: 21 us -> 18.4 us
  waiting for transfers between devices: 7.04 us -> 8.4 us
    ppermute x6 -> x5, starting transfers between devices: 17.3 us -> 14.8 us  [passed_along(): return lax.ppermute(block, axis, route)]
    ppermute x6 -> x5, waiting for transfers between devices: 2.75 us -> 4.46 us  [passed_along(): return lax.ppermute(block, axis, route)]
    pallas_call x1, Pallas kernels: 1.78 us -> 1.1 us  [shards(): pl.pallas_call(functools.partial(far_kernel, head_width), grid=(1,), in_s...]
  transfers between devices with their start and end apart: 8 -> 7, of which waited for: 4 -> 4; matrix products, arithmetic and copies ran while one was open for 3% -> 3% of each run, Pallas kernels for 27% -> 23%
where the time goes in v5:
time: 42.6 us; the launch traced here: 42.3 us
  starting transfers between devices  18.4 us (43%)
  Pallas kernels  13.2 us (31%)
  waiting for transfers between devices  8.4 us (20%)
  other arithmetic  1.34 us (3%)
  between operations  0.82 us (2%)
    ppermute x5, starting transfers between devices, passed_along(): return lax.ppermute(block, axis, route)  14.8 us
    ppermute x5, waiting for transfers between devices, passed_along(): return lax.ppermute(block, axis, route)  4.46 us
    pallas_call x1, Pallas kernels, shards(): pl.pallas_call(functools.partial(local_kernel, heads, head_width), grid=(...  3.98 us
    ppermute x2, waiting for transfers between devices, exchanged(): return lax.ppermute(block, axis, route)  3.94 us
    ppermute x2, starting transfers between devices, exchanged(): return lax.ppermute(block, axis, route)  3.64 us
    pallas_call x1, Pallas kernels, shards(): pl.pallas_call(functools.partial(attn_kernel, kv, 2 * kv + state + 3 * he...  3.24 us
    pallas_call x1, Pallas kernels, shards(): pl.pallas_call(pack_kernel, out_shape=shape((tokens, m_cols), BF16), comp...  1.83 us
    pallas_call x1, Pallas kernels, shards(): pl.pallas_call(functools.partial(returned_kernel, heads, head_width, half...  1.78 us
  transfers between devices with their start and end apart: 7, of which 4 were waited for; matrix products, arithmetic and copies ran while one was open for 3% of the time, Pallas kernels for 23%

profile of v5, /device:TPU:14, one launch (start us, length us, event | category | flops | bytes accessed | tf_op | source)
XLA Modules:
  0.0 42.3 jit_solution(9911113090088667097)
XLA Ops:
  0.6 1.8 %pack.1.m0 = bf16[128,768]{1,0:T(8,128)(2,1)} custom-call(bf16[128,256]{1,0:T(8,128)(2,1)} %key_ref.1, bf16[128,256]{1,0:T(8,128)(2,1)} %value_ref.1, bf16[128,128]{1,0:T(8,128)(2,1)} %write_ref.5, f32[32,128]{1,0:T(8,128)} %bitcast.3, s32[1,128]{1,0:T(1,128)} %bitcast.6), custom_call_target="tpu_custom_call" | custom-call | tf_op jit(solution)/shard_map/pack/pallas_call | solution.py:419
  2.5 3.4 %collective-permute-start = (bf16[128,768]{1,0:T(8,128)(2,1)}, bf16[128,768]{1,0:T(8,128)(2,1)S(1)}, u32[]{:S(2)}, u32[]{:S(2)}) collective-permute-start(bf16[128,768]{1,0:T(8,128)(2,1)} %pack.1.m0), channel_id=1, source_target_pairs={{0,4},{4,8},{8,12},{12,16},{16,20},{20,24},{24,28},{1,5},{5,9},{9,... | collective-permute-start | bytes 589832 | tf_op jit(solution)/shard_map/ppermute | solution.py:23
  5.9 3.5 %collective-permute-start.1 = (bf16[128,768]{1,0:T(8,128)(2,1)}, bf16[128,768]{1,0:T(8,128)(2,1)S(1)}, u32[]{:S(2)}, u32[]{:S(2)}) collective-permute-start(bf16[128,768]{1,0:T(8,128)(2,1)} %pack.1.m0), channel_id=1, source_target_pairs={{0,8},{4,12},{8,16},{12,20},{16,24},{20,28},{1,9},{5,13},{9,17},{1... | collective-permute-start | bytes 589832 | tf_op jit(solution)/shard_map/ppermute | solution.py:23
  9.4 0.0 copy-start
  9.4 0.0 copy-start.3
  9.4 0.0 copy-start.7
  9.5 0.0 copy-start.6
  9.5 1.3 %broadcast_select_fusion = (bf16[128,2048]{1,0:T(8,128)(2,1)S(1)}, bf16[128,2048]{1,0:T(8,128)(2,1)S(1)}) fusion(bf16[128,2048]{1,0:T(8,128)(2,1)} %cot_ref.5, bf16[128,2048]{1,0:T(8,128)(2,1)} %x_ref.1, pred[]{:T(512)S(6)} %eq.6), kind=kLoop, calls=%fused_computation | loop fusion | flops 524288 | bytes 2097153 | tf_op jit(solution)/shard_map/jit(_where)/select_n | solution.py:428
  10.8 0.0 copy-start.8
  10.8 0.5 %collective-permute-start.2 = (bf16[128,2048]{1,0:T(8,128)(2,1)S(1)}, bf16[128,2048]{1,0:T(8,128)(2,1)S(1)}, u32[]{:S(2)}, u32[]{:S(2)}) collective-permute-start(bf16[128,2048]{1,0:T(8,128)(2,1)S(1)} %get-tuple-element.50), channel_id=1, source_target_pairs={{0,4},{4,0},{8,12},{12,8},{16,20},{20,16},{24,28},{28,24},{1,5},{5... | collective-permute-start | bytes 1572872 | tf_op jit(solution)/shard_map/ppermute | solution.py:31
  11.4 0.0 copy-start.1
  11.4 0.0 copy-start.2
  11.4 0.0 copy-start.5
  11.4 3.1 %collective-permute-start.3 = (bf16[128,2048]{1,0:T(8,128)(2,1)S(1)}, bf16[128,2048]{1,0:T(8,128)(2,1)S(1)}, u32[]{:S(2)}, u32[]{:S(2)}) collective-permute-start(bf16[128,2048]{1,0:T(8,128)(2,1)S(1)} %get-tuple-element.49), channel_id=1, source_target_pairs={{4,8},{8,4},{12,16},{16,12},{20,24},{24,20},{5,9},{9,5},{13,17},{1... | collective-permute-start | bytes 1572872 | tf_op jit(solution)/shard_map/ppermute | solution.py:31
  14.5 0.0 collective-permute-done.aux1_ref.m1.write1_ref
  14.5 0.9 %collective-permute-done.1.write2_ref.aux2_ref.m2 = bf16[128,768]{1,0:T(8,128)(2,1)S(1)} collective-permute-done((bf16[128,768]{1,0:T(8,128)(2,1)}, bf16[128,768]{1,0:T(8,128)(2,1)S(1)}, u32[]{:S(2)}, u32[]{:S(2)}) %collective-permute-start.1) | collective-permute-done | bytes 196640 | tf_op jit(solution)/shard_map/ppermute | solution.py:23
  15.4 0.0 copy-done
  15.4 0.0 copy-done.3
  15.4 0.0 copy-done.7
  15.4 0.0 copy-done.8
  15.4 1.1 %far.1 = (bf16[128,1024]{1,0:T(8,128)(2,1)S(1)}, bf16[128,128]{1,0:T(8,128)(2,1)S(1)}, f32[8,128]{1,0:T(8,128)S(1)}) custom-call(f32[32,128]{1,0:T(8,128)S(1)} %bitcast.4, s32[1,128]{1,0:T(1,128)S(1)} %bitcast.7, bf16[128,128]{1,0:T(8,128)(2,1)S(1)} %copy-done.3, bf16[128,768]{1,0:T(8,128)(2,1)S(1)} %collective-permute-done.aux1_ref.m1.write1_ref, ...), custom_call_target="tpu_custom_call" | custom-call | tf_op jit(solution)/shard_map/far/pallas_call | solution.py:453
  16.5 0.0 copy-done.1
  16.5 4.1 %collective-permute-start.4 = (bf16[128,2048]{1,0:T(8,128)(2,1)S(1)}, bf16[128,2048]{1,0:T(8,128)(2,1)S(1)}, u32[]{:S(2)}, u32[]{:S(2)}) collective-permute-start(bf16[128,2048]{1,0:T(8,128)(2,1)S(1)} %copy-done.1), channel_id=1, source_target_pairs={{0,8},{4,12},{8,16},{12,20},{16,24},{20,28},{1,9},{5,13},{9,17},{1... | collective-permute-start | bytes 1572872 | tf_op jit(solution)/shard_map/ppermute | solution.py:23
  20.6 0.0 copy-done.6
  20.6 0.0 copy-done.2
  20.6 0.0 copy-done.5
  20.6 0.0 copy-start.4
  20.6 3.2 %attention.1 = (bf16[128,1024]{1,0:T(8,128)(2,1)}, f32[128,512]{1,0:T(8,128)S(1)}, bf16[128,768]{1,0:T(8,128)(2,1)S(1)}, bf16[128,1664]{1,0:T(8,128)(2,1)S(1)}) custom-call(s32[1,128]{1,0:T(1,128)S(1)} %bitcast.8, bf16[128,128]{1,0:T(8,128)(2,1)S(1)} %copy-done.3, bf16[128,768]{1,0:T(8,128)(2,1)S(1)} %copy-done.2, ...), custom_call_target="tpu_custom_call" | custom-call | tf_op jit(solution)/shard_map/attention/pallas_call | solution.py:474
  23.8 1.9 %collective-permute-start.6 = (bf16[128,1664]{1,0:T(8,128)(2,1)S(1)}, bf16[128,1664]{1,0:T(8,128)(2,1)S(1)}, u32[]{:S(2)}, u32[]{:S(2)}) collective-permute-start(bf16[128,1664]{1,0:T(8,128)(2,1)S(1)} %get-tuple-element.42), channel_id=1, source_target_pairs={{8,0},{12,4},{16,8},{20,12},{24,16},{28,20},{9,1},{13,5},{17,9},{2... | collective-permute-start | bytes 1277960 | tf_op jit(solution)/shard_map/ppermute | solution.py:23
  25.8 1.9 %collective-permute-start.5 = (bf16[128,768]{1,0:T(8,128)(2,1)S(1)}, bf16[128,768]{1,0:T(8,128)(2,1)S(1)}, u32[]{:S(2)}, u32[]{:S(2)}) collective-permute-start(bf16[128,768]{1,0:T(8,128)(2,1)S(1)} %get-tuple-element.41), channel_id=1, source_target_pairs={{4,0},{8,4},{12,8},{16,12},{20,16},{24,20},{28,24},{5,1},{9,5},{13... | collective-permute-start | bytes 589832 | tf_op jit(solution)/shard_map/ppermute | solution.py:23
  27.7 0.0 copy-done.4
  27.7 4.0 %local_mixer.1 = (f32[128,2048]{1,0:T(8,128)S(1)}, f32[128,2048]{1,0:T(8,128)S(1)}, f32[128,2048]{1,0:T(8,128)S(1)}, f32[128,2048]{1,0:T(8,128)S(1)}, f32[128,2048]{1,0:T(8,128)S(1)}, /*index=5*/f32[128,2048]{1,0:T(8,128)S(1)}) custom-call(s32[1,128]{1,0:T(1,128)S(1)} %bitcast.9, bf16[128,128]{1,0:T(8,128)(2,1)S(1)} %copy-done.4, ...), custom_call_target="tpu_custom_call" | custom-call | tf_op jit(solution)/shard_map/local_mixer/pallas_call | solution.py:434
  31.7 3.9 %collective-permute-done.2.first_ref = bf16[128,2048]{1,0:T(8,128)(2,1)S(1)} collective-permute-done((bf16[128,2048]{1,0:T(8,128)(2,1)S(1)}, bf16[128,2048]{1,0:T(8,128)(2,1)S(1)}, u32[]{:S(2)}, u32[]{:S(2)}) %collective-permute-start.2) | collective-permute-done | bytes 524320 | tf_op jit(solution)/shard_map/ppermute | solution.py:31
  35.6 0.0 collective-permute-done.3.then_ref
  35.6 2.8 %collective-permute-done.4.x2_ref = bf16[128,2048]{1,0:T(8,128)(2,1)S(1)} collective-permute-done((bf16[128,2048]{1,0:T(8,128)(2,1)S(1)}, bf16[128,2048]{1,0:T(8,128)(2,1)S(1)}, u32[]{:S(2)}, u32[]{:S(2)}) %collective-permute-start.4) | collective-permute-done | bytes 524320 | tf_op jit(solution)/shard_map/ppermute | solution.py:23
  38.5 1.3 %carried.1 = bf16[128,2048]{1,0:T(8,128)(2,1)} custom-call(bf16[128,128]{1,0:T(8,128)(2,1)S(1)} %copy-done.3, bf16[128,768]{1,0:T(8,128)(2,1)S(1)} %collective-permute-done.aux1_ref.m1.write1_ref, bf16[128,768]{1,0:T(8,128)(2,1)S(1)} %collective-permute-done.1.write2_ref.aux2_ref.m2, s32[1,1]{1,0:T(1,128)} %bitcast.2.odd_ref, ...), custom_call_target="tpu_custom_call" | custom-call | tf_op jit(solution)/shard_map/carried/pallas_call | solution.py:508
  39.8 0.7 %collective-permute-done.5.r1_ref = bf16[128,768]{1,0:T(8,128)(2,1)S(1)} collective-permute-done((bf16[128,768]{1,0:T(8,128)(2,1)S(1)}, bf16[128,768]{1,0:T(8,128)(2,1)S(1)}, u32[]{:S(2)}, u32[]{:S(2)}) %collective-permute-start.5) | collective-permute-done | bytes 196640 | tf_op jit(solution)/shard_map/ppermute | solution.py:23
  40.5 0.0 collective-permute-done.6.r2_ref
  40.5 1.8 %returned.1 = (bf16[128,2048]{1,0:T(8,128)(2,1)}, bf16[128,256]{1,0:T(8,128)(2,1)}, bf16[128,256]{1,0:T(8,128)(2,1)}) custom-call(bf16[128,128]{1,0:T(8,128)(2,1)S(1)} %copy-done.4, f32[8,128]{1,0:T(8,128)S(1)} %get-tuple-element.40.long_ref, bf16[128,768]{1,0:T(8,128)(2,1)S(1)} %collective-permute-done.5.r1_ref, ...), custom_call_target="tpu_custom_call" | custom-call | tf_op jit(solution)/shard_map/returned/pallas_call | solution.py:526
Async XLA Ops:
  2.5 12.0 %collective-permute-start = (bf16[128,768]{1,0:T(8,128)(2,1)}, bf16[128,768]{1,0:T(8,128)(2,1)S(1)}, u32[]{:S(2)}, u32[]{:S(2)}) collective-permute-start(bf16[128,768]{1,0:T(8,128)(2,1)} %pack.1.m0), channel_id=1, source_target_pairs={{0,4},{4,8},{8,12},{12,16},{16,20},{20,24},{24,28},{1,5},{5,9},{9,... | collective-permute-start | bytes 589832 | tf_op jit(solution)/shard_map/ppermute | solution.py:23
  5.9 9.5 %collective-permute-start.1 = (bf16[128,768]{1,0:T(8,128)(2,1)}, bf16[128,768]{1,0:T(8,128)(2,1)S(1)}, u32[]{:S(2)}, u32[]{:S(2)}) collective-permute-start(bf16[128,768]{1,0:T(8,128)(2,1)} %pack.1.m0), channel_id=1, source_target_pairs={{0,8},{4,12},{8,16},{12,20},{16,24},{20,28},{1,9},{5,13},{9,17},{1... | collective-permute-start | bytes 589832 | tf_op jit(solution)/shard_map/ppermute | solution.py:23
  9.4 6.0 %copy-start = (bf16[128,2048]{1,0:T(8,128)(2,1)S(1)}, bf16[128,2048]{1,0:T(8,128)(2,1)}, u32[]{:S(2)}) copy-start(bf16[128,2048]{1,0:T(8,128)(2,1)} %cot_ref.5) | copy-start | bytes 1572868
  9.4 6.0 %copy-start.3 = (bf16[128,128]{1,0:T(8,128)(2,1)S(1)}, bf16[128,128]{1,0:T(8,128)(2,1)}, u32[]{:S(2)}) copy-start(bf16[128,128]{1,0:T(8,128)(2,1)} %read_ref.7) | copy-start | bytes 98308
  9.4 5.9 %copy-start.7 = (f32[128,32]{0,1:T(8,128)S(1)}, f32[128,32]{0,1:T(8,128)}, u32[]{:S(2)}) copy-start(f32[128,32]{0,1:T(8,128)} %param.14) | copy-start | bytes 49156
  9.5 11.1 %copy-start.6 = (bf16[128,1024]{1,0:T(8,128)(2,1)S(1)}, bf16[128,1024]{1,0:T(8,128)(2,1)}, u32[]{:S(2)}) copy-start(bf16[128,1024]{1,0:T(8,128)(2,1)} %cot_ref.4) | copy-start | bytes 786436
  10.8 4.6 %copy-start.8 = (s32[128]{0:T(128)S(1)}, s32[128]{0:T(128)}, u32[]{:S(2)}) copy-start(s32[128]{0:T(128)} %param.17) | copy-start | bytes 1540
  10.8 24.8 %collective-permute-start.2 = (bf16[128,2048]{1,0:T(8,128)(2,1)S(1)}, bf16[128,2048]{1,0:T(8,128)(2,1)S(1)}, u32[]{:S(2)}, u32[]{:S(2)}) collective-permute-start(bf16[128,2048]{1,0:T(8,128)(2,1)S(1)} %get-tuple-element.50), channel_id=1, source_target_pairs={{0,4},{4,0},{8,12},{12,8},{16,20},{20,16},{24,28},{28,24},{1,5},{5... | collective-permute-start | bytes 1572872 | tf_op jit(solution)/shard_map/ppermute | solution.py:31
  11.4 5.1 %copy-start.1 = (bf16[128,2048]{1,0:T(8,128)(2,1)S(1)}, bf16[128,2048]{1,0:T(8,128)(2,1)}, u32[]{:S(2)}) copy-start(bf16[128,2048]{1,0:T(8,128)(2,1)} %x_ref.1) | copy-start | bytes 1572868
  11.4 9.2 %copy-start.2 = (bf16[128,768]{1,0:T(8,128)(2,1)S(1)}, bf16[128,768]{1,0:T(8,128)(2,1)}, u32[]{:S(2)}) copy-start(bf16[128,768]{1,0:T(8,128)(2,1)} %pack.1.m0) | copy-start | bytes 589828
  11.4 9.2 %copy-start.5 = (bf16[128,1024]{1,0:T(8,128)(2,1)S(1)}, bf16[128,1024]{1,0:T(8,128)(2,1)}, u32[]{:S(2)}) copy-start(bf16[128,1024]{1,0:T(8,128)(2,1)} %q_ref.1) | copy-start | bytes 786436
  11.4 24.3 %collective-permute-start.3 = (bf16[128,2048]{1,0:T(8,128)(2,1)S(1)}, bf16[128,2048]{1,0:T(8,128)(2,1)S(1)}, u32[]{:S(2)}, u32[]{:S(2)}) collective-permute-start(bf16[128,2048]{1,0:T(8,128)(2,1)S(1)} %get-tuple-element.49), channel_id=1, source_target_pairs={{4,8},{8,4},{12,16},{16,12},{20,24},{24,20},{5,9},{9,5},{13,17},{1... | collective-permute-start | bytes 1572872 | tf_op jit(solution)/shard_map/ppermute | solution.py:31
  16.5 22.0 %collective-permute-start.4 = (bf16[128,2048]{1,0:T(8,128)(2,1)S(1)}, bf16[128,2048]{1,0:T(8,128)(2,1)S(1)}, u32[]{:S(2)}, u32[]{:S(2)}) collective-permute-start(bf16[128,2048]{1,0:T(8,128)(2,1)S(1)} %copy-done.1), channel_id=1, source_target_pairs={{0,8},{4,12},{8,16},{12,20},{16,24},{20,28},{1,9},{5,13},{9,17},{1... | collective-permute-start | bytes 1572872 | tf_op jit(solution)/shard_map/ppermute | solution.py:23
  20.6 7.1 %copy-start.4 = (bf16[128,128]{1,0:T(8,128)(2,1)S(1)}, bf16[128,128]{1,0:T(8,128)(2,1)}, u32[]{:S(2)}) copy-start(bf16[128,128]{1,0:T(8,128)(2,1)} %write_ref.5) | copy-start | bytes 98308
  23.8 16.6 %collective-permute-start.6 = (bf16[128,1664]{1,0:T(8,128)(2,1)S(1)}, bf16[128,1664]{1,0:T(8,128)(2,1)S(1)}, u32[]{:S(2)}, u32[]{:S(2)}) collective-permute-start(bf16[128,1664]{1,0:T(8,128)(2,1)S(1)} %get-tuple-element.42), channel_id=1, source_target_pairs={{8,0},{12,4},{16,8},{20,12},{24,16},{28,20},{9,1},{13,5},{17,9},{2... | collective-permute-start | bytes 1277960 | tf_op jit(solution)/shard_map/ppermute | solution.py:23
  25.8 14.7 %collective-permute-start.5 = (bf16[128,768]{1,0:T(8,128)(2,1)S(1)}, bf16[128,768]{1,0:T(8,128)(2,1)S(1)}, u32[]{:S(2)}, u32[]{:S(2)}) collective-permute-start(bf16[128,768]{1,0:T(8,128)(2,1)S(1)} %get-tuple-element.41), channel_id=1, source_target_pairs={{4,0},{8,4},{12,8},{16,12},{20,16},{24,20},{28,24},{5,1},{9,5},{13... | collective-permute-start | bytes 589832 | tf_op jit(solution)/shard_map/ppermute | solution.py:23

commit v6 on v5

--- a/solution.py
+++ b/solution.py
@@ -174,6 +174,7 @@
     exit_ref,
     exit1_ref,
     exit2_ref,
+    spread_ref,
 ):
     tokens, cols = x_ref.shape
     step_heads = cols // head_width
@@ -197,6 +198,7 @@
     gain = jnp.exp(last(lam1)) * same(last(doc1), last(doc2))
     exit2 = jnp.exp(last(lam2) - lam2) * same(doc2, last(doc2)) * gain
     to_cols = spread(heads, head_width, pl.program_id(0) * cols, cols)
+    spread_ref[...] = to_cols
     exit1_ref[...] = dot(thirds(exit1), to_cols)
     exit2_ref[...] = dot(thirds(exit2), to_cols)
     per = HEAD_CHANNELS // head_width
@@ -280,19 +282,6 @@
         ).astype(BF16)
 
 
-def in_steps(cols, step, out_ref, held_ref, sems, columns_of):
-    copies = []
-    for place, low in enumerate(range(0, cols, step)):
-        at = slice(low, low + step)
-        held_ref[:, at] = columns_of(low, at)
-        copies.append(
-            pltpu.make_async_copy(held_ref.at[:, at], out_ref.at[:, at], sems.at[place])
-        )
-        copies[-1].start()
-    for copy in copies:
-        copy.wait()
-
-
 def carried_kernel(
     step,
     read_ref,
@@ -307,8 +296,6 @@
     exit1_ref,
     exit2_ref,
     out_ref,
-    held_ref,
-    sems,
 ):
     cols = first_ref.shape[1]
     odd = odd_ref[0, 0] == 1
@@ -322,7 +309,9 @@
         carried = dot(score2, x2) + dot(score1, x1)
         return (mixed_ref[:, at] + carried * entry_ref[:, at]).astype(BF16)
 
-    in_steps(cols, step, out_ref, held_ref, sems, columns_of)
+    for low in range(0, cols, step):
+        at = slice(low, low + step)
+        out_ref[:, at] = columns_of(low, at)
 
 
 def returned_kernel(
@@ -339,6 +328,7 @@
     then_ref,
     grad_ref,
     exit_ref,
+    spread_ref,
     out_ref,
     grad_key_ref,
     grad_value_ref,
@@ -363,7 +353,7 @@
 
     def columns_of(low, at):
         c1 = jnp.where(odd, then_ref[:, at], first_ref[:, at])
-        entry = dot(entry1, spread(heads, head_width, low, step))
+        entry = dot(entry1, spread_ref[:, at])
         c1 = (c1.astype(F32) * entry).astype(BF16)
         row = low // (cols // 2) * half
         col = kv2 + low % (cols // 2)
@@ -431,7 +421,7 @@
     then = exchanged(then_sent, "ctx", 1)
     decay_local, m1, m2 = lax.optimization_barrier((decay_t, m1, m2))
     write_at = 2 * kv
-    mixed, grad, entry_w, exit_w, exit1_w, exit2_w = pl.pallas_call(
+    mixed, grad, entry_w, exit_w, exit1_w, exit2_w, to_cols = pl.pallas_call(
         functools.partial(local_kernel, heads, head_width),
         grid=(steps,),
         in_specs=[
@@ -444,8 +434,8 @@
             columns(tokens, step_cols),
             columns(tokens, step_cols),
         ],
-        out_specs=[columns(tokens, step_cols)] * 6,
-        out_shape=(shape(ssm_input.shape, F32),) * 6,
+        out_specs=[columns(tokens, step_cols)] * 6 + [columns(3 * heads, step_cols)],
+        out_shape=(shape(ssm_input.shape, F32),) * 6 + (shape((3 * heads, cols), BF16),),
         compiler_params=params,
         name="local_mixer",
     )(doc_row, state_write, state_read, decay_local, m1, m2, ssm_input, cot_mixer)
@@ -501,10 +491,6 @@
 
     smem = pl.BlockSpec(memory_space=pltpu.SMEM)
     half_step = min(step_cols, cols // 2)
-    held = [
-        pltpu.VMEM((tokens, cols), BF16),
-        pltpu.SemaphoreType.DMA((cols // half_step,)),
-    ]
     mixer_out = pl.pallas_call(
         functools.partial(carried_kernel, half_step),
         grid=(1,),
@@ -515,9 +501,8 @@
             smem,
         ]
         + [whole((tokens, cols))] * 7,
-        out_specs=pl.BlockSpec(memory_space=pl.ANY),
+        out_specs=whole((tokens, cols)),
         out_shape=shape(ssm_input.shape, BF16),
-        scratch_shapes=held,
         compiler_params=params,
         name="carried",
     )(state_read, m1, m2, odd, first, then, x2, mixed, entry_w, exit1_w, exit2_w)
@@ -534,7 +519,8 @@
             whole((tokens, 2 * kv)),
             smem,
         ]
-        + [whole((tokens, cols))] * 4,
+        + [whole((tokens, cols))] * 4
+        + [whole((3 * heads, cols))],
         out_specs=[whole((tokens, cols))] + [whole((tokens, kv))] * 2,
         out_shape=(
             shape(cot_mixer.shape, BF16),
@@ -543,7 +529,7 @@
         ),
         compiler_params=params,
         name="returned",
-    )(state_write, long_tail, r1, r2, own, odd, first, then, grad, exit_w)
+    )(state_write, long_tail, r1, r2, own, odd, first, then, grad, exit_w, to_cols)
     return (attention_out, mixer_out, grad_key, grad_value, grad_input)
 
 

time: 42.6 us -> 42.6 us (level)
  no operation moved by 1% of the time
where the time goes in v6:
time: 42.6 us; the launch traced here: 42.3 us
  starting transfers between devices  18.4 us (43%)
  Pallas kernels  13.4 us (31%)
  waiting for transfers between devices  8.2 us (19%)
  other arithmetic  1.34 us (3%)
  between operations  0.82 us (2%)
    ppermute x5, starting transfers between devices, passed_along(): return lax.ppermute(block, axis, route)  14.8 us
    ppermute x5, waiting for transfers between devices, passed_along(): return lax.ppermute(block, axis, route)  4.36 us
    pallas_call x1, Pallas kernels, shards(): pl.pallas_call(functools.partial(local_kernel, heads, head_width), grid=(...  4.08 us
    ppermute x2, waiting for transfers between devices, exchanged(): return lax.ppermute(block, axis, route)  3.84 us
    ppermute x2, starting transfers between devices, exchanged(): return lax.ppermute(block, axis, route)  3.64 us
    pallas_call x1, Pallas kernels, shards(): pl.pallas_call(functools.partial(attn_kernel, kv, 2 * kv + state + 3 * he...  3.24 us
    pallas_call x1, Pallas kernels, shards(): pl.pallas_call(pack_kernel, out_shape=shape((tokens, m_cols), BF16), comp...  1.83 us
    pallas_call x1, Pallas kernels, shards(): pl.pallas_call(functools.partial(returned_kernel, heads, head_width, half...  1.77 us
  transfers between devices with their start and end apart: 7, of which 4 were waited for; matrix products, arithmetic and copies ran while one was open for 3% of the time, Pallas kernels for 23%

profile of v6, /device:TPU:14, one launch (start us, length us, event | category | flops | bytes accessed | tf_op | source)
XLA Modules:
  0.0 42.3 jit_solution(16310285857627257252)
XLA Ops:
  0.6 1.8 %pack.1.m0 = bf16[128,768]{1,0:T(8,128)(2,1)} custom-call(bf16[128,256]{1,0:T(8,128)(2,1)} %key_ref.1, bf16[128,256]{1,0:T(8,128)(2,1)} %value_ref.1, bf16[128,128]{1,0:T(8,128)(2,1)} %write_ref.5, f32[32,128]{1,0:T(8,128)} %bitcast.3, s32[1,128]{1,0:T(1,128)} %bitcast.6), custom_call_target="tpu_custom_call" | custom-call | tf_op jit(solution)/shard_map/pack/pallas_call | solution.py:409
  2.5 3.4 %collective-permute-start = (bf16[128,768]{1,0:T(8,128)(2,1)}, bf16[128,768]{1,0:T(8,128)(2,1)S(1)}, u32[]{:S(2)}, u32[]{:S(2)}) collective-permute-start(bf16[128,768]{1,0:T(8,128)(2,1)} %pack.1.m0), channel_id=1, source_target_pairs={{0,4},{4,8},{8,12},{12,16},{16,20},{20,24},{24,28},{1,5},{5,9},{9,... | collective-permute-start | bytes 589832 | tf_op jit(solution)/shard_map/ppermute | solution.py:23
  5.9 3.5 %collective-permute-start.1 = (bf16[128,768]{1,0:T(8,128)(2,1)}, bf16[128,768]{1,0:T(8,128)(2,1)S(1)}, u32[]{:S(2)}, u32[]{:S(2)}) collective-permute-start(bf16[128,768]{1,0:T(8,128)(2,1)} %pack.1.m0), channel_id=1, source_target_pairs={{0,8},{4,12},{8,16},{12,20},{16,24},{20,28},{1,9},{5,13},{9,17},{1... | collective-permute-start | bytes 589832 | tf_op jit(solution)/shard_map/ppermute | solution.py:23
  9.4 0.0 copy-start
  9.4 0.0 copy-start.3
  9.4 0.0 copy-start.7
  9.5 0.0 copy-start.6
  9.5 1.3 %broadcast_select_fusion = (bf16[128,2048]{1,0:T(8,128)(2,1)S(1)}, bf16[128,2048]{1,0:T(8,128)(2,1)S(1)}) fusion(bf16[128,2048]{1,0:T(8,128)(2,1)} %cot_ref.5, bf16[128,2048]{1,0:T(8,128)(2,1)} %x_ref.1, pred[]{:T(512)S(6)} %eq.6), kind=kLoop, calls=%fused_computation | loop fusion | flops 524288 | bytes 2097153 | tf_op jit(solution)/shard_map/jit(_where)/select_n | solution.py:418
  10.8 0.0 copy-start.8
  10.8 0.5 %collective-permute-start.2 = (bf16[128,2048]{1,0:T(8,128)(2,1)S(1)}, bf16[128,2048]{1,0:T(8,128)(2,1)S(1)}, u32[]{:S(2)}, u32[]{:S(2)}) collective-permute-start(bf16[128,2048]{1,0:T(8,128)(2,1)S(1)} %get-tuple-element.52), channel_id=1, source_target_pairs={{0,4},{4,0},{8,12},{12,8},{16,20},{20,16},{24,28},{28,24},{1,5},{5... | collective-permute-start | bytes 1572872 | tf_op jit(solution)/shard_map/ppermute | solution.py:31
  11.4 0.0 copy-start.1
  11.4 0.0 copy-start.2
  11.4 0.0 copy-start.5
  11.4 3.1 %collective-permute-start.3 = (bf16[128,2048]{1,0:T(8,128)(2,1)S(1)}, bf16[128,2048]{1,0:T(8,128)(2,1)S(1)}, u32[]{:S(2)}, u32[]{:S(2)}) collective-permute-start(bf16[128,2048]{1,0:T(8,128)(2,1)S(1)} %get-tuple-element.51), channel_id=1, source_target_pairs={{4,8},{8,4},{12,16},{16,12},{20,24},{24,20},{5,9},{9,5},{13,17},{1... | collective-permute-start | bytes 1572872 | tf_op jit(solution)/shard_map/ppermute | solution.py:31
  14.5 0.0 collective-permute-done.aux1_ref.m1.write1_ref
  14.5 0.9 %collective-permute-done.1.write2_ref.aux2_ref.m2 = bf16[128,768]{1,0:T(8,128)(2,1)S(1)} collective-permute-done((bf16[128,768]{1,0:T(8,128)(2,1)}, bf16[128,768]{1,0:T(8,128)(2,1)S(1)}, u32[]{:S(2)}, u32[]{:S(2)}) %collective-permute-start.1) | collective-permute-done | bytes 196640 | tf_op jit(solution)/shard_map/ppermute | solution.py:23
  15.4 0.0 copy-done
  15.4 0.0 copy-done.3
  15.4 0.0 copy-done.7
  15.4 0.0 copy-done.8
  15.4 1.1 %far.1 = (bf16[128,1024]{1,0:T(8,128)(2,1)S(1)}, bf16[128,128]{1,0:T(8,128)(2,1)S(1)}, f32[8,128]{1,0:T(8,128)S(1)}) custom-call(f32[32,128]{1,0:T(8,128)S(1)} %bitcast.4, s32[1,128]{1,0:T(1,128)S(1)} %bitcast.7, bf16[128,128]{1,0:T(8,128)(2,1)S(1)} %copy-done.3, bf16[128,768]{1,0:T(8,128)(2,1)S(1)} %collective-permute-done.aux1_ref.m1.write1_ref, ...), custom_call_target="tpu_custom_call" | custom-call | tf_op jit(solution)/shard_map/far/pallas_call | solution.py:443
  16.5 0.0 copy-done.1
  16.5 4.1 %collective-permute-start.4 = (bf16[128,2048]{1,0:T(8,128)(2,1)S(1)}, bf16[128,2048]{1,0:T(8,128)(2,1)S(1)}, u32[]{:S(2)}, u32[]{:S(2)}) collective-permute-start(bf16[128,2048]{1,0:T(8,128)(2,1)S(1)} %copy-done.1), channel_id=1, source_target_pairs={{0,8},{4,12},{8,16},{12,20},{16,24},{20,28},{1,9},{5,13},{9,17},{1... | collective-permute-start | bytes 1572872 | tf_op jit(solution)/shard_map/ppermute | solution.py:23
  20.6 0.0 copy-done.6
  20.6 0.0 copy-done.2
  20.6 0.0 copy-done.5
  20.6 0.0 copy-start.4
  20.6 3.2 %attention.1 = (bf16[128,1024]{1,0:T(8,128)(2,1)}, f32[128,512]{1,0:T(8,128)S(1)}, bf16[128,768]{1,0:T(8,128)(2,1)S(1)}, bf16[128,1664]{1,0:T(8,128)(2,1)S(1)}) custom-call(s32[1,128]{1,0:T(1,128)S(1)} %bitcast.8, bf16[128,128]{1,0:T(8,128)(2,1)S(1)} %copy-done.3, bf16[128,768]{1,0:T(8,128)(2,1)S(1)} %copy-done.2, ...), custom_call_target="tpu_custom_call" | custom-call | tf_op jit(solution)/shard_map/attention/pallas_call | solution.py:464
  23.8 1.9 %collective-permute-start.6 = (bf16[128,1664]{1,0:T(8,128)(2,1)S(1)}, bf16[128,1664]{1,0:T(8,128)(2,1)S(1)}, u32[]{:S(2)}, u32[]{:S(2)}) collective-permute-start(bf16[128,1664]{1,0:T(8,128)(2,1)S(1)} %get-tuple-element.43), channel_id=1, source_target_pairs={{8,0},{12,4},{16,8},{20,12},{24,16},{28,20},{9,1},{13,5},{17,9},{2... | collective-permute-start | bytes 1277960 | tf_op jit(solution)/shard_map/ppermute | solution.py:23
  25.8 1.9 %collective-permute-start.5 = (bf16[128,768]{1,0:T(8,128)(2,1)S(1)}, bf16[128,768]{1,0:T(8,128)(2,1)S(1)}, u32[]{:S(2)}, u32[]{:S(2)}) collective-permute-start(bf16[128,768]{1,0:T(8,128)(2,1)S(1)} %get-tuple-element.42), channel_id=1, source_target_pairs={{4,0},{8,4},{12,8},{16,12},{20,16},{24,20},{28,24},{5,1},{9,5},{13... | collective-permute-start | bytes 589832 | tf_op jit(solution)/shard_map/ppermute | solution.py:23
  27.7 0.0 copy-done.4
  27.7 4.1 %local_mixer.1 = (f32[128,2048]{1,0:T(8,128)S(1)}, f32[128,2048]{1,0:T(8,128)S(1)}, f32[128,2048]{1,0:T(8,128)S(1)}, f32[128,2048]{1,0:T(8,128)S(1)}, f32[128,20...) custom-call(s32[1,128]{1,0:T(1,128)S(1)} %bitcast.9, bf16[128,128]{1,0:T(8,128)(2,1)S(1)} %copy-done.4, ...), custom_call_target="tpu_custom_call" | custom-call | tf_op jit(solution)/shard_map/local_mixer/pallas_call | solution.py:424
  31.8 3.8 %collective-permute-done.2.first_ref = bf16[128,2048]{1,0:T(8,128)(2,1)S(1)} collective-permute-done((bf16[128,2048]{1,0:T(8,128)(2,1)S(1)}, bf16[128,2048]{1,0:T(8,128)(2,1)S(1)}, u32[]{:S(2)}, u32[]{:S(2)}) %collective-permute-start.2) | collective-permute-done | bytes 524320 | tf_op jit(solution)/shard_map/ppermute | solution.py:31
  35.6 0.0 collective-permute-done.3.then_ref
  35.6 2.8 %collective-permute-done.4.x2_ref = bf16[128,2048]{1,0:T(8,128)(2,1)S(1)} collective-permute-done((bf16[128,2048]{1,0:T(8,128)(2,1)S(1)}, bf16[128,2048]{1,0:T(8,128)(2,1)S(1)}, u32[]{:S(2)}, u32[]{:S(2)}) %collective-permute-start.4) | collective-permute-done | bytes 524320 | tf_op jit(solution)/shard_map/ppermute | solution.py:23
  38.5 1.4 %carried.1 = bf16[128,2048]{1,0:T(8,128)(2,1)} custom-call(bf16[128,128]{1,0:T(8,128)(2,1)S(1)} %copy-done.3, bf16[128,768]{1,0:T(8,128)(2,1)S(1)} %collective-permute-done.aux1_ref.m1.write1_ref, bf16[128,768]{1,0:T(8,128)(2,1)S(1)} %collective-permute-done.1.write2_ref.aux2_ref.m2, s32[1,1]{1,0:T(1,128)} %bitcast.2.odd_ref, ...), custom_call_target="tpu_custom_call" | custom-call | tf_op jit(solution)/shard_map/carried/pallas_call | solution.py:494
  39.9 0.6 %collective-permute-done.5.r1_ref = bf16[128,768]{1,0:T(8,128)(2,1)S(1)} collective-permute-done((bf16[128,768]{1,0:T(8,128)(2,1)S(1)}, bf16[128,768]{1,0:T(8,128)(2,1)S(1)}, u32[]{:S(2)}, u32[]{:S(2)}) %collective-permute-start.5) | collective-permute-done | bytes 196640 | tf_op jit(solution)/shard_map/ppermute | solution.py:23
  40.5 0.0 collective-permute-done.6.r2_ref
  40.5 1.8 %returned.1 = (bf16[128,2048]{1,0:T(8,128)(2,1)}, bf16[128,256]{1,0:T(8,128)(2,1)}, bf16[128,256]{1,0:T(8,128)(2,1)}) custom-call(bf16[128,128]{1,0:T(8,128)(2,1)S(1)} %copy-done.4, f32[8,128]{1,0:T(8,128)S(1)} %get-tuple-element.41.long_ref, bf16[128,768]{1,0:T(8,128)(2,1)S(1)} %collective-permute-done.5.r1_ref, ...), custom_call_target="tpu_custom_call" | custom-call | tf_op jit(solution)/shard_map/returned/pallas_call | solution.py:511
Async XLA Ops:
  2.5 12.0 %collective-permute-start = (bf16[128,768]{1,0:T(8,128)(2,1)}, bf16[128,768]{1,0:T(8,128)(2,1)S(1)}, u32[]{:S(2)}, u32[]{:S(2)}) collective-permute-start(bf16[128,768]{1,0:T(8,128)(2,1)} %pack.1.m0), channel_id=1, source_target_pairs={{0,4},{4,8},{8,12},{12,16},{16,20},{20,24},{24,28},{1,5},{5,9},{9,... | collective-permute-start | bytes 589832 | tf_op jit(solution)/shard_map/ppermute | solution.py:23
  5.9 9.5 %collective-permute-start.1 = (bf16[128,768]{1,0:T(8,128)(2,1)}, bf16[128,768]{1,0:T(8,128)(2,1)S(1)}, u32[]{:S(2)}, u32[]{:S(2)}) collective-permute-start(bf16[128,768]{1,0:T(8,128)(2,1)} %pack.1.m0), channel_id=1, source_target_pairs={{0,8},{4,12},{8,16},{12,20},{16,24},{20,28},{1,9},{5,13},{9,17},{1... | collective-permute-start | bytes 589832 | tf_op jit(solution)/shard_map/ppermute | solution.py:23
  9.4 6.0 %copy-start = (bf16[128,2048]{1,0:T(8,128)(2,1)S(1)}, bf16[128,2048]{1,0:T(8,128)(2,1)}, u32[]{:S(2)}) copy-start(bf16[128,2048]{1,0:T(8,128)(2,1)} %cot_ref.5) | copy-start | bytes 1572868
  9.4 6.0 %copy-start.3 = (bf16[128,128]{1,0:T(8,128)(2,1)S(1)}, bf16[128,128]{1,0:T(8,128)(2,1)}, u32[]{:S(2)}) copy-start(bf16[128,128]{1,0:T(8,128)(2,1)} %read_ref.7) | copy-start | bytes 98308
  9.4 5.9 %copy-start.7 = (f32[128,32]{0,1:T(8,128)S(1)}, f32[128,32]{0,1:T(8,128)}, u32[]{:S(2)}) copy-start(f32[128,32]{0,1:T(8,128)} %param.14) | copy-start | bytes 49156
  9.5 11.1 %copy-start.6 = (bf16[128,1024]{1,0:T(8,128)(2,1)S(1)}, bf16[128,1024]{1,0:T(8,128)(2,1)}, u32[]{:S(2)}) copy-start(bf16[128,1024]{1,0:T(8,128)(2,1)} %cot_ref.4) | copy-start | bytes 786436
  10.8 4.6 %copy-start.8 = (s32[128]{0:T(128)S(1)}, s32[128]{0:T(128)}, u32[]{:S(2)}) copy-start(s32[128]{0:T(128)} %param.17) | copy-start | bytes 1540
  10.8 24.8 %collective-permute-start.2 = (bf16[128,2048]{1,0:T(8,128)(2,1)S(1)}, bf16[128,2048]{1,0:T(8,128)(2,1)S(1)}, u32[]{:S(2)}, u32[]{:S(2)}) collective-permute-start(bf16[128,2048]{1,0:T(8,128)(2,1)S(1)} %get-tuple-element.52), channel_id=1, source_target_pairs={{0,4},{4,0},{8,12},{12,8},{16,20},{20,16},{24,28},{28,24},{1,5},{5... | collective-permute-start | bytes 1572872 | tf_op jit(solution)/shard_map/ppermute | solution.py:31
  11.4 5.1 %copy-start.1 = (bf16[128,2048]{1,0:T(8,128)(2,1)S(1)}, bf16[128,2048]{1,0:T(8,128)(2,1)}, u32[]{:S(2)}) copy-start(bf16[128,2048]{1,0:T(8,128)(2,1)} %x_ref.1) | copy-start | bytes 1572868
  11.4 9.2 %copy-start.2 = (bf16[128,768]{1,0:T(8,128)(2,1)S(1)}, bf16[128,768]{1,0:T(8,128)(2,1)}, u32[]{:S(2)}) copy-start(bf16[128,768]{1,0:T(8,128)(2,1)} %pack.1.m0) | copy-start | bytes 589828
  11.4 9.2 %copy-start.5 = (bf16[128,1024]{1,0:T(8,128)(2,1)S(1)}, bf16[128,1024]{1,0:T(8,128)(2,1)}, u32[]{:S(2)}) copy-start(bf16[128,1024]{1,0:T(8,128)(2,1)} %q_ref.1) | copy-start | bytes 786436
  11.4 24.3 %collective-permute-start.3 = (bf16[128,2048]{1,0:T(8,128)(2,1)S(1)}, bf16[128,2048]{1,0:T(8,128)(2,1)S(1)}, u32[]{:S(2)}, u32[]{:S(2)}) collective-permute-start(bf16[128,2048]{1,0:T(8,128)(2,1)S(1)} %get-tuple-element.51), channel_id=1, source_target_pairs={{4,8},{8,4},{12,16},{16,12},{20,24},{24,20},{5,9},{9,5},{13,17},{1... | collective-permute-start | bytes 1572872 | tf_op jit(solution)/shard_map/ppermute | solution.py:31
  16.5 22.0 %collective-permute-start.4 = (bf16[128,2048]{1,0:T(8,128)(2,1)S(1)}, bf16[128,2048]{1,0:T(8,128)(2,1)S(1)}, u32[]{:S(2)}, u32[]{:S(2)}) collective-permute-start(bf16[128,2048]{1,0:T(8,128)(2,1)S(1)} %copy-done.1), channel_id=1, source_target_pairs={{0,8},{4,12},{8,16},{12,20},{16,24},{20,28},{1,9},{5,13},{9,17},{1... | collective-permute-start | bytes 1572872 | tf_op jit(solution)/shard_map/ppermute | solution.py:23
  20.6 7.1 %copy-start.4 = (bf16[128,128]{1,0:T(8,128)(2,1)S(1)}, bf16[128,128]{1,0:T(8,128)(2,1)}, u32[]{:S(2)}) copy-start(bf16[128,128]{1,0:T(8,128)(2,1)} %write_ref.5) | copy-start | bytes 98308
  23.8 16.6 %collective-permute-start.6 = (bf16[128,1664]{1,0:T(8,128)(2,1)S(1)}, bf16[128,1664]{1,0:T(8,128)(2,1)S(1)}, u32[]{:S(2)}, u32[]{:S(2)}) collective-permute-start(bf16[128,1664]{1,0:T(8,128)(2,1)S(1)} %get-tuple-element.43), channel_id=1, source_target_pairs={{8,0},{12,4},{16,8},{20,12},{24,16},{28,20},{9,1},{13,5},{17,9},{2... | collective-permute-start | bytes 1277960 | tf_op jit(solution)/shard_map/ppermute | solution.py:23
  25.8 14.7 %collective-permute-start.5 = (bf16[128,768]{1,0:T(8,128)(2,1)S(1)}, bf16[128,768]{1,0:T(8,128)(2,1)S(1)}, u32[]{:S(2)}, u32[]{:S(2)}) collective-permute-start(bf16[128,768]{1,0:T(8,128)(2,1)S(1)} %get-tuple-element.42), channel_id=1, source_target_pairs={{4,0},{8,4},{12,8},{16,12},{20,16},{24,20},{28,24},{5,1},{9,5},{13... | collective-permute-start | bytes 589832 | tf_op jit(solution)/shard_map/ppermute | solution.py:23

commit v7 on v5

--- a/solution.py
+++ b/solution.py
@@ -314,12 +314,13 @@
     odd = odd_ref[0, 0] == 1
     score1 = dot(read_ref[...], write1_ref[...], NT).astype(BF16)
     score2 = dot(read_ref[...], write2_ref[...], NT).astype(BF16)
+    scores = jnp.concatenate([score1, score2], axis=1)
 
     def columns_of(low, at):
         x1 = jnp.where(odd, first_ref[:, at], then_ref[:, at])
         x1 = (x1.astype(F32) * exit1_ref[:, at]).astype(BF16)
         x2 = (x2_ref[:, at].astype(F32) * exit2_ref[:, at]).astype(BF16)
-        carried = dot(score2, x2) + dot(score1, x1)
+        carried = dot(scores, jnp.concatenate([x1, x2], axis=0))
         return (mixed_ref[:, at] + carried * entry_ref[:, at]).astype(BF16)
 
     in_steps(cols, step, out_ref, held_ref, sems, columns_of)
@@ -354,6 +355,7 @@
     sums = dot(write_ref[...], r2_ref[:half, kv2 + cols // 2 :], NT)
     take = jnp.where(iota((tokens, half), 0) == iota((tokens, half), 1) + half, 1.0, 0.0)
     score2 = choose(long_ref[:1, :1] > 0.5, sums, take).astype(BF16)
+    scores = jnp.concatenate([score1, score2], axis=1)
     total = own_ref[...] + r1_ref[:, :kv2].astype(F32) + r2_ref[:, :kv2].astype(F32)
     for g in range(kv2 // (2 * width)):
         at = slice(g * width, (g + 1) * width)
@@ -368,7 +370,7 @@
         row = low // (cols // 2) * half
         col = kv2 + low % (cols // 2)
         far = r2_ref[row : row + half, col : col + step]
-        returned = dot(score1, c1) + dot(score2, far)
+        returned = dot(scores, jnp.concatenate([c1, far], axis=0))
         return (grad_ref[:, at] + returned * exit_ref[:, at]).astype(BF16)
 
     for low in range(0, cols, step):

time: 42.6 us -> 42.6 us (level)
  no operation moved by 1% of the time
where the time goes in v7:
time: 42.6 us; the launch traced here: 42.3 us
  starting transfers between devices  18.4 us (43%)
  Pallas kernels  13.2 us (31%)
  waiting for transfers between devices  8.49 us (20%)
  other arithmetic  1.34 us (3%)
  between operations  0.82 us (2%)
    ppermute x5, starting transfers between devices, passed_along(): return lax.ppermute(block, axis, route)  14.8 us
    ppermute x5, waiting for transfers between devices, passed_along(): return lax.ppermute(block, axis, route)  4.55 us
    pallas_call x1, Pallas kernels, shards(): pl.pallas_call(functools.partial(local_kernel, heads, head_width), grid=(...  3.98 us
    ppermute x2, waiting for transfers between devices, exchanged(): return lax.ppermute(block, axis, route)  3.94 us
    ppermute x2, starting transfers between devices, exchanged(): return lax.ppermute(block, axis, route)  3.64 us
    pallas_call x1, Pallas kernels, shards(): pl.pallas_call(functools.partial(attn_kernel, kv, 2 * kv + state + 3 * he...  3.24 us
    pallas_call x1, Pallas kernels, shards(): pl.pallas_call(pack_kernel, out_shape=shape((tokens, m_cols), BF16), comp...  1.83 us
    pallas_call x1, Pallas kernels, shards(): pl.pallas_call(functools.partial(returned_kernel, heads, head_width, half...  1.81 us
  transfers between devices with their start and end apart: 7, of which 4 were waited for; matrix products, arithmetic and copies ran while one was open for 3% of the time, Pallas kernels for 23%

profile of v7, /device:TPU:14, one launch (start us, length us, event | category | flops | bytes accessed | tf_op | source)
XLA Modules:
  0.0 42.3 jit_solution(11875323809517708964)
XLA Ops:
  0.6 1.8 %pack.1.m0 = bf16[128,768]{1,0:T(8,128)(2,1)} custom-call(bf16[128,256]{1,0:T(8,128)(2,1)} %key_ref.1, bf16[128,256]{1,0:T(8,128)(2,1)} %value_ref.1, bf16[128,128]{1,0:T(8,128)(2,1)} %write_ref.5, f32[32,128]{1,0:T(8,128)} %bitcast.3, s32[1,128]{1,0:T(1,128)} %bitcast.6), custom_call_target="tpu_custom_call" | custom-call | tf_op jit(solution)/shard_map/pack/pallas_call | solution.py:421
  2.5 3.4 %collective-permute-start = (bf16[128,768]{1,0:T(8,128)(2,1)}, bf16[128,768]{1,0:T(8,128)(2,1)S(1)}, u32[]{:S(2)}, u32[]{:S(2)}) collective-permute-start(bf16[128,768]{1,0:T(8,128)(2,1)} %pack.1.m0), channel_id=1, source_target_pairs={{0,4},{4,8},{8,12},{12,16},{16,20},{20,24},{24,28},{1,5},{5,9},{9,... | collective-permute-start | bytes 589832 | tf_op jit(solution)/shard_map/ppermute | solution.py:23
  5.9 3.5 %collective-permute-start.1 = (bf16[128,768]{1,0:T(8,128)(2,1)}, bf16[128,768]{1,0:T(8,128)(2,1)S(1)}, u32[]{:S(2)}, u32[]{:S(2)}) collective-permute-start(bf16[128,768]{1,0:T(8,128)(2,1)} %pack.1.m0), channel_id=1, source_target_pairs={{0,8},{4,12},{8,16},{12,20},{16,24},{20,28},{1,9},{5,13},{9,17},{1... | collective-permute-start | bytes 589832 | tf_op jit(solution)/shard_map/ppermute | solution.py:23
  9.4 0.0 copy-start
  9.4 0.0 copy-start.3
  9.4 0.0 copy-start.7
  9.5 0.0 copy-start.6
  9.5 1.3 %broadcast_select_fusion = (bf16[128,2048]{1,0:T(8,128)(2,1)S(1)}, bf16[128,2048]{1,0:T(8,128)(2,1)S(1)}) fusion(bf16[128,2048]{1,0:T(8,128)(2,1)} %cot_ref.5, bf16[128,2048]{1,0:T(8,128)(2,1)} %x_ref.1, pred[]{:T(512)S(6)} %eq.6), kind=kLoop, calls=%fused_computation | loop fusion | flops 524288 | bytes 2097153 | tf_op jit(solution)/shard_map/jit(_where)/select_n | solution.py:430
  10.8 0.0 copy-start.8
  10.8 0.5 %collective-permute-start.2 = (bf16[128,2048]{1,0:T(8,128)(2,1)S(1)}, bf16[128,2048]{1,0:T(8,128)(2,1)S(1)}, u32[]{:S(2)}, u32[]{:S(2)}) collective-permute-start(bf16[128,2048]{1,0:T(8,128)(2,1)S(1)} %get-tuple-element.50), channel_id=1, source_target_pairs={{0,4},{4,0},{8,12},{12,8},{16,20},{20,16},{24,28},{28,24},{1,5},{5... | collective-permute-start | bytes 1572872 | tf_op jit(solution)/shard_map/ppermute | solution.py:31
  11.4 0.0 copy-start.1
  11.4 0.0 copy-start.2
  11.4 0.0 copy-start.5
  11.4 3.1 %collective-permute-start.3 = (bf16[128,2048]{1,0:T(8,128)(2,1)S(1)}, bf16[128,2048]{1,0:T(8,128)(2,1)S(1)}, u32[]{:S(2)}, u32[]{:S(2)}) collective-permute-start(bf16[128,2048]{1,0:T(8,128)(2,1)S(1)} %get-tuple-element.49), channel_id=1, source_target_pairs={{4,8},{8,4},{12,16},{16,12},{20,24},{24,20},{5,9},{9,5},{13,17},{1... | collective-permute-start | bytes 1572872 | tf_op jit(solution)/shard_map/ppermute | solution.py:31
  14.5 0.0 collective-permute-done.aux1_ref.m1.write1_ref
  14.5 0.9 %collective-permute-done.1.write2_ref.aux2_ref.m2 = bf16[128,768]{1,0:T(8,128)(2,1)S(1)} collective-permute-done((bf16[128,768]{1,0:T(8,128)(2,1)}, bf16[128,768]{1,0:T(8,128)(2,1)S(1)}, u32[]{:S(2)}, u32[]{:S(2)}) %collective-permute-start.1) | collective-permute-done | bytes 196640 | tf_op jit(solution)/shard_map/ppermute | solution.py:23
  15.4 0.0 copy-done
  15.4 0.0 copy-done.3
  15.4 0.0 copy-done.7
  15.4 0.0 copy-done.8
  15.4 1.1 %far.1 = (bf16[128,1024]{1,0:T(8,128)(2,1)S(1)}, bf16[128,128]{1,0:T(8,128)(2,1)S(1)}, f32[8,128]{1,0:T(8,128)S(1)}) custom-call(f32[32,128]{1,0:T(8,128)S(1)} %bitcast.4, s32[1,128]{1,0:T(1,128)S(1)} %bitcast.7, bf16[128,128]{1,0:T(8,128)(2,1)S(1)} %copy-done.3, bf16[128,768]{1,0:T(8,128)(2,1)S(1)} %collective-permute-done.aux1_ref.m1.write1_ref, ...), custom_call_target="tpu_custom_call" | custom-call | tf_op jit(solution)/shard_map/far/pallas_call | solution.py:455
  16.5 0.0 copy-done.1
  16.5 4.1 %collective-permute-start.4 = (bf16[128,2048]{1,0:T(8,128)(2,1)S(1)}, bf16[128,2048]{1,0:T(8,128)(2,1)S(1)}, u32[]{:S(2)}, u32[]{:S(2)}) collective-permute-start(bf16[128,2048]{1,0:T(8,128)(2,1)S(1)} %copy-done.1), channel_id=1, source_target_pairs={{0,8},{4,12},{8,16},{12,20},{16,24},{20,28},{1,9},{5,13},{9,17},{1... | collective-permute-start | bytes 1572872 | tf_op jit(solution)/shard_map/ppermute | solution.py:23
  20.6 0.0 copy-done.6
  20.6 0.0 copy-done.2
  20.6 0.0 copy-done.5
  20.6 0.0 copy-start.4
  20.6 3.2 %attention.1 = (bf16[128,1024]{1,0:T(8,128)(2,1)}, f32[128,512]{1,0:T(8,128)S(1)}, bf16[128,768]{1,0:T(8,128)(2,1)S(1)}, bf16[128,1664]{1,0:T(8,128)(2,1)S(1)}) custom-call(s32[1,128]{1,0:T(1,128)S(1)} %bitcast.8, bf16[128,128]{1,0:T(8,128)(2,1)S(1)} %copy-done.3, bf16[128,768]{1,0:T(8,128)(2,1)S(1)} %copy-done.2, ...), custom_call_target="tpu_custom_call" | custom-call | tf_op jit(solution)/shard_map/attention/pallas_call | solution.py:476
  23.8 1.9 %collective-permute-start.6 = (bf16[128,1664]{1,0:T(8,128)(2,1)S(1)}, bf16[128,1664]{1,0:T(8,128)(2,1)S(1)}, u32[]{:S(2)}, u32[]{:S(2)}) collective-permute-start(bf16[128,1664]{1,0:T(8,128)(2,1)S(1)} %get-tuple-element.42), channel_id=1, source_target_pairs={{8,0},{12,4},{16,8},{20,12},{24,16},{28,20},{9,1},{13,5},{17,9},{2... | collective-permute-start | bytes 1277960 | tf_op jit(solution)/shard_map/ppermute | solution.py:23
  25.8 1.9 %collective-permute-start.5 = (bf16[128,768]{1,0:T(8,128)(2,1)S(1)}, bf16[128,768]{1,0:T(8,128)(2,1)S(1)}, u32[]{:S(2)}, u32[]{:S(2)}) collective-permute-start(bf16[128,768]{1,0:T(8,128)(2,1)S(1)} %get-tuple-element.41), channel_id=1, source_target_pairs={{4,0},{8,4},{12,8},{16,12},{20,16},{24,20},{28,24},{5,1},{9,5},{13... | collective-permute-start | bytes 589832 | tf_op jit(solution)/shard_map/ppermute | solution.py:23
  27.7 0.0 copy-done.4
  27.7 4.0 %local_mixer.1 = (f32[128,2048]{1,0:T(8,128)S(1)}, f32[128,2048]{1,0:T(8,128)S(1)}, f32[128,2048]{1,0:T(8,128)S(1)}, f32[128,2048]{1,0:T(8,128)S(1)}, f32[128,2048]{1,0:T(8,128)S(1)}, /*index=5*/f32[128,2048]{1,0:T(8,128)S(1)}) custom-call(s32[1,128]{1,0:T(1,128)S(1)} %bitcast.9, bf16[128,128]{1,0:T(8,128)(2,1)S(1)} %copy-done.4, ...), custom_call_target="tpu_custom_call" | custom-call | tf_op jit(solution)/shard_map/local_mixer/pallas_call | solution.py:436
  31.7 3.9 %collective-permute-done.2.first_ref = bf16[128,2048]{1,0:T(8,128)(2,1)S(1)} collective-permute-done((bf16[128,2048]{1,0:T(8,128)(2,1)S(1)}, bf16[128,2048]{1,0:T(8,128)(2,1)S(1)}, u32[]{:S(2)}, u32[]{:S(2)}) %collective-permute-start.2) | collective-permute-done | bytes 524320 | tf_op jit(solution)/shard_map/ppermute | solution.py:31
  35.6 0.0 collective-permute-done.3.then_ref
  35.6 2.8 %collective-permute-done.4.x2_ref = bf16[128,2048]{1,0:T(8,128)(2,1)S(1)} collective-permute-done((bf16[128,2048]{1,0:T(8,128)(2,1)S(1)}, bf16[128,2048]{1,0:T(8,128)(2,1)S(1)}, u32[]{:S(2)}, u32[]{:S(2)}) %collective-permute-start.4) | collective-permute-done | bytes 524320 | tf_op jit(solution)/shard_map/ppermute | solution.py:23
  38.5 1.2 %carried.1 = bf16[128,2048]{1,0:T(8,128)(2,1)} custom-call(bf16[128,128]{1,0:T(8,128)(2,1)S(1)} %copy-done.3, bf16[128,768]{1,0:T(8,128)(2,1)S(1)} %collective-permute-done.aux1_ref.m1.write1_ref, bf16[128,768]{1,0:T(8,128)(2,1)S(1)} %collective-permute-done.1.write2_ref.aux2_ref.m2, s32[1,1]{1,0:T(1,128)} %bitcast.2.odd_ref, ...), custom_call_target="tpu_custom_call" | custom-call | tf_op jit(solution)/shard_map/carried/pallas_call | solution.py:510
  39.7 0.8 %collective-permute-done.5.r1_ref = bf16[128,768]{1,0:T(8,128)(2,1)S(1)} collective-permute-done((bf16[128,768]{1,0:T(8,128)(2,1)S(1)}, bf16[128,768]{1,0:T(8,128)(2,1)S(1)}, u32[]{:S(2)}, u32[]{:S(2)}) %collective-permute-start.5) | collective-permute-done | bytes 196640 | tf_op jit(solution)/shard_map/ppermute | solution.py:23
  40.5 0.0 collective-permute-done.6.r2_ref
  40.5 1.8 %returned.1 = (bf16[128,2048]{1,0:T(8,128)(2,1)}, bf16[128,256]{1,0:T(8,128)(2,1)}, bf16[128,256]{1,0:T(8,128)(2,1)}) custom-call(bf16[128,128]{1,0:T(8,128)(2,1)S(1)} %copy-done.4, f32[8,128]{1,0:T(8,128)S(1)} %get-tuple-element.40.long_ref, bf16[128,768]{1,0:T(8,128)(2,1)S(1)} %collective-permute-done.5.r1_ref, ...), custom_call_target="tpu_custom_call" | custom-call | tf_op jit(solution)/shard_map/returned/pallas_call | solution.py:528
Async XLA Ops:
  2.5 12.0 %collective-permute-start = (bf16[128,768]{1,0:T(8,128)(2,1)}, bf16[128,768]{1,0:T(8,128)(2,1)S(1)}, u32[]{:S(2)}, u32[]{:S(2)}) collective-permute-start(bf16[128,768]{1,0:T(8,128)(2,1)} %pack.1.m0), channel_id=1, source_target_pairs={{0,4},{4,8},{8,12},{12,16},{16,20},{20,24},{24,28},{1,5},{5,9},{9,... | collective-permute-start | bytes 589832 | tf_op jit(solution)/shard_map/ppermute | solution.py:23
  5.9 9.5 %collective-permute-start.1 = (bf16[128,768]{1,0:T(8,128)(2,1)}, bf16[128,768]{1,0:T(8,128)(2,1)S(1)}, u32[]{:S(2)}, u32[]{:S(2)}) collective-permute-start(bf16[128,768]{1,0:T(8,128)(2,1)} %pack.1.m0), channel_id=1, source_target_pairs={{0,8},{4,12},{8,16},{12,20},{16,24},{20,28},{1,9},{5,13},{9,17},{1... | collective-permute-start | bytes 589832 | tf_op jit(solution)/shard_map/ppermute | solution.py:23
  9.4 6.0 %copy-start = (bf16[128,2048]{1,0:T(8,128)(2,1)S(1)}, bf16[128,2048]{1,0:T(8,128)(2,1)}, u32[]{:S(2)}) copy-start(bf16[128,2048]{1,0:T(8,128)(2,1)} %cot_ref.5) | copy-start | bytes 1572868
  9.4 6.0 %copy-start.3 = (bf16[128,128]{1,0:T(8,128)(2,1)S(1)}, bf16[128,128]{1,0:T(8,128)(2,1)}, u32[]{:S(2)}) copy-start(bf16[128,128]{1,0:T(8,128)(2,1)} %read_ref.7) | copy-start | bytes 98308
  9.4 5.9 %copy-start.7 = (f32[128,32]{0,1:T(8,128)S(1)}, f32[128,32]{0,1:T(8,128)}, u32[]{:S(2)}) copy-start(f32[128,32]{0,1:T(8,128)} %param.14) | copy-start | bytes 49156
  9.5 11.1 %copy-start.6 = (bf16[128,1024]{1,0:T(8,128)(2,1)S(1)}, bf16[128,1024]{1,0:T(8,128)(2,1)}, u32[]{:S(2)}) copy-start(bf16[128,1024]{1,0:T(8,128)(2,1)} %cot_ref.4) | copy-start | bytes 786436
  10.8 4.6 %copy-start.8 = (s32[128]{0:T(128)S(1)}, s32[128]{0:T(128)}, u32[]{:S(2)}) copy-start(s32[128]{0:T(128)} %param.17) | copy-start | bytes 1540
  10.8 24.8 %collective-permute-start.2 = (bf16[128,2048]{1,0:T(8,128)(2,1)S(1)}, bf16[128,2048]{1,0:T(8,128)(2,1)S(1)}, u32[]{:S(2)}, u32[]{:S(2)}) collective-permute-start(bf16[128,2048]{1,0:T(8,128)(2,1)S(1)} %get-tuple-element.50), channel_id=1, source_target_pairs={{0,4},{4,0},{8,12},{12,8},{16,20},{20,16},{24,28},{28,24},{1,5},{5... | collective-permute-start | bytes 1572872 | tf_op jit(solution)/shard_map/ppermute | solution.py:31
  11.4 5.1 %copy-start.1 = (bf16[128,2048]{1,0:T(8,128)(2,1)S(1)}, bf16[128,2048]{1,0:T(8,128)(2,1)}, u32[]{:S(2)}) copy-start(bf16[128,2048]{1,0:T(8,128)(2,1)} %x_ref.1) | copy-start | bytes 1572868
  11.4 9.2 %copy-start.2 = (bf16[128,768]{1,0:T(8,128)(2,1)S(1)}, bf16[128,768]{1,0:T(8,128)(2,1)}, u32[]{:S(2)}) copy-start(bf16[128,768]{1,0:T(8,128)(2,1)} %pack.1.m0) | copy-start | bytes 589828
  11.4 9.2 %copy-start.5 = (bf16[128,1024]{1,0:T(8,128)(2,1)S(1)}, bf16[128,1024]{1,0:T(8,128)(2,1)}, u32[]{:S(2)}) copy-start(bf16[128,1024]{1,0:T(8,128)(2,1)} %q_ref.1) | copy-start | bytes 786436
  11.4 24.3 %collective-permute-start.3 = (bf16[128,2048]{1,0:T(8,128)(2,1)S(1)}, bf16[128,2048]{1,0:T(8,128)(2,1)S(1)}, u32[]{:S(2)}, u32[]{:S(2)}) collective-permute-start(bf16[128,2048]{1,0:T(8,128)(2,1)S(1)} %get-tuple-element.49), channel_id=1, source_target_pairs={{4,8},{8,4},{12,16},{16,12},{20,24},{24,20},{5,9},{9,5},{13,17},{1... | collective-permute-start | bytes 1572872 | tf_op jit(solution)/shard_map/ppermute | solution.py:31
  16.5 22.0 %collective-permute-start.4 = (bf16[128,2048]{1,0:T(8,128)(2,1)S(1)}, bf16[128,2048]{1,0:T(8,128)(2,1)S(1)}, u32[]{:S(2)}, u32[]{:S(2)}) collective-permute-start(bf16[128,2048]{1,0:T(8,128)(2,1)S(1)} %copy-done.1), channel_id=1, source_target_pairs={{0,8},{4,12},{8,16},{12,20},{16,24},{20,28},{1,9},{5,13},{9,17},{1... | collective-permute-start | bytes 1572872 | tf_op jit(solution)/shard_map/ppermute | solution.py:23
  20.6 7.1 %copy-start.4 = (bf16[128,128]{1,0:T(8,128)(2,1)S(1)}, bf16[128,128]{1,0:T(8,128)(2,1)}, u32[]{:S(2)}) copy-start(bf16[128,128]{1,0:T(8,128)(2,1)} %write_ref.5) | copy-start | bytes 98308
  23.8 16.6 %collective-permute-start.6 = (bf16[128,1664]{1,0:T(8,128)(2,1)S(1)}, bf16[128,1664]{1,0:T(8,128)(2,1)S(1)}, u32[]{:S(2)}, u32[]{:S(2)}) collective-permute-start(bf16[128,1664]{1,0:T(8,128)(2,1)S(1)} %get-tuple-element.42), channel_id=1, source_target_pairs={{8,0},{12,4},{16,8},{20,12},{24,16},{28,20},{9,1},{13,5},{17,9},{2... | collective-permute-start | bytes 1277960 | tf_op jit(solution)/shard_map/ppermute | solution.py:23
  25.8 14.7 %collective-permute-start.5 = (bf16[128,768]{1,0:T(8,128)(2,1)S(1)}, bf16[128,768]{1,0:T(8,128)(2,1)S(1)}, u32[]{:S(2)}, u32[]{:S(2)}) collective-permute-start(bf16[128,768]{1,0:T(8,128)(2,1)S(1)} %get-tuple-element.41), channel_id=1, source_target_pairs={{4,0},{8,4},{12,8},{16,12},{20,16},{24,20},{28,24},{5,1},{9,5},{13... | collective-permute-start | bytes 589832 | tf_op jit(solution)/shard_map/ppermute | solution.py:23
